TPU v7x, 32 devices: a whole 2x2x4 slice. The times are simulated.
32 devices in a mesh: wide: 8 (over z, y), narrow: 4 (over x, core).
Axes of the slice: x: 2, y: 2, z: 4, core: 2. Of those that a mesh axis runs over, the one named last changes fastest.
Arguments:
- dense_feats: bfloat16 [32768, 384], P(('wide', 'narrow')), may hold values from -6 to 6
- sparse_ids: int32 [32768, 8], P(('wide', 'narrow')), may hold values from 0 to 1023
- presence: int32 [32768, 8], P(('wide', 'narrow')), may hold values 0 or 1
- embed_table: bfloat16 [1024, 16], replicated, may hold values from -6 to 6
- w_first: bfloat16 [6, 512, 256], replicated, may hold values from -0.25 to 0.25
- b_first: bfloat16 [6, 256], replicated, may hold values from -4 to 4
- w_second: bfloat16 [6, 256, 256], replicated, may hold values from -0.375 to 0.375
- b_second: bfloat16 [6, 256], replicated, may hold values from -4 to 4
- ln_gain: bfloat16 [6, 256], replicated, may hold values from 0.5 to 1.5
- ln_bias: bfloat16 [6, 256], replicated, may hold values from -4 to 4
- gate_task: bfloat16 [2, 512, 4], replicated, may hold values from -0.5 to 0.5
- gate_task_bias: bfloat16 [2, 4], replicated, may hold values from -1 to 1
- gate_shared: bfloat16 [512, 6], replicated, may hold values from -0.5 to 0.5
- gate_shared_bias: bfloat16 [6], replicated, may hold values from -1 to 1
- cotangent: bfloat16 [3, 32768, 256], P(None, ('wide', 'narrow')), may hold values from -6 to 6
Outputs:
- mixed: bfloat16 [3, 32768, 256], P(None, ('wide', 'narrow'))
- dense_grad: float32 [32768, 384], P(('wide', 'narrow'))
- table_grad: float32 [1024, 16], replicated
- w_first_grad: float32 [6, 512, 256], replicated
- b_first_grad: float32 [6, 256], replicated
- w_second_grad: float32 [6, 256, 256], replicated
- b_second_grad: float32 [6, 256], replicated
- ln_gain_grad: float32 [6, 256], replicated
- ln_bias_grad: float32 [6, 256], replicated
- gate_task_grad: float32 [2, 512, 4], replicated
- gate_task_bias_grad: float32 [2, 4], replicated
- gate_shared_grad: float32 [512, 6], replicated
- gate_shared_bias_grad: float32 [6], replicated
All inputs are finite; a program needn't handle non-finite values. No bound on the sum of `presence` on one device may be relied on, other than what follows from the above.
Results may differ from a plain program's by a relative error of at most 0.013.
Values sent between devices are 32-bit elements; how exact they have to be, the bound alone decides.
No kernel may reach another device: no remote copies, remote signals or barrier semaphores. Data moves between devices by JAX's collectives and lax.ppermute only.
A program may use at most 128 MiB of HBM per device.

v0:
```python
import functools
import math

import jax
import jax.numpy as jnp
from jax import lax
from jax.experimental import pallas as pl
from jax.experimental.pallas import tpu as pltpu
from jax.sharding import PartitionSpec as P

f32 = jnp.float32
bf16 = jnp.bfloat16
epsilon = 1e-05
LANES = 128
SHARDS = 32
MIB = 1 << 20
BOTH = ("wide", "narrow")
SPANS = ((0, 2), (2, 4), (4, 6))
ORDERS = ("cxy12", "cy12x", "c12xy")


def dot(a, b):
    return lax.dot_general(a, b, (((1,), (0,)), ((), ())), preferred_element_type=f32)


def dot_nt(a, b):
    return lax.dot_general(a, b, (((1,), (1,)), ((), ())), preferred_element_type=f32)


def dot_tn(a, b):
    return lax.dot_general(a, b, (((0,), (0,)), ((), ())), preferred_element_type=f32)


def iota(shape, axis):
    return lax.broadcasted_iota(jnp.int32, shape, axis)


def ones_where(condition):
    return jnp.where(condition, 1.0, 0.0).astype(bf16)


class Sizes:
    def __init__(self, dense, ids, table, w_first, w_second, gate_task):
        self.rows, self.dense = dense.shape
        self.fields = ids.shape[1]
        self.vocab, self.emb = table.shape
        self.experts, self.d_in, self.hidden = w_first.shape
        self.out = w_second.shape[2]
        self.tasks, _, self.gate = gate_task.shape
        self.spec = (self.experts - self.gate) // (self.tasks - 1)
        self.chunk = min(256, self.rows)
        self.chunks = self.rows // self.chunk
        self.low = LANES // self.emb
        self.high = self.vocab // self.low
        self.columns = gate_columns(self.experts, self.tasks, self.spec)
        self.width = self.tasks * self.gate + self.experts
        self.first_rows = self.d_in // SHARDS
        self.second_rows = self.hidden // SHARDS
        self.halves = self.out // LANES
        self.expert_rows = (self.first_rows + self.second_rows) * self.halves
        self.sum_rows = 4 * self.halves
        self.gate_rows = 16 * (self.d_in // LANES)
        self.gate_at = self.high
        self.sums_at = self.gate_at + self.gate_rows
        self.bias_at = self.sums_at + self.experts * self.sum_rows
        self.small_rows = -(-(self.bias_at + 1) // (8 * SHARDS)) * 8

    def piece_rows(self, index):
        last = index == len(SPANS) - 1
        lo, hi = SPANS[index]
        return (hi - lo) * self.expert_rows + (self.small_rows if last else 0)


def gate_columns(experts, tasks, spec):
    shared = tasks * spec
    gate = spec + experts - shared
    columns = []
    for e in range(experts):
        found = []
        for k in range(tasks):
            if e >= shared:
                found.append((k, k * gate + spec + e - shared))
            elif e // spec == k:
                found.append((k, k * gate + e - k * spec))
        found.append((tasks, tasks * gate + e))
        columns.append(found)
    return columns


def gate_matrix(z, gate_task_ref, gate_shared_ref):
    total = None
    for k in range(z.tasks + 1):
        mat = gate_task_ref[k] if k < z.tasks else gate_shared_ref[...]
        n = mat.shape[1]
        place = ones_where(iota((n, LANES), 1) == iota((n, LANES), 0) + k * z.gate)
        part = dot(mat, place)
        total = part if total is None else total + part
    return total.astype(bf16)


def gate_bias(z, task_ref, shared_ref):
    total = None
    for k in range(z.tasks + 1):
        row = task_ref[k : k + 1, :] if k < z.tasks else shared_ref[...]
        n = row.shape[1]
        place = ones_where(iota((n, LANES), 1) == iota((n, LANES), 0) + k * z.gate)
        part = dot(row, place)
        total = part if total is None else total + part
    return total


def gate_lanes(z, k, shape):
    lane = iota(shape, 1)
    first = k * z.gate
    last = first + (z.gate if k < z.tasks else z.experts)
    return (lane >= first) & (lane < last)


def spread_matrix(z, f):
    a = iota((LANES, LANES), 0)
    b = iota((LANES, LANES), 1)
    return ones_where(b == f * z.emb + lax.rem(a, z.emb))


def table_block(z, table_ref):
    total = None
    for low in range(z.low):
        place = ones_where(iota((z.emb, LANES), 1) == iota((z.emb, LANES), 0) + low * z.emb)
        part = dot(table_ref[low * z.high : (low + 1) * z.high, :], place)
        total = part if total is None else total + part
    return total.astype(bf16)


def features_part(z, rows, block, spreads, ids_ref, presence_ref, dense_ref, features_ref):
    ids = ids_ref[rows, :]
    row = jnp.where(presence_ref[rows, :] > 0, lax.rem(ids, z.high), -1)
    low = lax.div(ids, z.high)
    lane_high = iota((z.chunk, z.high), 1)
    lane_low = lax.div(iota((z.chunk, LANES), 1), z.emb)
    total = None
    for f in range(z.fields):
        found = dot(ones_where(row[:, f : f + 1] == lane_high), block)
        kept = jnp.where(low[:, f : f + 1] == lane_low, found, 0.0).astype(bf16)
        part = dot(kept, spreads[f])
        total = part if total is None else total + part
    features_ref[rows, : z.dense] = dense_ref[rows, :]
    features_ref[rows, z.dense :] = total.astype(bf16)


def softmax_part(z, logits):
    result = None
    for k in range(z.tasks + 1):
        lanes = gate_lanes(z, k, logits.shape)
        top = jnp.max(jnp.where(lanes, logits, -jnp.inf), axis=1, keepdims=True)
        value = jnp.exp(jnp.where(lanes, logits - top, -jnp.inf))
        value = value / jnp.sum(value, axis=1, keepdims=True)
        result = value if result is None else result + value
    return result


def logit_part(z, weights, along):
    product = weights * along
    total = jnp.zeros_like(product)
    for k in range(z.tasks + 1):
        lanes = gate_lanes(z, k, product.shape)
        found = jnp.sum(jnp.where(lanes, product, 0.0), axis=1, keepdims=True)
        total = jnp.where(lanes, found, total)
    return (weights * (along - total)).astype(bf16)


def table_part(z, rows, embed, spreads, ids_ref, presence_ref):
    ids = ids_ref[rows, :]
    row = jnp.where(presence_ref[rows, :] > 0, lax.rem(ids, z.high), -1)
    low = lax.div(ids, z.high)
    lane_high = iota((z.chunk, z.high), 1)
    lane_low = lax.div(iota((z.chunk, LANES), 1), z.emb)
    hots = []
    kept = []
    for f in range(z.fields):
        hots.append(ones_where(row[:, f : f + 1] == lane_high))
        wide = dot_nt(embed, spreads[f])
        kept.append(jnp.where(low[:, f : f + 1] == lane_low, wide, 0.0).astype(bf16))
    return dot_tn(jnp.concatenate(hots, axis=0), jnp.concatenate(kept, axis=0))


def experts_kernel(z, index, *refs):
    first = index == 0
    last = index == len(SPANS) - 1
    span = SPANS[index]
    n = span[1] - span[0]
    refs = list(refs)

    def take(count):
        return [refs.pop(0) for _ in range(count)]

    (place_ref,) = take(1)
    w_first_ref, b_first_ref, w_second_ref, b_second_ref, gain_ref, bias_ref, cot_ref = take(7)
    if first:
        dense_ref, ids_ref, presence_ref, table_ref = take(4)
        gate_task_ref, gate_task_bias_ref, gate_shared_ref, gate_shared_bias_ref = take(4)
    else:
        features_ref, weights_ref, part_ref = take(3)
    if last:
        ids_ref, presence_ref, gate_task_ref, gate_shared_ref = take(4)
        earlier_refs = take(index)
    packed_ref, normed_ref, first_ref = take(3)
    if first:
        features_ref, weights_ref = take(2)
    if last:
        (logit_ref,) = take(1)
    else:
        out_ref, sums_ref = take(2)
    hidden_s, second_s, total_s, sums_s = take(4)
    if last:
        gate_s, small_s = take(2)
    if first:
        block = table_block(z, table_ref)
        gates_bias = gate_bias(z, gate_task_bias_ref, gate_shared_bias_ref)
    if first or last:
        spreads = [spread_matrix(z, f) for f in range(z.fields)]
        gates = gate_matrix(z, gate_task_ref, gate_shared_ref)
    sums_s[...] = jnp.zeros_like(sums_s)
    if last:
        gate_s[...] = jnp.zeros_like(gate_s)
        small_s[...] = jnp.zeros_like(small_s)
    scale = 1.0 / z.out

    def step(at, carry):
        rows = pl.ds(pl.multiple_of(at * z.chunk, z.chunk), z.chunk)
        if first:
            features_part(
                z, rows, block, spreads, ids_ref, presence_ref, dense_ref, features_ref
            )
            weights_ref[rows, :] = softmax_part(z, dot(features_ref[rows, :], gates) + gates_bias)
        features = features_ref[rows, :]
        weights = weights_ref[rows, :]
        along = jnp.zeros((z.chunk, LANES), f32) if first else part_ref[0, rows, :]
        embed = jnp.zeros((z.chunk, LANES), f32) if first else part_ref[1, rows, :]
        lane = iota((z.chunk, LANES), 1)
        cots = [cot_ref[k, rows, :].astype(f32) for k in range(z.tasks + 1)]
        for i in range(n):
            e = span[0] + i

            def row(ref):
                return ref[e : e + 1, :].astype(f32)

            gain = row(gain_ref)
            pre = dot(features, w_first_ref[i]) + row(b_first_ref)
            sig = 0.5 * jnp.tanh(0.5 * pre) + 0.5
            hidden = (pre * sig).astype(bf16)
            hidden_s[i, rows, :] = hidden
            second = dot(hidden, w_second_ref[i]) + row(b_second_ref)
            center = second - jnp.sum(second, axis=1, keepdims=True) * scale
            inverse = lax.rsqrt(jnp.sum(center * center, axis=1, keepdims=True) * scale + epsilon)
            normed = center * inverse
            normed_ref[i, rows, :] = normed.astype(bf16)
            expert_out = normed * gain + row(bias_ref)
            upstream = None
            for k, column in z.columns[e]:
                part = weights[:, column : column + 1] * cots[k]
                upstream = part if upstream is None else upstream + part
                found = jnp.sum(cots[k] * expert_out, axis=1, keepdims=True)
                along = jnp.where(lane == column, found, along)
            scaled = upstream * gain
            mean = jnp.sum(scaled, axis=1, keepdims=True) * scale
            mean_normed = jnp.sum(scaled * normed, axis=1, keepdims=True) * scale
            second_grad = (inverse * (scaled - mean - normed * mean_normed)).astype(bf16)
            second_s[i, rows, :] = second_grad
            hidden_grad = dot_nt(second_grad, w_second_ref[i])
            first_grad = (hidden_grad * (sig * (1.0 + pre * (1.0 - sig)))).astype(bf16)
            first_ref[i, rows, :] = first_grad
            embed = embed + dot_nt(first_grad, w_first_ref[i, z.dense :, :])

            def eights(v):
                return jnp.sum(v.reshape(z.chunk // 8, 8, z.out), axis=0)

            sums_s[i, 0] += eights(first_grad.astype(f32))
            sums_s[i, 1] += eights(second_grad.astype(f32))
            sums_s[i, 2] += eights(upstream * normed)
            sums_s[i, 3] += eights(upstream)
        if not last:
            out_ref[0, rows, :] = along
            out_ref[1, rows, :] = embed
            return carry
        logit_grad = logit_part(z, weights, along)
        logit_ref[rows, :] = logit_grad
        gate_s[...] += dot_tn(logit_grad, features)
        embed = embed + dot_nt(logit_grad, gates[z.dense :, :])
        small_s[: z.high, :] += table_part(
            z, rows, embed.astype(bf16), spreads, ids_ref, presence_ref
        )
        small_s[z.bias_at : z.bias_at + 1, :] += jnp.sum(
            logit_grad.astype(f32), axis=0, keepdims=True
        )
        return carry

    lax.fori_loop(0, z.chunks, step, 0)

    for i in range(n):
        for q in range(4):
            found = jnp.sum(sums_s[i, q], axis=0, keepdims=True)
            for h in range(z.halves):
                line = i * z.sum_rows + q * z.halves + h
                part = found[:, h * LANES : (h + 1) * LANES]
                if last:
                    line = z.sums_at + span[0] * z.sum_rows + line
                    small_s[line : line + 1, :] = part
                else:
                    sums_ref[line : line + 1, :] = part
    if last:
        line = z.sums_at
        for ref in earlier_refs:
            small_s[line : line + ref.shape[0], :] = ref[...]
            line += ref.shape[0]
        for q in range(z.d_in // LANES):
            line = z.gate_at + q * 16
            small_s[line : line + 16, :] = gate_s[:16, q * LANES : (q + 1) * LANES]

    place = place_ref[index]
    for i in range(n):
        total_s[i, : z.d_in, :] = dot_tn(features_ref[...], first_ref[i])
        total_s[i, z.d_in :, :] = dot_tn(hidden_s[i], second_s[i])

    def pack(r, carry):
        block = lax.bitwise_xor(r, place)
        for i in range(n):
            line = i * z.expert_rows
            for start, count in ((0, z.first_rows), (z.d_in, z.second_rows)):
                lines = pl.ds(pl.multiple_of(start + block * count, 8), count)
                for h in range(z.halves):
                    packed_ref[r, line : line + count, :] = total_s[
                        i, lines, h * LANES : (h + 1) * LANES
                    ]
                    line += count
        if last:
            lines = pl.ds(pl.multiple_of(block * z.small_rows, 8), z.small_rows)
            packed_ref[r, n * z.expert_rows :, :] = small_s[lines, :]
        return carry

    lax.fori_loop(0, SHARDS, pack, 0)


def outputs_kernel(z, *refs):
    refs = list(refs)
    weights_ref, logit_ref, w_first_ref, gain_ref, bias_ref, gate_task_ref, gate_shared_ref = refs[
        :7
    ]
    normed_refs = refs[7 : 7 + len(SPANS)]
    first_refs = refs[7 + len(SPANS) : 7 + 2 * len(SPANS)]
    mixed_ref, dense_ref = refs[7 + 2 * len(SPANS) :]
    weights = weights_ref[...]
    mixed = [None] * (z.tasks + 1)
    gates = gate_matrix(z, gate_task_ref, gate_shared_ref)
    dense = dot_nt(logit_ref[...], gates[: z.dense, :])
    for index, span in enumerate(SPANS):
        for i in range(span[1] - span[0]):
            e = span[0] + i
            expert_out = normed_refs[index][i].astype(f32) * gain_ref[e : e + 1, :].astype(
                f32
            ) + bias_ref[e : e + 1, :].astype(f32)
            for k, column in z.columns[e]:
                part = weights[:, column : column + 1] * expert_out
                mixed[k] = part if mixed[k] is None else mixed[k] + part
            dense = dense + dot_nt(first_refs[index][i], w_first_ref[e, : z.dense, :])
    for k in range(z.tasks + 1):
        mixed_ref[k] = mixed[k].astype(bf16)
    dense_ref[...] = dense


def unpack_kernel(z, group, grad_scale, place_ref, *refs):
    pieces = refs[: len(SPANS)]
    small_ref = refs[len(SPANS)]
    w_first_ref, w_second_ref = refs[len(SPANS) + 1 : len(SPANS) + 3]
    table_ref, gate_task_ref, gate_shared_ref, gate_bias_ref = refs[len(SPANS) + 3 :][:4]
    sum_refs = refs[len(SPANS) + 7 :][:4]
    small_s = refs[-1]
    for index, span in enumerate(SPANS):
        low_bits = lax.bitwise_and(place_ref[index], group - 1)
        for j in range(group):
            block = lax.bitwise_xor(low_bits, j)
            line = 0
            for e in range(*span):
                for ref, count in ((w_first_ref, z.first_rows), (w_second_ref, z.second_rows)):
                    for h in range(z.halves):
                        ref[e, j * count : (j + 1) * count, h * LANES : (h + 1) * LANES] = (
                            pieces[index][block, line : line + count, :] * grad_scale
                        )
                        line += count

    @pl.when(pl.program_id(0) == 0)
    def _():
        place = place_ref[len(SPANS) - 1]
        for a in range(SHARDS):
            small_s[a * z.small_rows : (a + 1) * z.small_rows, :] = (
                small_ref[lax.bitwise_xor(place, a)] * grad_scale
            )
        for low in range(z.low):
            table_ref[low * z.high : (low + 1) * z.high, :] = small_s[
                : z.high, low * z.emb : (low + 1) * z.emb
            ]
        for q in range(z.d_in // LANES):
            line = z.gate_at + q * 16
            found = small_s[line : line + 16, :].T
            lines = slice(q * LANES, (q + 1) * LANES)
            for k in range(z.tasks):
                gate_task_ref[k, lines, :] = found[:, k * z.gate : (k + 1) * z.gate]
            gate_shared_ref[lines, :] = found[:, z.tasks * z.gate : z.width]
        gate_bias_ref[...] = small_s[z.bias_at : z.bias_at + 1, :]
        for e in range(z.experts):
            for q in range(4):
                for h in range(z.halves):
                    line = z.sums_at + e * z.sum_rows + q * z.halves + h
                    sum_refs[q][e : e + 1, h * LANES : (h + 1) * LANES] = small_s[
                        line : line + 1, :
                    ]


VMEM = pl.BlockSpec(memory_space=pltpu.VMEM)
SMEM = pl.BlockSpec(memory_space=pltpu.SMEM)


def shape_of(shape, dtype=f32):
    return jax.ShapeDtypeStruct(shape, dtype)


def run_experts(z, index, places, params, cotangent, extra, earlier):
    first = index == 0
    last = index == len(SPANS) - 1
    span = SPANS[index]
    n = span[1] - span[0]
    w_first, b_first, w_second, b_second, gain, bias = params

    def experts_block(array):
        return pl.BlockSpec(
            (n,) + array.shape[1:], lambda at: (span[0] // n, 0, 0), memory_space=pltpu.VMEM
        )

    def whole(array):
        return pl.BlockSpec(array.shape, lambda at: (0,) * array.ndim, memory_space=pltpu.VMEM)

    operands = [places, w_first, b_first, w_second, b_second, gain, bias, cotangent]
    operands += list(extra) + list(earlier)
    in_specs = [SMEM] + [
        experts_block(v) if v is w_first or v is w_second else whole(v) for v in operands[1:]
    ]
    rows = z.rows
    out_shape = [
        shape_of((SHARDS, z.piece_rows(index), LANES)),
        shape_of((n, rows, z.out), bf16),
        shape_of((n, rows, z.hidden), bf16),
    ]
    if first:
        out_shape += [shape_of((rows, z.d_in), bf16), shape_of((rows, LANES))]
    if last:
        out_shape += [shape_of((rows, LANES), bf16)]
    else:
        out_shape += [shape_of((2, rows, LANES)), shape_of((n * z.sum_rows, LANES))]
    scratch = [
        pltpu.VMEM((n, rows, z.hidden), bf16),
        pltpu.VMEM((n, rows, z.out), bf16),
        pltpu.VMEM((n, z.d_in + z.hidden, z.out), f32),
        pltpu.VMEM((n, 4, 8, z.out), f32),
    ]
    if last:
        scratch += [
            pltpu.VMEM((LANES, z.d_in), f32),
            pltpu.VMEM((z.small_rows * SHARDS, LANES), f32),
        ]
    macs = rows * n * 3 * (z.d_in * z.hidden + z.hidden * z.out)
    return pl.pallas_call(
        functools.partial(experts_kernel, z, index),
        grid=(1,),
        in_specs=in_specs,
        out_specs=[whole(v) for v in out_shape],
        out_shape=out_shape,
        scratch_shapes=scratch,
        compiler_params=pltpu.CompilerParams(vmem_limit_bytes=48 * MIB),
        cost_estimate=pl.CostEstimate(
            flops=2 * macs, bytes_accessed=6 * MIB, transcendentals=rows * n * z.hidden
        ),
        name="experts_%d" % index,
    )(*operands)


def run_outputs(z, weights, logit_grad, w_first, gain, bias, gates, normed, firsts):
    block = z.chunk

    def whole(array):
        return pl.BlockSpec(array.shape, lambda at: (0,) * array.ndim)

    def rows_of(array):
        if array.ndim == 2:
            return pl.BlockSpec((block, array.shape[1]), lambda at: (at, 0))
        return pl.BlockSpec((array.shape[0], block, array.shape[2]), lambda at: (0, at, 0))

    out_shape = [shape_of((z.tasks + 1, z.rows, z.out), bf16), shape_of((z.rows, z.dense))]
    return pl.pallas_call(
        functools.partial(outputs_kernel, z),
        grid=(z.rows // block,),
        in_specs=[rows_of(weights), rows_of(logit_grad)]
        + [whole(v) for v in (w_first, gain, bias) + gates]
        + [rows_of(v) for v in normed + firsts],
        out_specs=[rows_of(v) for v in out_shape],
        out_shape=out_shape,
        compiler_params=pltpu.CompilerParams(vmem_limit_bytes=32 * MIB),
        cost_estimate=pl.CostEstimate(
            flops=2 * z.rows * z.experts * z.hidden * z.dense,
            bytes_accessed=11 * MIB,
            transcendentals=0,
        ),
        name="outputs",
    )(weights, logit_grad, w_first, gain, bias, *gates, *normed, *firsts)


def run_unpack(z, places, pieces, grad_scale):
    group = 4
    steps = SHARDS // group

    def piece_spec(index):
        rows = (SPANS[index][1] - SPANS[index][0]) * z.expert_rows
        return pl.BlockSpec(
            (group, rows, LANES),
            lambda at, place: (lax.bitwise_xor(at, lax.div(place[index], group)), 0, 0),
        )

    small = pieces[-1][:, -z.small_rows :, :]

    def whole(array):
        return pl.BlockSpec(array.shape, lambda at, place: (0,) * array.ndim)

    out_shape = [
        shape_of((z.experts, z.d_in, z.hidden)),
        shape_of((z.experts, z.hidden, z.out)),
        shape_of((z.vocab, z.emb)),
        shape_of((z.tasks, z.d_in, z.gate)),
        shape_of((z.d_in, z.experts)),
        shape_of((1, LANES)),
    ] + [shape_of((z.experts, z.out))] * 4

    def sharded(array):
        return pl.BlockSpec(
            (array.shape[0], array.shape[1] // steps, array.shape[2]), lambda at, place: (0, at, 0)
        )

    pieces = [v if v.shape[1] % z.expert_rows == 0 else v[:, : -z.small_rows] for v in pieces]
    return pl.pallas_call(
        functools.partial(unpack_kernel, z, group, grad_scale),
        grid_spec=pltpu.PrefetchScalarGridSpec(
            num_scalar_prefetch=1,
            grid=(steps,),
            in_specs=[piece_spec(i) for i in range(len(SPANS))] + [whole(small)],
            out_specs=[sharded(out_shape[0]), sharded(out_shape[1])]
            + [whole(v) for v in out_shape[2:]],
            scratch_shapes=[pltpu.VMEM((z.small_rows * SHARDS, LANES), f32)],
        ),
        out_shape=out_shape,
        compiler_params=pltpu.CompilerParams(vmem_limit_bytes=32 * MIB),
        cost_estimate=pl.CostEstimate(flops=0, bytes_accessed=10 * MIB, transcendentals=0),
        name="unpack",
    )(places, *pieces, small)


class Ring:
    FLIPS = {"c": 1, "x": 2, "y": 4, "1": 8, "2": 16}

    def __init__(self, fits):
        self.fits = fits

    def exchange(self, value, axis):
        flip = self.FLIPS[axis]
        return lax.ppermute(value, BOTH, [(i, i ^ flip) for i in range(SHARDS)])

    def place(self, order):
        if not self.fits:
            return jnp.int32(0)
        device = lax.axis_index("wide") * 4 + lax.axis_index("narrow")
        result = jnp.int32(0)
        for axis in order:
            bit = lax.rem(lax.div(device, self.FLIPS[axis]), 2)
            result = result * 2 + bit
        return result

    def reduce(self, pieces):
        if not self.fits:
            return lax.psum(pieces, BOTH)
        pieces = list(pieces)
        for stage in range(5):
            halves = [v.shape[0] // 2 for v in pieces]
            got = [
                self.exchange(v[h:], order[stage])
                for v, h, order in zip(pieces, halves, ORDERS)
            ]
            pieces = [v[:h] + g for v, h, g in zip(pieces, halves, got)]
        for stage in reversed(range(5)):
            got = [self.exchange(v, order[stage]) for v, order in zip(pieces, ORDERS)]
            pieces = [jnp.concatenate([v, g], axis=0) for v, g in zip(pieces, got)]
        return pieces


def local(
    fits,
    dense_feats,
    sparse_ids,
    presence,
    embed_table,
    w_first,
    b_first,
    w_second,
    b_second,
    ln_gain,
    ln_bias,
    gate_task,
    gate_task_bias,
    gate_shared,
    gate_shared_bias,
    cotangent,
):
    z = Sizes(dense_feats, sparse_ids, embed_table, w_first, w_second, gate_task)
    ring = Ring(fits)
    places = jnp.stack([ring.place(order) for order in ORDERS])
    params = (w_first, b_first, w_second, b_second, ln_gain, ln_bias)
    pieces, normed, firsts, sums = [], [], [], []
    extra = (
        dense_feats,
        sparse_ids,
        presence,
        embed_table,
        gate_task,
        gate_task_bias,
        gate_shared,
        gate_shared_bias.reshape(1, -1),
    )
    for index in range(len(SPANS)):
        last = index == len(SPANS) - 1
        found = run_experts(
            z, index, places, params, cotangent, extra, sums if last else []
        )
        pieces.append(found[0])
        normed.append(found[1])
        firsts.append(found[2])
        rest = found[3:]
        if index == 0:
            features, weights = rest[:2]
            rest = rest[2:]
        if last:
            logit_grad = rest[0]
        else:
            part, sum_rows = rest
            sums.append(sum_rows)
            extra = (features, weights, part)
            if index == len(SPANS) - 2:
                extra += (sparse_ids, presence, gate_task, gate_shared)
    pieces = ring.reduce(pieces)
    mixed, dense_grad = run_outputs(
        z, weights, logit_grad, w_first, ln_gain, ln_bias, (gate_task, gate_shared), normed, firsts
    )
    total_rows = z.rows * lax.axis_size("wide") * lax.axis_size("narrow")
    grads = run_unpack(z, places, pieces, 1.0 / math.sqrt(total_rows))
    w_first_grad, w_second_grad, table_grad, gate_task_grad, gate_shared_grad, bias_row = grads[:6]
    b_first_grad, b_second_grad, gain_grad, bias_grad = grads[6:]
    task_width = z.tasks * z.gate
    return (
        mixed,
        dense_grad,
        table_grad,
        w_first_grad,
        b_first_grad,
        w_second_grad,
        b_second_grad,
        gain_grad,
        bias_grad,
        gate_task_grad,
        bias_row[0, :task_width].reshape(z.tasks, z.gate),
        gate_shared_grad,
        bias_row[0, task_width : z.width],
    )


def solution(mesh):
    fits = (mesh.shape["wide"], mesh.shape["narrow"]) == (8, 4)
    rows = P(BOTH, None)
    middle = P(None, BOTH, None)
    return jax.shard_map(
        functools.partial(local, fits),
        mesh=mesh,
        in_specs=(rows, rows, rows) + (P(),) * 11 + (middle,),
        out_specs=(middle, rows) + (P(),) * 11,
        check_vma=False,
    )
```

profile of v0, /device:TPU:0, one launch (start us, length us, event | category | flops | bytes accessed | tf_op | source)
XLA Modules:
  0.0 144.4 jit_solution(13381705799134769106)
XLA Ops:
  5.7 16.1 %experts_0.1 = (f32[32,96,128]{2,1,0:T(8,128)}, bf16[2,1024,256]{2,1,0:T(8,128)(2,1)S(1)}, bf16[2,1024,256]{2,1,0:T(8,128)(2,1)S(1)}, bf16[1024,512]{1,0:T(8,128...) custom-call(s32[3]{0:T(128)S(1)} %pad_add_fusion.refs_0_.place_ref, ...), custom_call_target="tpu_custom_call" | custom-call | flops 2415919104 | bytes 6291456 | tf_op jit(solution)/shard_map/experts_0/pallas_call | solution.py:470
  21.8 1.3 slice.103
  23.6 11.3 %experts_1.1 = (f32[32,96,128]{2,1,0:T(8,128)}, bf16[2,1024,256]{2,1,0:T(8,128)(2,1)S(1)}, bf16[2,1024,256]{2,1,0:T(8,128)(2,1)S(1)}, f32[2,1024,128]{2,1,0:T(8,128)S(1)}, f32[16,128]{1,0:T(8,128)S(1)}) custom-call(s32[3]{0:T(128)S(1)} %pad_add_fusion.refs_0_.place_ref, bf16[6,512,256]{2,1,0:T(8,128)(2,1)} %refs_2_.7, bf16[6,256]{1,0:T(8,128)(2,1)S(1)} %copy-done.5, ...), custom_call_target="tpu_custom_call" | custom-call | flops 2415919104 | bytes 6291456 | tf_op jit(solution)/shard_map/experts_1/pallas_call | solution.py:470
  34.9 1.6 %slice.113 = f32[16,96,128]{2,1,0:T(8,128)S(1)} slice(f32[32,96,128]{2,1,0:T(8,128)} %get-tuple-element.57), slice={[16:32], [0:96], [0:128]} | slice | bytes 1572864 | tf_op jit(solution)/shard_map/slice | solution.py:590
  36.6 14.3 %experts_2.1 = (f32[32,104,128]{2,1,0:T(8,128)}, bf16[2,1024,256]{2,1,0:T(8,128)(2,1)S(1)}, bf16[2,1024,256]{2,1,0:T(8,128)(2,1)S(1)}, bf16[1024,128]{1,0:T(8,128)(2,1)S(1)}) custom-call(s32[3]{0:T(128)S(1)} %pad_add_fusion.refs_0_.place_ref, bf16[6,512,256]{2,1,0:T(8,128)(2,1)} %refs_2_.7, bf16[6,256]{1,0:T(8,128)(2,1)S(1)} %copy-done.5, ...), custom_call_target="tpu_custom_call" | custom-call | flops 2415919104 | bytes 6291456 | tf_op jit(solution)/shard_map/experts_2/pallas_call | solution.py:470
  50.9 1.3 slice.123
  52.8 2.8 %collective-permute-start.1 = (f32[8,96,128]{2,1,0:T(8,128)S(1)}, f32[8,96,128]{2,1,0:T(8,128)S(1)}, u32[]{:S(2)}, u32[]{:S(2)}) collective-permute-start(f32[8,96,128]{2,1,0:T(8,128)S(1)} %slice.137), channel_id=1, source_target_pairs={{0,2},{1,3},{2,0},{3,1},{4,6},{5,7},{6,4},{7,5},{8,10},{9,11},{10,... | collective-permute-start | bytes 1179656 | tf_op jit(solution)/shard_map/ppermute | solution.py:571
  55.8 1.6 %collective-permute-start.11 = (f32[8,96,128]{2,1,0:T(8,128)S(1)}, f32[8,96,128]{2,1,0:T(8,128)S(1)}, u32[]{:S(2)}, u32[]{:S(2)}) collective-permute-start(f32[8,96,128]{2,1,0:T(8,128)S(1)} %slice.145), channel_id=1, source_target_pairs={{0,4},{1,5},{2,6},{3,7},{4,0},{5,1},{6,2},{7,3},{8,12},{9,13},{10,... | collective-permute-start | bytes 1179656 | tf_op jit(solution)/shard_map/ppermute | solution.py:571
  57.5 1.7 %collective-permute-start.21 = (f32[8,104,128]{2,1,0:T(8,128)S(1)}, f32[8,104,128]{2,1,0:T(8,128)S(1)}, u32[]{:S(2)}, u32[]{:S(2)}) collective-permute-start(f32[8,104,128]{2,1,0:T(8,128)S(1)} %slice.153), channel_id=1, source_target_pairs={{0,8},{1,9},{2,10},{3,11},{4,12},{5,13},{6,14},{7,15},{8,0},{9,1},... | collective-permute-start | bytes 1277960 | tf_op jit(solution)/shard_map/ppermute | solution.py:571
  59.1 6.1 %collective-permute-done.1 = f32[8,96,128]{2,1,0:T(8,128)S(1)} collective-permute-done((f32[8,96,128]{2,1,0:T(8,128)S(1)}, f32[8,96,128]{2,1,0:T(8,128)S(1)}, u32[]{:S(2)}, u32[]{:S(2)}) %collective-permute-start.1) | collective-permute-done | bytes 393248 | tf_op jit(solution)/shard_map/ppermute | solution.py:571
  65.3 1.8 %collective-permute-start.2 = (f32[4,96,128]{2,1,0:T(8,128)S(1)}, f32[4,96,128]{2,1,0:T(8,128)S(1)}, u32[]{:S(2)}, u32[]{:S(2)}) collective-permute-start(f32[4,96,128]{2,1,0:T(8,128)S(1)} %slice.139), channel_id=1, source_target_pairs={{0,4},{1,5},{2,6},{3,7},{4,0},{5,1},{6,2},{7,3},{8,12},{9,13},{10,... | collective-permute-start | bytes 589832 | tf_op jit(solution)/shard_map/ppermute | solution.py:571
  67.2 1.6 %collective-permute-start.12 = (f32[4,96,128]{2,1,0:T(8,128)S(1)}, f32[4,96,128]{2,1,0:T(8,128)S(1)}, u32[]{:S(2)}, u32[]{:S(2)}) collective-permute-start(f32[4,96,128]{2,1,0:T(8,128)S(1)} %slice.147), channel_id=1, source_target_pairs={{0,8},{1,9},{2,10},{3,11},{4,12},{5,13},{6,14},{7,15},{8,0},{9,1},... | collective-permute-start | bytes 589832 | tf_op jit(solution)/shard_map/ppermute | solution.py:571
  69.1 2.7 %collective-permute-start.22 = (f32[4,104,128]{2,1,0:T(8,128)S(1)}, f32[4,104,128]{2,1,0:T(8,128)S(1)}, u32[]{:S(2)}, u32[]{:S(2)}) collective-permute-start(f32[4,104,128]{2,1,0:T(8,128)S(1)} %slice.155), channel_id=1, source_target_pairs={{0,16},{1,17},{2,18},{3,19},{4,20},{5,21},{6,22},{7,23},{8,24},{9,... | collective-permute-start | bytes 638984 | tf_op jit(solution)/shard_map/ppermute | solution.py:571
  72.0 1.6 %collective-permute-start.3 = (f32[2,96,128]{2,1,0:T(8,128)S(1)}, f32[2,96,128]{2,1,0:T(8,128)S(1)}, u32[]{:S(2)}, u32[]{:S(2)}) collective-permute-start(f32[2,96,128]{2,1,0:T(8,128)S(1)} %slice.141), channel_id=1, source_target_pairs={{0,8},{1,9},{2,10},{3,11},{4,12},{5,13},{6,14},{7,15},{8,0},{9,1},... | collective-permute-start | bytes 294920 | tf_op jit(solution)/shard_map/ppermute | solution.py:571
  73.5 4.6 %collective-permute-done.12 = f32[4,96,128]{2,1,0:T(8,128)S(1)} collective-permute-done((f32[4,96,128]{2,1,0:T(8,128)S(1)}, f32[4,96,128]{2,1,0:T(8,128)S(1)}, u32[]{:S(2)}, u32[]{:S(2)}) %collective-permute-start.12) | collective-permute-done | bytes 196640 | tf_op jit(solution)/shard_map/ppermute | solution.py:571
  78.3 1.9 %collective-permute-done.3 = f32[2,96,128]{2,1,0:T(8,128)S(1)} collective-permute-done((f32[2,96,128]{2,1,0:T(8,128)S(1)}, f32[2,96,128]{2,1,0:T(8,128)S(1)}, u32[]{:S(2)}, u32[]{:S(2)}) %collective-permute-start.3) | collective-permute-done | bytes 98336 | tf_op jit(solution)/shard_map/ppermute | solution.py:571
  80.2 3.4 %collective-permute-start.4 = (f32[1,96,128]{2,1,0:T(8,128)S(1)}, f32[1,96,128]{2,1,0:T(8,128)S(1)}, u32[]{:S(2)}, u32[]{:S(2)}) collective-permute-start(f32[1,96,128]{2,1,0:T(8,128)S(1)} %slice.143), channel_id=1, source_target_pairs={{0,16},{1,17},{2,18},{3,19},{4,20},{5,21},{6,22},{7,23},{8,24},{9,... | collective-permute-start | bytes 147464 | tf_op jit(solution)/shard_map/ppermute | solution.py:571
  83.6 2.2 %collective-permute-done.13 = f32[2,96,128]{2,1,0:T(8,128)S(1)} collective-permute-done((f32[2,96,128]{2,1,0:T(8,128)S(1)}, f32[2,96,128]{2,1,0:T(8,128)S(1)}, u32[]{:S(2)}, u32[]{:S(2)}) %collective-permute-start.13) | collective-permute-done | bytes 98336 | tf_op jit(solution)/shard_map/ppermute | solution.py:571
  85.9 1.5 %collective-permute-start.14 = (f32[1,96,128]{2,1,0:T(8,128)S(1)}, f32[1,96,128]{2,1,0:T(8,128)S(1)}, u32[]{:S(2)}, u32[]{:S(2)}) collective-permute-start(f32[1,96,128]{2,1,0:T(8,128)S(1)} %slice.151), channel_id=1, source_target_pairs={{0,2},{1,3},{2,0},{3,1},{4,6},{5,7},{6,4},{7,5},{8,10},{9,11},{10,... | collective-permute-start | bytes 147464 | tf_op jit(solution)/shard_map/ppermute | solution.py:571
  88.8 1.3 collective-permute-done.14
  90.1 1.5 %collective-permute-start.15 = (f32[1,96,128]{2,1,0:T(8,128)S(1)}, f32[1,96,128]{2,1,0:T(8,128)S(1)}, u32[]{:S(2)}, u32[]{:S(2)}) collective-permute-start(f32[1,96,128]{2,1,0:T(8,128)S(1)} %get-tuple-element.85), channel_id=1, source_target_pairs={{0,2},{1,3},{2,0},{3,1},{4,6},{5,7},{6,4},{7,5},{8,10},{9,11},{10,... | collective-permute-start | bytes 147464 | tf_op jit(solution)/shard_map/ppermute | solution.py:571
  91.6 1.7 %collective-permute-done.5 = f32[1,96,128]{2,1,0:T(8,128)S(1)} collective-permute-done((f32[1,96,128]{2,1,0:T(8,128)S(1)}, f32[1,96,128]{2,1,0:T(8,128)S(1)}, u32[]{:S(2)}, u32[]{:S(2)}) %collective-permute-start.5) | collective-permute-done | bytes 49184 | tf_op jit(solution)/shard_map/ppermute | solution.py:571
  93.3 2.6 %collective-permute-start.6 = (f32[2,96,128]{2,1,0:T(8,128)S(1)}, f32[2,96,128]{2,1,0:T(8,128)S(1)}, u32[]{:S(2)}, u32[]{:S(2)}) collective-permute-start(f32[2,96,128]{2,1,0:T(8,128)S(1)} %pad_maximum_fusion.7), channel_id=1, source_target_pairs={{0,8},{1,9},{2,10},{3,11},{4,12},{5,13},{6,14},{7,15},{8,0},{9,1},... | collective-permute-start | bytes 294920 | tf_op jit(solution)/shard_map/ppermute | solution.py:571
  95.9 2.5 %collective-permute-start.16 = (f32[2,96,128]{2,1,0:T(8,128)S(1)}, f32[2,96,128]{2,1,0:T(8,128)S(1)}, u32[]{:S(2)}, u32[]{:S(2)}) collective-permute-start(f32[2,96,128]{2,1,0:T(8,128)S(1)} %pad_maximum_fusion.8), channel_id=1, source_target_pairs={{0,16},{1,17},{2,18},{3,19},{4,20},{5,21},{6,22},{7,23},{8,24},{9,... | collective-permute-start | bytes 294920 | tf_op jit(solution)/shard_map/ppermute | solution.py:571
  99.3 3.7 %collective-permute-done.24 = f32[1,104,128]{2,1,0:T(8,128)S(1)} collective-permute-done((f32[1,104,128]{2,1,0:T(8,128)S(1)}, f32[1,104,128]{2,1,0:T(8,128)S(1)}, u32[]{:S(2)}, u32[]{:S(2)}) %collective-permute-start.24) | collective-permute-done | bytes 53280 | tf_op jit(solution)/shard_map/ppermute | solution.py:571
  105.2 1.5 %collective-permute-start.17 = (f32[4,96,128]{2,1,0:T(8,128)S(1)}, f32[4,96,128]{2,1,0:T(8,128)S(1)}, u32[]{:S(2)}, u32[]{:S(2)}) collective-permute-start(f32[4,96,128]{2,1,0:T(8,128)S(1)} %pad_maximum_fusion.5), channel_id=1, source_target_pairs={{0,8},{1,9},{2,10},{3,11},{4,12},{5,13},{6,14},{7,15},{8,0},{9,1},... | collective-permute-start | bytes 589832 | tf_op jit(solution)/shard_map/ppermute | solution.py:571
  108.4 4.2 %collective-permute-done.26 = f32[2,104,128]{2,1,0:T(8,128)S(1)} collective-permute-done((f32[2,104,128]{2,1,0:T(8,128)S(1)}, f32[2,104,128]{2,1,0:T(8,128)S(1)}, u32[]{:S(2)}, u32[]{:S(2)}) %collective-permute-start.26) | collective-permute-done | bytes 106528 | tf_op jit(solution)/shard_map/ppermute | solution.py:571
  114.6 2.0 %collective-permute-start.18 = (f32[8,96,128]{2,1,0:T(8,128)S(1)}, f32[8,96,128]{2,1,0:T(8,128)S(1)}, u32[]{:S(2)}, u32[]{:S(2)}) collective-permute-start(f32[8,96,128]{2,1,0:T(8,128)S(1)} %pad_maximum_fusion.2), channel_id=1, source_target_pairs={{0,4},{1,5},{2,6},{3,7},{4,0},{5,1},{6,2},{7,3},{8,12},{9,13},{10,... | collective-permute-start | bytes 1179656 | tf_op jit(solution)/shard_map/ppermute | solution.py:571
  116.6 5.2 %collective-permute-done.27 = f32[4,104,128]{2,1,0:T(8,128)S(1)} collective-permute-done((f32[4,104,128]{2,1,0:T(8,128)S(1)}, f32[4,104,128]{2,1,0:T(8,128)S(1)}, u32[]{:S(2)}, u32[]{:S(2)}) %collective-permute-start.27) | collective-permute-done | bytes 213024 | tf_op jit(solution)/shard_map/ppermute | solution.py:571
  123.2 6.9 %collective-permute-done.28 = f32[8,104,128]{2,1,0:T(8,128)S(1)} collective-permute-done((f32[8,104,128]{2,1,0:T(8,128)S(1)}, f32[8,104,128]{2,1,0:T(8,128)S(1)}, u32[]{:S(2)}, u32[]{:S(2)}) %collective-permute-start.28) | collective-permute-done | bytes 426016 | tf_op jit(solution)/shard_map/ppermute | solution.py:571
  130.2 5.6 %outputs.1 = (bf16[3,1024,256]{2,1,0:T(8,128)(2,1)}, f32[1024,384]{1,0:T(8,128)}) custom-call(f32[1024,128]{1,0:T(8,128)S(1)} %get-tuple-element.41.refs_9_.refs_0_, bf16[1024,128]{1,0:T(8,128)(2,1)S(1)} %get-tuple-element.47.refs_1_, bf16[6,512,256]{2,1,0:T(8,128)(2,1)S(1)} %copy-done, bf16[6,256]{1,0:T(8,128)(2,1)S(1)} %copy-done.1, ...), custom_call_target="tpu_custom_call" | custom-call | flops 1207959552 | bytes 11534336 | tf_op jit(solution)/shard_map/outputs/pallas_call | solution.py:497
  136.2 4.7 %unpack.1 = (f32[6,512,256]{2,1,0:T(8,128)}, f32[6,256,256]{2,1,0:T(8,128)}, f32[1024,16]{1,0:T(8,128)S(1)}, f32[2,512,4]{2,1,0:T(8,128)S(1)}, f32[512,6]{1,0:T(...) custom-call(s32[3]{0:T(128)S(1)} %pad_add_fusion.refs_0_.place_ref, ...), custom_call_target="tpu_custom_call" | custom-call | bytes 10485760 | tf_op jit(solution)/shard_map/unpack/pallas_call | solution.py:546
  (132 shorter events, 20.5 us)
Async XLA Ops:
  0.6 5.0 %copy-start.2 = (bf16[6,256]{1,0:T(8,128)(2,1)S(1)}, bf16[6,256]{1,0:T(8,128)(2,1)}, u32[]{:S(2)}) copy-start(bf16[6,256]{1,0:T(8,128)(2,1)} %refs_4_.7) | copy-start | bytes 9220
  23.1 29.6 %collective-permute-start = (f32[16,96,128]{2,1,0:T(8,128)S(1)}, f32[16,96,128]{2,1,0:T(8,128)S(1)}, u32[]{:S(2)}, u32[]{:S(2)}) collective-permute-start(f32[16,96,128]{2,1,0:T(8,128)S(1)} %slice.103), channel_id=1, source_target_pairs={{0,1},{1,0},{2,3},{3,2},{4,5},{5,4},{6,7},{7,6},{8,9},{9,8},{10,11... | collective-permute-start | bytes 2359304 | tf_op jit(solution)/shard_map/ppermute | solution.py:571
  36.4 19.2 %collective-permute-start.10 = (f32[16,96,128]{2,1,0:T(8,128)S(1)}, f32[16,96,128]{2,1,0:T(8,128)S(1)}, u32[]{:S(2)}, u32[]{:S(2)}) collective-permute-start(f32[16,96,128]{2,1,0:T(8,128)S(1)} %slice.113), channel_id=1, source_target_pairs={{0,1},{1,0},{2,3},{3,2},{4,5},{5,4},{6,7},{7,6},{8,9},{9,8},{10,11... | collective-permute-start | bytes 2359304 | tf_op jit(solution)/shard_map/ppermute | solution.py:571
  52.2 5.1 %collective-permute-start.20 = (f32[16,104,128]{2,1,0:T(8,128)S(1)}, f32[16,104,128]{2,1,0:T(8,128)S(1)}, u32[]{:S(2)}, u32[]{:S(2)}) collective-permute-start(f32[16,104,128]{2,1,0:T(8,128)S(1)} %slice.123), channel_id=1, source_target_pairs={{0,1},{1,0},{2,3},{3,2},{4,5},{5,4},{6,7},{7,6},{8,9},{9,8},{10,11... | collective-permute-start | bytes 2555912 | tf_op jit(solution)/shard_map/ppermute | solution.py:571
  52.8 12.3 %collective-permute-start.1 = (f32[8,96,128]{2,1,0:T(8,128)S(1)}, f32[8,96,128]{2,1,0:T(8,128)S(1)}, u32[]{:S(2)}, u32[]{:S(2)}) collective-permute-start(f32[8,96,128]{2,1,0:T(8,128)S(1)} %slice.137), channel_id=1, source_target_pairs={{0,2},{1,3},{2,0},{3,1},{4,6},{5,7},{6,4},{7,5},{8,10},{9,11},{10,... | collective-permute-start | bytes 1179656 | tf_op jit(solution)/shard_map/ppermute | solution.py:571
  55.8 11.3 %collective-permute-start.11 = (f32[8,96,128]{2,1,0:T(8,128)S(1)}, f32[8,96,128]{2,1,0:T(8,128)S(1)}, u32[]{:S(2)}, u32[]{:S(2)}) collective-permute-start(f32[8,96,128]{2,1,0:T(8,128)S(1)} %slice.145), channel_id=1, source_target_pairs={{0,4},{1,5},{2,6},{3,7},{4,0},{5,1},{6,2},{7,3},{8,12},{9,13},{10,... | collective-permute-start | bytes 1179656 | tf_op jit(solution)/shard_map/ppermute | solution.py:571
  57.5 11.5 %collective-permute-start.21 = (f32[8,104,128]{2,1,0:T(8,128)S(1)}, f32[8,104,128]{2,1,0:T(8,128)S(1)}, u32[]{:S(2)}, u32[]{:S(2)}) collective-permute-start(f32[8,104,128]{2,1,0:T(8,128)S(1)} %slice.153), channel_id=1, source_target_pairs={{0,8},{1,9},{2,10},{3,11},{4,12},{5,13},{6,14},{7,15},{8,0},{9,1},... | collective-permute-start | bytes 1277960 | tf_op jit(solution)/shard_map/ppermute | solution.py:571
  65.3 6.6 %collective-permute-start.2 = (f32[4,96,128]{2,1,0:T(8,128)S(1)}, f32[4,96,128]{2,1,0:T(8,128)S(1)}, u32[]{:S(2)}, u32[]{:S(2)}) collective-permute-start(f32[4,96,128]{2,1,0:T(8,128)S(1)} %slice.139), channel_id=1, source_target_pairs={{0,4},{1,5},{2,6},{3,7},{4,0},{5,1},{6,2},{7,3},{8,12},{9,13},{10,... | collective-permute-start | bytes 589832 | tf_op jit(solution)/shard_map/ppermute | solution.py:571
  67.2 11.0 %collective-permute-start.12 = (f32[4,96,128]{2,1,0:T(8,128)S(1)}, f32[4,96,128]{2,1,0:T(8,128)S(1)}, u32[]{:S(2)}, u32[]{:S(2)}) collective-permute-start(f32[4,96,128]{2,1,0:T(8,128)S(1)} %slice.147), channel_id=1, source_target_pairs={{0,8},{1,9},{2,10},{3,11},{4,12},{5,13},{6,14},{7,15},{8,0},{9,1},... | collective-permute-start | bytes 589832 | tf_op jit(solution)/shard_map/ppermute | solution.py:571
  69.1 18.3 %collective-permute-start.22 = (f32[4,104,128]{2,1,0:T(8,128)S(1)}, f32[4,104,128]{2,1,0:T(8,128)S(1)}, u32[]{:S(2)}, u32[]{:S(2)}) collective-permute-start(f32[4,104,128]{2,1,0:T(8,128)S(1)} %slice.155), channel_id=1, source_target_pairs={{0,16},{1,17},{2,18},{3,19},{4,20},{5,21},{6,22},{7,23},{8,24},{9,... | collective-permute-start | bytes 638984 | tf_op jit(solution)/shard_map/ppermute | solution.py:571
  72.0 8.2 %collective-permute-start.3 = (f32[2,96,128]{2,1,0:T(8,128)S(1)}, f32[2,96,128]{2,1,0:T(8,128)S(1)}, u32[]{:S(2)}, u32[]{:S(2)}) collective-permute-start(f32[2,96,128]{2,1,0:T(8,128)S(1)} %slice.141), channel_id=1, source_target_pairs={{0,8},{1,9},{2,10},{3,11},{4,12},{5,13},{6,14},{7,15},{8,0},{9,1},... | collective-permute-start | bytes 294920 | tf_op jit(solution)/shard_map/ppermute | solution.py:571
  78.2 7.7 %collective-permute-start.13 = (f32[2,96,128]{2,1,0:T(8,128)S(1)}, f32[2,96,128]{2,1,0:T(8,128)S(1)}, u32[]{:S(2)}, u32[]{:S(2)}) collective-permute-start(f32[2,96,128]{2,1,0:T(8,128)S(1)} %slice.149), channel_id=1, source_target_pairs={{0,16},{1,17},{2,18},{3,19},{4,20},{5,21},{6,22},{7,23},{8,24},{9,... | collective-permute-start | bytes 294920 | tf_op jit(solution)/shard_map/ppermute | solution.py:571
  80.2 7.9 %collective-permute-start.4 = (f32[1,96,128]{2,1,0:T(8,128)S(1)}, f32[1,96,128]{2,1,0:T(8,128)S(1)}, u32[]{:S(2)}, u32[]{:S(2)}) collective-permute-start(f32[1,96,128]{2,1,0:T(8,128)S(1)} %slice.143), channel_id=1, source_target_pairs={{0,16},{1,17},{2,18},{3,19},{4,20},{5,21},{6,22},{7,23},{8,24},{9,... | collective-permute-start | bytes 147464 | tf_op jit(solution)/shard_map/ppermute | solution.py:571
  85.9 4.2 %collective-permute-start.14 = (f32[1,96,128]{2,1,0:T(8,128)S(1)}, f32[1,96,128]{2,1,0:T(8,128)S(1)}, u32[]{:S(2)}, u32[]{:S(2)}) collective-permute-start(f32[1,96,128]{2,1,0:T(8,128)S(1)} %slice.151), channel_id=1, source_target_pairs={{0,2},{1,3},{2,0},{3,1},{4,6},{5,7},{6,4},{7,5},{8,10},{9,11},{10,... | collective-permute-start | bytes 147464 | tf_op jit(solution)/shard_map/ppermute | solution.py:571
  87.4 11.0 %collective-permute-start.23 = (f32[2,104,128]{2,1,0:T(8,128)S(1)}, f32[2,104,128]{2,1,0:T(8,128)S(1)}, u32[]{:S(2)}, u32[]{:S(2)}) collective-permute-start(f32[2,104,128]{2,1,0:T(8,128)S(1)} %slice.157), channel_id=1, source_target_pairs={{0,2},{1,3},{2,0},{3,1},{4,6},{5,7},{6,4},{7,5},{8,10},{9,11},{10,... | collective-permute-start | bytes 319496 | tf_op jit(solution)/shard_map/ppermute | solution.py:571
  88.1 5.2 %collective-permute-start.5 = (f32[1,96,128]{2,1,0:T(8,128)S(1)}, f32[1,96,128]{2,1,0:T(8,128)S(1)}, u32[]{:S(2)}, u32[]{:S(2)}) collective-permute-start(f32[1,96,128]{2,1,0:T(8,128)S(1)} %get-tuple-element.87), channel_id=1, source_target_pairs={{0,16},{1,17},{2,18},{3,19},{4,20},{5,21},{6,22},{7,23},{8,24},{9,... | collective-permute-start | bytes 147464 | tf_op jit(solution)/shard_map/ppermute | solution.py:571
  90.1 5.8 %collective-permute-start.15 = (f32[1,96,128]{2,1,0:T(8,128)S(1)}, f32[1,96,128]{2,1,0:T(8,128)S(1)}, u32[]{:S(2)}, u32[]{:S(2)}) collective-permute-start(f32[1,96,128]{2,1,0:T(8,128)S(1)} %get-tuple-element.85), channel_id=1, source_target_pairs={{0,2},{1,3},{2,0},{3,1},{4,6},{5,7},{6,4},{7,5},{8,10},{9,11},{10,... | collective-permute-start | bytes 147464 | tf_op jit(solution)/shard_map/ppermute | solution.py:571
  93.3 10.7 %collective-permute-start.6 = (f32[2,96,128]{2,1,0:T(8,128)S(1)}, f32[2,96,128]{2,1,0:T(8,128)S(1)}, u32[]{:S(2)}, u32[]{:S(2)}) collective-permute-start(f32[2,96,128]{2,1,0:T(8,128)S(1)} %pad_maximum_fusion.7), channel_id=1, source_target_pairs={{0,8},{1,9},{2,10},{3,11},{4,12},{5,13},{6,14},{7,15},{8,0},{9,1},... | collective-permute-start | bytes 294920 | tf_op jit(solution)/shard_map/ppermute | solution.py:571
  95.9 9.3 %collective-permute-start.16 = (f32[2,96,128]{2,1,0:T(8,128)S(1)}, f32[2,96,128]{2,1,0:T(8,128)S(1)}, u32[]{:S(2)}, u32[]{:S(2)}) collective-permute-start(f32[2,96,128]{2,1,0:T(8,128)S(1)} %pad_maximum_fusion.8), channel_id=1, source_target_pairs={{0,16},{1,17},{2,18},{3,19},{4,20},{5,21},{6,22},{7,23},{8,24},{9,... | collective-permute-start | bytes 294920 | tf_op jit(solution)/shard_map/ppermute | solution.py:571
  98.5 4.5 %collective-permute-start.24 = (f32[1,104,128]{2,1,0:T(8,128)S(1)}, f32[1,104,128]{2,1,0:T(8,128)S(1)}, u32[]{:S(2)}, u32[]{:S(2)}) collective-permute-start(f32[1,104,128]{2,1,0:T(8,128)S(1)} %slice.159), channel_id=1, source_target_pairs={{0,4},{1,5},{2,6},{3,7},{4,0},{5,1},{6,2},{7,3},{8,12},{9,13},{10,... | collective-permute-start | bytes 159752 | tf_op jit(solution)/shard_map/ppermute | solution.py:571
  103.0 4.2 %collective-permute-start.25 = (f32[1,104,128]{2,1,0:T(8,128)S(1)}, f32[1,104,128]{2,1,0:T(8,128)S(1)}, u32[]{:S(2)}, u32[]{:S(2)}) collective-permute-start(f32[1,104,128]{2,1,0:T(8,128)S(1)} %get-tuple-element.83), channel_id=1, source_target_pairs={{0,4},{1,5},{2,6},{3,7},{4,0},{5,1},{6,2},{7,3},{8,12},{9,13},{10,... | collective-permute-start | bytes 159752 | tf_op jit(solution)/shard_map/ppermute | solution.py:571
  104.0 9.8 %collective-permute-start.7 = (f32[4,96,128]{2,1,0:T(8,128)S(1)}, f32[4,96,128]{2,1,0:T(8,128)S(1)}, u32[]{:S(2)}, u32[]{:S(2)}) collective-permute-start(f32[4,96,128]{2,1,0:T(8,128)S(1)} %pad_maximum_fusion.4), channel_id=1, source_target_pairs={{0,4},{1,5},{2,6},{3,7},{4,0},{5,1},{6,2},{7,3},{8,12},{9,13},{10,... | collective-permute-start | bytes 589832 | tf_op jit(solution)/shard_map/ppermute | solution.py:571
  105.2 9.3 %collective-permute-start.17 = (f32[4,96,128]{2,1,0:T(8,128)S(1)}, f32[4,96,128]{2,1,0:T(8,128)S(1)}, u32[]{:S(2)}, u32[]{:S(2)}) collective-permute-start(f32[4,96,128]{2,1,0:T(8,128)S(1)} %pad_maximum_fusion.5), channel_id=1, source_target_pairs={{0,8},{1,9},{2,10},{3,11},{4,12},{5,13},{6,14},{7,15},{8,0},{9,1},... | collective-permute-start | bytes 589832 | tf_op jit(solution)/shard_map/ppermute | solution.py:571
  107.2 5.4 %collective-permute-start.26 = (f32[2,104,128]{2,1,0:T(8,128)S(1)}, f32[2,104,128]{2,1,0:T(8,128)S(1)}, u32[]{:S(2)}, u32[]{:S(2)}) collective-permute-start(f32[2,104,128]{2,1,0:T(8,128)S(1)} %pad_maximum_fusion.6), channel_id=1, source_target_pairs={{0,2},{1,3},{2,0},{3,1},{4,6},{5,7},{6,4},{7,5},{8,10},{9,11},{10,... | collective-permute-start | bytes 319496 | tf_op jit(solution)/shard_map/ppermute | solution.py:571
  112.7 9.1 %collective-permute-start.27 = (f32[4,104,128]{2,1,0:T(8,128)S(1)}, f32[4,104,128]{2,1,0:T(8,128)S(1)}, u32[]{:S(2)}, u32[]{:S(2)}) collective-permute-start(f32[4,104,128]{2,1,0:T(8,128)S(1)} %pad_maximum_fusion.3), channel_id=1, source_target_pairs={{0,16},{1,17},{2,18},{3,19},{4,20},{5,21},{6,22},{7,23},{8,24},{9,... | collective-permute-start | bytes 638984 | tf_op jit(solution)/shard_map/ppermute | solution.py:571
  113.8 8.6 %collective-permute-start.8 = (f32[8,96,128]{2,1,0:T(8,128)S(1)}, f32[8,96,128]{2,1,0:T(8,128)S(1)}, u32[]{:S(2)}, u32[]{:S(2)}) collective-permute-start(f32[8,96,128]{2,1,0:T(8,128)S(1)} %pad_maximum_fusion.1), channel_id=1, source_target_pairs={{0,2},{1,3},{2,0},{3,1},{4,6},{5,7},{6,4},{7,5},{8,10},{9,11},{10,... | collective-permute-start | bytes 1179656 | tf_op jit(solution)/shard_map/ppermute | solution.py:571
  114.6 8.0 %collective-permute-start.18 = (f32[8,96,128]{2,1,0:T(8,128)S(1)}, f32[8,96,128]{2,1,0:T(8,128)S(1)}, u32[]{:S(2)}, u32[]{:S(2)}) collective-permute-start(f32[8,96,128]{2,1,0:T(8,128)S(1)} %pad_maximum_fusion.2), channel_id=1, source_target_pairs={{0,4},{1,5},{2,6},{3,7},{4,0},{5,1},{6,2},{7,3},{8,12},{9,13},{10,... | collective-permute-start | bytes 1179656 | tf_op jit(solution)/shard_map/ppermute | solution.py:571
  121.9 8.2 %collective-permute-start.28 = (f32[8,104,128]{2,1,0:T(8,128)S(1)}, f32[8,104,128]{2,1,0:T(8,128)S(1)}, u32[]{:S(2)}, u32[]{:S(2)}) collective-permute-start(f32[8,104,128]{2,1,0:T(8,128)S(1)} %pad_maximum_fusion), channel_id=1, source_target_pairs={{0,8},{1,9},{2,10},{3,11},{4,12},{5,13},{6,14},{7,15},{8,0},{9,1},... | collective-permute-start | bytes 1277960 | tf_op jit(solution)/shard_map/ppermute | solution.py:571
  122.4 7.8 %copy-start = (bf16[6,512,256]{2,1,0:T(8,128)(2,1)S(1)}, bf16[6,512,256]{2,1,0:T(8,128)(2,1)}, u32[]{:S(2)}) copy-start(bf16[6,512,256]{2,1,0:T(8,128)(2,1)} %refs_2_.7) | copy-start | bytes 4718596
  122.5 13.3 %collective-permute-start.9 = (f32[16,96,128]{2,1,0:T(8,128)S(1)}, f32[16,96,128]{2,1,0:T(8,128)S(1)}, u32[]{:S(2)}, u32[]{:S(2)}) collective-permute-start(f32[16,96,128]{2,1,0:T(8,128)S(1)} %get-tuple-element.92), channel_id=1, source_target_pairs={{0,1},{1,0},{2,3},{3,2},{4,5},{5,4},{6,7},{7,6},{8,9},{9,8},{10,11... | collective-permute-start | bytes 2359304 | tf_op jit(solution)/shard_map/ppermute | solution.py:571
  122.6 13.2 %collective-permute-start.19 = (f32[16,96,128]{2,1,0:T(8,128)S(1)}, f32[16,96,128]{2,1,0:T(8,128)S(1)}, u32[]{:S(2)}, u32[]{:S(2)}) collective-permute-start(f32[16,96,128]{2,1,0:T(8,128)S(1)} %get-tuple-element.90), channel_id=1, source_target_pairs={{0,1},{1,0},{2,3},{3,2},{4,5},{5,4},{6,7},{7,6},{8,9},{9,8},{10,11... | collective-permute-start | bytes 2359304 | tf_op jit(solution)/shard_map/ppermute | solution.py:571
  130.1 5.8 %collective-permute-start.29 = (f32[16,104,128]{2,1,0:T(8,128)S(1)}, f32[16,104,128]{2,1,0:T(8,128)S(1)}, u32[]{:S(2)}, u32[]{:S(2)}) collective-permute-start(f32[16,104,128]{2,1,0:T(8,128)S(1)} %get-tuple-element.88), channel_id=1, source_target_pairs={{0,1},{1,0},{2,3},{3,2},{4,5},{5,4},{6,7},{7,6},{8,9},{9,8},{10,11... | collective-permute-start | bytes 2555912 | tf_op jit(solution)/shard_map/ppermute | solution.py:571
  (12 other events, 48.0 us)
where the time goes:
time: 145 us; the launch traced here: 144 us
  Pallas kernels  51.9 us (36%)
  waiting for transfers between devices  38.6 us (27%)
  starting transfers between devices  38.4 us (26%)
  local copies, waits for them, and re-layouts  13.4 us (9%)
    pallas_call x3, Pallas kernels, run_experts(): pl.pallas_call(functools.partial(experts_kernel, z, index), grid=(1,), in...  41.6 us
    ppermute x30, waiting for transfers between devices, exchange(): return lax.ppermute(value, BOTH, [(i, i ^ flip) for i in range(SHARDS)])  38.6 us
    ppermute x30, starting transfers between devices, exchange(): return lax.ppermute(value, BOTH, [(i, i ^ flip) for i in range(SHARDS)])  38.4 us
    unnamed x48, local copies, waits for them, and re-layouts  7.26 us
    pallas_call x1, Pallas kernels, run_outputs(): pl.pallas_call(functools.partial(outputs_kernel, z), grid=(z.rows // bloc...  5.57 us
    pallas_call x1, Pallas kernels, run_unpack(): pl.pallas_call(functools.partial(unpack_kernel, z, group, grad_scale), gr...  4.66 us
    slice x15, local copies, waits for them, and re-layouts, reduce(): v[h:]  4.34 us
  transfers between devices with their start and end apart: 30, of which 13 were waited for; matrix products, arithmetic and copies ran while one was open for 3% of the time, Pallas kernels for 22%

commit v1 on v0

v1 whole, which is shorter than its diff:
```python
import functools
import math

import jax
import jax.numpy as jnp
from jax import lax
from jax.experimental import pallas as pl
from jax.experimental.pallas import tpu as pltpu
from jax.sharding import PartitionSpec as P

f32 = jnp.float32
bf16 = jnp.bfloat16
epsilon = 1e-05
LANES = 128
DEVICES = 32
MIB = 1 << 20
LAG = 2
BOTH = ("wide", "narrow")
SPANS = ((0, 2), (2, 4), (4, 6))
FLIPS = {"c": 1, "x": 2, "y": 4, "1": 8, "2": 16}
AXES = "xy1"
ORDERS = ("xy1", "y1x", "1xy")
HALVED = len(AXES)
BLOCKS = 2 << HALVED


def dot(a, b):
    return lax.dot_general(a, b, (((1,), (0,)), ((), ())), preferred_element_type=f32)


def dot_nt(a, b):
    return lax.dot_general(a, b, (((1,), (1,)), ((), ())), preferred_element_type=f32)


def dot_tn(a, b):
    return lax.dot_general(a, b, (((0,), (0,)), ((), ())), preferred_element_type=f32)


def iota(shape, axis):
    return lax.broadcasted_iota(jnp.int32, shape, axis)


def ones_where(condition):
    return jnp.where(condition, 1.0, 0.0).astype(bf16)


class Sizes:
    def __init__(self, dense, ids, table, w_first, w_second, gate_task):
        self.rows, self.dense = dense.shape
        self.fields = ids.shape[1]
        self.vocab, self.emb = table.shape
        self.experts, self.d_in, self.hidden = w_first.shape
        self.out = w_second.shape[2]
        self.tasks, _, self.gate = gate_task.shape
        self.spec = (self.experts - self.gate) // (self.tasks - 1)
        self.low = LANES // self.emb
        self.high = self.vocab // self.low
        self.columns = gate_columns(self.experts, self.tasks, self.spec)
        self.width = self.tasks * self.gate + self.experts
        self.first_rows = self.d_in // BLOCKS
        self.second_rows = self.hidden // BLOCKS
        self.halves = self.out // LANES
        self.expert_rows = (self.first_rows + self.second_rows) * self.halves
        self.sum_rows = 4 * self.halves
        self.gate_rows = 16 * (self.d_in // LANES)
        self.gate_at = self.high
        self.sums_at = self.gate_at + self.gate_rows
        self.bias_at = self.sums_at + self.experts * self.sum_rows
        self.small_rows = -(-(self.bias_at + 1) // (8 * BLOCKS)) * 8

    def piece_rows(self, index):
        lo, hi = SPANS[index]
        last = index == len(SPANS) - 1
        return (hi - lo) * self.expert_rows + (self.small_rows if last else 0)


def gate_columns(experts, tasks, spec):
    shared = tasks * spec
    gate = spec + experts - shared
    columns = []
    for e in range(experts):
        found = []
        for k in range(tasks):
            if e >= shared:
                found.append((k, k * gate + spec + e - shared))
            elif e // spec == k:
                found.append((k, k * gate + e - k * spec))
        found.append((tasks, tasks * gate + e))
        columns.append(found)
    return columns


def gate_matrix(z, gate_task_ref, gate_shared_ref):
    total = None
    for k in range(z.tasks + 1):
        mat = gate_task_ref[k] if k < z.tasks else gate_shared_ref[...]
        n = mat.shape[0]
        place = ones_where(iota((LANES, n), 0) == iota((LANES, n), 1) + k * z.gate)
        part = dot(place, mat)
        total = part if total is None else total + part
    return total.astype(bf16)


def gate_bias(z, task_ref, shared_ref):
    total = None
    for k in range(z.tasks + 1):
        row = task_ref[k : k + 1, :] if k < z.tasks else shared_ref[...]
        n = row.shape[1]
        place = ones_where(iota((n, LANES), 1) == iota((n, LANES), 0) + k * z.gate)
        part = dot(row, place)
        total = part if total is None else total + part
    return total


def gate_lanes(z, k, shape):
    lane = iota(shape, 1)
    first = k * z.gate
    last = first + (z.gate if k < z.tasks else z.experts)
    return (lane >= first) & (lane < last)


def spread_matrix(z, f):
    a = iota((LANES, LANES), 0)
    b = iota((LANES, LANES), 1)
    return ones_where(b == f * z.emb + lax.rem(a, z.emb))


def table_block(z, table_ref):
    return jnp.concatenate(
        [table_ref[:, low * z.high : (low + 1) * z.high] for low in range(z.low)], axis=0
    )


def split_ids(z, ids_ref, presence_ref):
    ids = ids_ref[...]
    row = jnp.where(presence_ref[...] > 0, lax.bitwise_and(ids, z.high - 1), -1)
    return row, lax.div(ids, z.high)


def turned(v):
    return v.astype(f32).T.astype(jnp.int32)


def lookup_part(z, block, spreads, ids_ref, presence_ref):
    row, low = split_ids(z, ids_ref, presence_ref)
    row, low = turned(row), turned(low)
    lane_high = iota((z.rows, z.high), 1)
    lane_low = lax.div(iota((z.rows, LANES), 1), z.emb)
    total = None
    for f in range(z.fields):
        found = dot_nt(ones_where(row[:, f : f + 1] == lane_high), block)
        kept = jnp.where(low[:, f : f + 1] == lane_low, found, 0.0).astype(bf16)
        part = dot(kept, spreads[f])
        total = part if total is None else total + part
    return total


def softmax_part(z, logits):
    result = None
    for k in range(z.tasks + 1):
        lanes = gate_lanes(z, k, logits.shape)
        top = jnp.max(jnp.where(lanes, logits, -jnp.inf), axis=1, keepdims=True)
        value = jnp.exp(jnp.where(lanes, logits - top, -jnp.inf))
        value = value / jnp.sum(value, axis=1, keepdims=True)
        result = value if result is None else result + value
    return result


def logit_part(z, weights, along):
    product = weights * along
    total = jnp.zeros_like(product)
    for k in range(z.tasks + 1):
        lanes = gate_lanes(z, k, product.shape)
        found = jnp.sum(jnp.where(lanes, product, 0.0), axis=1, keepdims=True)
        total = jnp.where(lanes, found, total)
    return (weights * (along - total)).astype(bf16)


def table_part(z, embed, spreads, ids_ref, presence_ref):
    row, low = split_ids(z, ids_ref, presence_ref)
    low = turned(low)
    line_high = iota((z.high, z.rows), 0)
    lane_low = lax.div(iota((z.rows, LANES), 1), z.emb)
    hots = []
    kept = []
    for f in range(z.fields):
        hots.append(ones_where(row[f : f + 1, :] == line_high))
        wide = dot_nt(embed, spreads[f])
        kept.append(jnp.where(low[:, f : f + 1] == lane_low, wide, 0.0).astype(bf16))
    return dot(jnp.concatenate(hots, axis=1), jnp.concatenate(kept, axis=0))


def device_bits(device):
    own = jnp.int32(0)
    for axis in AXES:
        own = own * 2 + lax.bitwise_and(lax.div(device, FLIPS[axis]), 1)
    return lax.bitwise_and(device, 1), own


def block_of(shard, order, core, own):
    count = BLOCKS // 2
    flips = lax.bitwise_xor(own, shard % count)
    q = jnp.int32(0)
    for axis in order:
        bit = lax.bitwise_and(lax.shift_right_logical(flips, HALVED - 1 - AXES.index(axis)), 1)
        q = q * 2 + bit
    return lax.bitwise_xor(core, shard // count) * count + q


def column_matrix(z, k, ref):
    total = None
    row = iota((LANES, z.out), 0)
    for e in range(z.experts):
        for gate, column in z.columns[e]:
            if gate == k:
                part = jnp.where(row == column, ref[e : e + 1, :].astype(f32), 0.0)
                total = part if total is None else total + part
    return total.astype(bf16)


def main_kernel(z, grad_scale, *refs):
    refs = list(refs)

    def take(count):
        return [refs.pop(0) for _ in range(count)]

    (device_ref,) = take(1)
    far_refs = take(15)
    piece_refs = [take(2) for _ in SPANS]
    normed_ref, first_ref, weights_ref, logit_ref = take(4)
    here = take(15)
    sems, out_sems, features_s, normed_s, first_s, weights_s, logit_s, small_s = take(8)
    packed_s = take(len(SPANS))
    copies = [
        pltpu.make_async_copy(a, b, sems.at[i]) for i, (a, b) in enumerate(zip(far_refs, here))
    ]
    for copy in copies:
        copy.start()
    sent = []

    def send(source, target):
        copy = pltpu.make_async_copy(source, target, out_sems.at[len(sent)])
        copy.start()
        sent.append(copy)

    core, own = device_bits(device_ref[0])
    ids_ref, presence_ref, table_ref, gate_task_ref, gate_task_bias_ref = here[:5]
    gate_shared_ref, gate_shared_bias_ref, dense_ref, w_first_ref, b_first_ref = here[5:10]
    w_second_ref, b_second_ref, gain_ref, bias_ref, cot_ref = here[10:]
    spreads = [spread_matrix(z, f) for f in range(z.fields)]
    for copy in copies[:3]:
        copy.wait()
    looked = lookup_part(z, table_block(z, table_ref), spreads, ids_ref, presence_ref)
    features_s[:, z.dense :] = (0.5 * looked).astype(bf16)
    for copy in copies[3:8]:
        copy.wait()
    features_s[:, : z.dense] = dense_ref[...] * 0.5
    gates = gate_matrix(z, gate_task_ref, gate_shared_ref)
    features = features_s[...]
    logits = 2.0 * dot_nt(features, gates)
    weights = softmax_part(z, logits + gate_bias(z, gate_task_bias_ref, gate_shared_bias_ref))
    weights_s[...] = weights
    send(weights_s, weights_ref)
    for copy in copies[8:]:
        copy.wait()
    lane = iota((z.rows, LANES), 1)
    along = None
    few = weights.astype(bf16)
    bias_sums = []
    for k in range(z.tasks + 1):
        part = dot_nt(cot_ref[k], column_matrix(z, k, bias_ref))
        along = part if along is None else along + part
        bias_sums.append(dot_tn(few, cot_ref[k]))
    embed = jnp.zeros((z.rows, LANES), f32)
    scale = 1.0 / z.out
    for index, span in enumerate(SPANS):
        for e in range(*span):

            def row(ref):
                return ref[e : e + 1, :].astype(f32)

            def mean(v):
                return jnp.sum(v, axis=1, keepdims=True) * scale

            def keep(q, v):
                for h in range(z.halves):
                    line = z.sums_at + e * z.sum_rows + q * z.halves + h
                    small_s[line : line + 1, :] = v[:, h * LANES : (h + 1) * LANES]

            def total(v):
                return jnp.sum(v, axis=0, keepdims=True)

            gain = row(gain_ref)
            half = dot(features_s[...], w_first_ref[e]) + 0.5 * row(b_first_ref)
            turn = jnp.tanh(half)
            up = 1.0 + turn
            smooth = half * up
            hidden = smooth.astype(bf16)
            second = dot(hidden, w_second_ref[e]) + row(b_second_ref)
            center = second - mean(second)
            inverse = lax.rsqrt(mean(center * center) + epsilon)
            normed = center * inverse
            normed_s[e] = normed.astype(bf16)
            send(normed_s.at[e], normed_ref.at[e])
            gained = normed * gain
            upstream = None
            for k, column in z.columns[e]:
                cot = cot_ref[k].astype(f32)
                part = weights_s[:, column : column + 1] * cot
                upstream = part if upstream is None else upstream + part
                found = jnp.sum(cot * gained, axis=1, keepdims=True)
                along = jnp.where(lane == column, along + found, along)
            product = upstream * normed
            scaled = upstream * gain
            second_grad = inverse * (scaled - mean(scaled) - normed * mean(product * gain))
            keep(1, total(second_grad))
            keep(2, total(product))
            second_grad = second_grad.astype(bf16)
            second_total = dot_tn(hidden, second_grad) * grad_scale
            first_grad = dot_nt(second_grad, w_second_ref[e]) * (up + smooth * (1.0 - turn))
            keep(0, 0.5 * total(first_grad))
            first_s[e] = first_grad.astype(bf16)
            send(first_s.at[e], first_ref.at[e])
            first_total = dot_tn(features_s[...], first_s[e]) * grad_scale
            embed = embed + dot_nt(first_s[e], w_first_ref[e, z.dense :, :])
            found = None
            for k, column in z.columns[e]:
                part = bias_sums[k][column : column + 1, :]
                found = part if found is None else found + part
            keep(3, found)
            line = (e - span[0]) * z.expert_rows
            lines = pl.ds(line, z.expert_rows)
            for shard in range(BLOCKS):
                at = block_of(shard, ORDERS[index], core, own)
                begin = line
                for v, count in ((first_total, z.first_rows), (second_total, z.second_rows)):
                    for h in range(z.halves):
                        packed_s[index][at, begin : begin + count, :] = v[
                            shard * count : (shard + 1) * count, h * LANES : (h + 1) * LANES
                        ]
                        begin += count
            for side in range(2):
                blocks = pl.ds(side * (BLOCKS // 2), BLOCKS // 2)
                send(packed_s[index].at[blocks, lines, :], piece_refs[index][side].at[:, lines, :])
    logit_grad = logit_part(z, weights_s[...], along)
    logit_s[...] = logit_grad
    send(logit_s, logit_ref)
    gate_total = 2.0 * dot_tn(logit_grad, features_s[...])
    embed = 0.5 * embed + dot(logit_grad, gates[:, z.dense :])
    table_total = table_part(z, embed.astype(bf16), spreads, ids_ref, presence_ref)
    small_s[: z.high, :] = table_total.T
    for q in range(z.d_in // LANES):
        line = z.gate_at + q * 16
        small_s[line : line + 16, :] = gate_total[:16, q * LANES : (q + 1) * LANES]
    small_s[z.bias_at :, :] = jnp.zeros_like(small_s[z.bias_at :, :])
    small_s[z.bias_at : z.bias_at + 1, :] = jnp.sum(logit_grad.astype(f32), axis=0, keepdims=True)
    lines = pl.ds((SPANS[-1][1] - SPANS[-1][0]) * z.expert_rows, z.small_rows)
    for shard in range(BLOCKS):
        at = block_of(shard, ORDERS[-1], core, own)
        packed_s[-1][at, lines, :] = (
            small_s[shard * z.small_rows : (shard + 1) * z.small_rows, :] * grad_scale
        )
    for side in range(2):
        blocks = pl.ds(side * (BLOCKS // 2), BLOCKS // 2)
        send(packed_s[-1].at[blocks, lines, :], piece_refs[-1][side].at[:, lines, :])
    for copy in sent:
        copy.wait()


def outputs_kernel(z, *refs):
    weights_ref, logit_ref, w_first_ref, gain_ref, bias_ref, gate_task_ref, gate_shared_ref = refs[
        :7
    ]
    normed_ref, first_ref, mixed_ref, dense_ref = refs[7:]
    weights = weights_ref[...]
    mixed = [None] * (z.tasks + 1)
    gates = gate_matrix(z, gate_task_ref, gate_shared_ref)
    dense = None
    for e in range(z.experts):
        expert_out = normed_ref[e].astype(f32) * gain_ref[e : e + 1, :].astype(f32) + bias_ref[
            e : e + 1, :
        ].astype(f32)
        for k, column in z.columns[e]:
            part = weights[:, column : column + 1] * expert_out
            mixed[k] = part if mixed[k] is None else mixed[k] + part
        part = dot_nt(first_ref[e], w_first_ref[e, : z.dense, :])
        dense = part if dense is None else dense + part
    for k in range(z.tasks + 1):
        mixed_ref[k] = mixed[k].astype(bf16)
    dense_ref[...] = 0.5 * dense + dot(logit_ref[...], gates[:, : z.dense])


def unpack_kernel(z, index, *refs):
    last = index == len(SPANS) - 1
    refs = list(refs)

    def take(count):
        return [refs.pop(0) for _ in range(count)]

    device_ref, near_ref, far_ref = take(3)
    if index:
        take(2)
    w_first_ref, w_second_ref = take(2)
    core, own = device_bits(device_ref[0])
    base = pl.program_id(0) * z.expert_rows
    count = BLOCKS // 2

    def unpack(shard, side, from_ref):
        at = lax.bitwise_and(block_of(shard, ORDERS[index], core, own), count - 1)
        line = 0
        for ref, rows in ((w_first_ref, z.first_rows), (w_second_ref, z.second_rows)):
            for h in range(z.halves):
                lines = pl.ds(pl.multiple_of(base + line, 8), rows)
                ref[0, shard * rows : (shard + 1) * rows, h * LANES : (h + 1) * LANES] = from_ref[
                    at, lines, :
                ]
                line += rows

    for side, from_ref in enumerate((near_ref, far_ref)):
        for owner in range(2):

            @pl.when(lax.bitwise_xor(core, owner) == side)
            def _():
                for shard in range(owner * count, (owner + 1) * count):
                    unpack(shard, side, from_ref)

    if not last:
        return
    table_ref, gate_task_ref, gate_task_bias_ref, gate_shared_ref, gate_shared_bias_ref = take(5)
    sum_refs = take(4)
    (small_s,) = take(1)

    @pl.when(pl.program_id(0) == 0)
    def _():
        start = (SPANS[index][1] - SPANS[index][0]) * z.expert_rows
        for side, from_ref in enumerate((near_ref, far_ref)):
            for owner in range(2):

                @pl.when(lax.bitwise_xor(core, owner) == side)
                def _():
                    for shard in range(owner * count, (owner + 1) * count):
                        at = block_of(shard, ORDERS[index], core, own)
                        small_s[shard * z.small_rows : (shard + 1) * z.small_rows, :] = from_ref[
                            lax.bitwise_and(at, count - 1), start:, :
                        ]

        for low in range(z.low):
            table_ref[:, low * z.high : (low + 1) * z.high] = small_s[
                low * z.emb : (low + 1) * z.emb, :
            ]
        for q in range(z.d_in // LANES):
            line = z.gate_at + q * 16
            lanes = slice(q * LANES, (q + 1) * LANES)
            for k in range(z.tasks):
                gate_task_ref[k, :, lanes] = small_s[
                    line + k * z.gate : line + (k + 1) * z.gate, :
                ]
            gate_shared_ref[:, lanes] = small_s[line + z.tasks * z.gate : line + z.width, :]
        bias_row = small_s[z.bias_at : z.bias_at + 1, :]
        for k in range(z.tasks):
            gate_task_bias_ref[k : k + 1, :] = bias_row[:, k * z.gate : (k + 1) * z.gate]
        gate_shared_bias_ref[...] = bias_row[:, z.tasks * z.gate : z.width]
        for e in range(z.experts):
            for q in range(4):
                for h in range(z.halves):
                    line = z.sums_at + e * z.sum_rows + q * z.halves + h
                    sum_refs[q][e : e + 1, h * LANES : (h + 1) * LANES] = small_s[
                        line : line + 1, :
                    ]


SMEM = pl.BlockSpec(memory_space=pltpu.SMEM)
ANY = pl.BlockSpec(memory_space=pl.ANY)
HBM = pl.BlockSpec(memory_space=pltpu.HBM)


def shape_of(shape, dtype=f32):
    return jax.ShapeDtypeStruct(shape, dtype)


def whole(array):
    return pl.BlockSpec(array.shape, lambda at: (0,) * len(array.shape))


def rows_spec(z, block, shape):
    if shape == (z.fields, z.rows):
        return pl.BlockSpec((z.fields, block), lambda at: (0, at))
    if len(shape) == 2:
        return pl.BlockSpec((block, shape[1]), lambda at: (at, 0))
    return pl.BlockSpec((shape[0], block, shape[2]), lambda at: (0, at, 0))


def run_main(z, grad_scale, device, operands):
    rows = z.rows
    out_shape = []
    for index in range(len(SPANS)):
        out_shape += [shape_of((BLOCKS // 2, z.piece_rows(index), LANES))] * 2
    rows_shape = [
        shape_of((z.experts, rows, z.out), bf16),
        shape_of((z.experts, rows, z.hidden), bf16),
        shape_of((rows, LANES)),
        shape_of((rows, LANES), bf16),
    ]
    out_shape += rows_shape
    scratch = [pltpu.VMEM(v.shape, v.dtype) for v in operands]
    scratch += [pltpu.SemaphoreType.DMA((len(operands),))]
    scratch += [pltpu.SemaphoreType.DMA((4 * z.experts + 4,))]
    scratch += [pltpu.VMEM((rows, z.d_in), bf16)]
    scratch += [pltpu.VMEM(v.shape, v.dtype) for v in rows_shape]
    scratch += [pltpu.VMEM((z.small_rows * BLOCKS, LANES), f32)]
    scratch += [
        pltpu.VMEM((BLOCKS, z.piece_rows(index), LANES), f32) for index in range(len(SPANS))
    ]
    macs = rows * z.experts * 3 * (z.d_in * z.hidden + z.hidden * z.out)
    return pl.pallas_call(
        functools.partial(main_kernel, z, grad_scale),
        in_specs=[SMEM] + [ANY] * len(operands),
        out_specs=[ANY] * len(out_shape),
        out_shape=out_shape,
        scratch_shapes=scratch,
        compiler_params=pltpu.CompilerParams(vmem_limit_bytes=54 * MIB),
        cost_estimate=pl.CostEstimate(
            flops=2 * macs,
            bytes_accessed=20 * MIB,
            transcendentals=rows * z.experts * z.hidden,
        ),
        name="experts",
    )(device, *operands)


def run_outputs(z, weights, logit_grad, w_first, gain, bias, gates, normed, firsts):
    block = z.rows // 4
    out_shape = [shape_of((z.tasks + 1, z.rows, z.out), bf16), shape_of((z.rows, z.dense))]
    return pl.pallas_call(
        functools.partial(outputs_kernel, z),
        grid=(z.rows // block,),
        in_specs=[rows_spec(z, block, v.shape) for v in (weights, logit_grad)]
        + [whole(v) for v in (w_first, gain, bias) + gates]
        + [rows_spec(z, block, v.shape) for v in (normed, firsts)],
        out_specs=[rows_spec(z, block, v.shape) for v in out_shape],
        out_shape=out_shape,
        compiler_params=pltpu.CompilerParams(vmem_limit_bytes=24 * MIB),
        cost_estimate=pl.CostEstimate(
            flops=2 * z.rows * z.experts * z.hidden * z.dense,
            bytes_accessed=11 * MIB,
            transcendentals=0,
        ),
        name="outputs",
    )(weights, logit_grad, w_first, gain, bias, *gates, normed, firsts)


def run_unpack(z, index, device, near, far, earlier):
    last = index == len(SPANS) - 1
    lo, hi = SPANS[index]
    out_shape = [
        shape_of((z.experts, z.d_in, z.hidden)),
        shape_of((z.experts, z.hidden, z.out)),
    ]
    out_specs = [pl.BlockSpec((1,) + v.shape[1:], lambda at: (lo + at, 0, 0)) for v in out_shape]
    scratch = []
    if last:
        small = [
            shape_of((z.emb, z.vocab)),
            shape_of((z.tasks, z.gate, z.d_in)),
            shape_of((z.tasks, z.gate)),
            shape_of((z.experts, z.d_in)),
            shape_of((1, z.experts)),
        ] + [shape_of((z.experts, z.out))] * 4
        out_shape += small
        out_specs += [whole(v) for v in small]
        scratch = [pltpu.VMEM((z.small_rows * BLOCKS, LANES), f32)]
    operands = [device, near, far] + list(earlier)
    return pl.pallas_call(
        functools.partial(unpack_kernel, z, index),
        grid=(hi - lo,),
        in_specs=[SMEM, whole(near), whole(far)] + [ANY] * len(earlier),
        out_specs=out_specs,
        out_shape=out_shape,
        scratch_shapes=scratch,
        input_output_aliases={3: 0, 4: 1} if earlier else {},
        compiler_params=pltpu.CompilerParams(vmem_limit_bytes=24 * MIB),
        cost_estimate=pl.CostEstimate(flops=0, bytes_accessed=4 * MIB, transcendentals=0),
        name="unpack_%d" % index,
    )(*operands)


def exchange(value, axis):
    flip = FLIPS[axis]
    count = lax.axis_size("wide") * lax.axis_size("narrow")
    return lax.ppermute(value, BOTH, [(i, i ^ flip) for i in range(count)])


def after(value, other):
    return lax.optimization_barrier((value, other))[0]


def sum_pieces(near, far, outputs):
    count = len(near)
    got = [exchange(v, "c") for v in far]
    sent = None
    for step in range(HALVED):
        for i in range(count):
            found = got[i] if sent is None else after(got[i], sent)
            half = near[i].shape[0] // 2
            low, high = near[i][:half] + found[:half], near[i][half:] + found[half:]
            near[i] = low
            got[i] = exchange(high, ORDERS[i][step])
            sent = high
    for i in range(count):
        near[i] = near[i] + after(got[i], sent)
    rows = [v.shape[1] for v in near]
    joined = jnp.concatenate(near, axis=1)
    results = outputs(joined)
    joined = joined + after(exchange(joined, "2"), results[0])
    near = []
    for i in range(count):
        near.append(joined[:, sum(rows[:i]) : sum(rows[: i + 1])])
    for step in reversed(range(HALVED)):
        for i in range(count):
            if step < HALVED - 1:
                near[i] = jnp.concatenate([near[i], after(got[i], sent)], axis=0)
            got[i] = exchange(near[i], ORDERS[i][step])
            sent = near[i]
    far = []
    for i in range(count):
        near[i] = jnp.concatenate([near[i], after(got[i], sent)], axis=0)
        sent = near[i]
        far.append(exchange(near[i], "c"))
    return near, far, results


def local(
    fits,
    dense_feats,
    sparse_ids,
    presence,
    embed_table,
    w_first,
    b_first,
    w_second,
    b_second,
    ln_gain,
    ln_bias,
    gate_task,
    gate_task_bias,
    gate_shared,
    gate_shared_bias,
    cotangent,
):
    z = Sizes(dense_feats, sparse_ids, embed_table, w_first, w_second, gate_task)
    total_rows = z.rows * lax.axis_size("wide") * lax.axis_size("narrow")
    grad_scale = 1.0 / math.sqrt(total_rows)
    if fits:
        device = lax.axis_index("wide") * lax.axis_size("narrow") + lax.axis_index("narrow")
    else:
        device = 0
    device = jnp.full((1,), device, jnp.int32)
    ids, present = sparse_ids.T, presence.T
    gates = (gate_task.transpose(0, 2, 1), gate_shared.T)
    found = run_main(
        z,
        grad_scale,
        device,
        [
            ids,
            present,
            embed_table.T,
            gates[0],
            gate_task_bias,
            gates[1],
            gate_shared_bias.reshape(1, -1),
            dense_feats,
            w_first,
            b_first,
            w_second,
            b_second,
            ln_gain,
            ln_bias,
            cotangent,
        ],
    )
    near, far = list(found[: 2 * len(SPANS) : 2]), list(found[1 : 2 * len(SPANS) : 2])
    normed, firsts, weights, logit_grad = found[2 * len(SPANS) :]

    def outputs(begin):
        first = weights if begin is None else after(weights, begin)
        return run_outputs(
            z, first, logit_grad, w_first, ln_gain, ln_bias, gates, normed, firsts
        )

    if fits:
        near, far, results = sum_pieces(near, far, outputs)
    else:
        results = outputs(None)
        near, far = lax.psum((near, far), BOTH)
    mixed, dense_grad = results
    grads = ()
    for index in range(len(SPANS)):
        grads = run_unpack(z, index, device, near[index], far[index], grads[:2])
    w_first_grad, w_second_grad, table_grad = grads[:3]
    gate_task_grad, gate_task_bias_grad, gate_shared_grad, gate_shared_bias_grad = grads[3:7]
    b_first_grad, b_second_grad, gain_grad, bias_grad = grads[7:]
    return (
        mixed,
        dense_grad,
        table_grad.T,
        w_first_grad,
        b_first_grad,
        w_second_grad,
        b_second_grad,
        gain_grad,
        bias_grad,
        gate_task_grad.transpose(0, 2, 1),
        gate_task_bias_grad,
        gate_shared_grad.T,
        gate_shared_bias_grad.reshape(-1),
    )


def solution(mesh):
    fits = (mesh.shape["wide"], mesh.shape["narrow"]) == (8, 4)
    rows = P(BOTH, None)
    middle = P(None, BOTH, None)
    return jax.shard_map(
        functools.partial(local, fits),
        mesh=mesh,
        in_specs=(rows, rows, rows) + (P(),) * 11 + (middle,),
        out_specs=(middle, rows) + (P(),) * 11,
        check_vma=False,
    )
```

time: 145 us -> 104 us (0.72)
  Pallas kernels: 51.9 us -> 36.1 us
  local copies, waits for them, and re-layouts: 13.4 us -> 0.08 us
  starting transfers between devices: 38.4 us -> 28.1 us
  waiting for transfers between devices: 38.6 us -> 36.2 us
    pallas_call x4, Pallas kernels: 46.3 us -> 30.9 us  [the longest x1 27 us: run_main(): pl.pallas_call(functools.partial(main_kernel, z, grad_scale), in_specs=[S...]
    ppermute x30 -> x25, starting transfers between devices: 38.4 us -> 28.1 us  [exchange(): return lax.ppermute(value, BOTH, [(i, i ^ flip) for i in range(count)])]
    unnamed x48 -> x22, local copies, waits for them, and re-layouts: 7.26 us -> 0.05 us
    slice x18 -> x2, local copies, waits for them, and re-layouts: 4.55 us -> 0.02 us  [sum_pieces(): near.append(joined[:, sum(rows[:i]):sum(rows[:i + 1])])]
    ppermute x30 -> x25, waiting for transfers between devices: 38.6 us -> 36.2 us  [exchange(): return lax.ppermute(value, BOTH, [(i, i ^ flip) for i in range(count)])]
  transfers between devices with their start and end apart: 30 -> 25, of which waited for: 13 -> 16; matrix products, arithmetic and copies ran while one was open for 3% -> 2% of each run, Pallas kernels for 22% -> 7%
where the time goes in v1:
time: 104 us
  waiting for transfers between devices  36.2 us (35%)
  Pallas kernels  36.1 us (35%)
  starting transfers between devices  28.1 us (27%)
  other arithmetic  2.19 us (2%)
  between operations  1.09 us (1%)
    ppermute x25, waiting for transfers between devices, exchange(): return lax.ppermute(value, BOTH, [(i, i ^ flip) for i in range(count)])  36.2 us
    ppermute x25, starting transfers between devices, exchange(): return lax.ppermute(value, BOTH, [(i, i ^ flip) for i in range(count)])  28.1 us
    pallas_call x1, Pallas kernels, run_main(): pl.pallas_call(functools.partial(main_kernel, z, grad_scale), in_specs=[S...  27 us
    pallas_call x1, Pallas kernels, run_outputs(): pl.pallas_call(functools.partial(outputs_kernel, z), grid=(z.rows // bloc...  5.21 us
    pallas_call x3, Pallas kernels, run_unpack(): pl.pallas_call(functools.partial(unpack_kernel, z, index), grid=(hi - lo,...  3.92 us
  transfers between devices with their start and end apart: 25, of which 16 were waited for; matrix products, arithmetic and copies ran while one was open for 2% of the time, Pallas kernels for 7%

profile of v1, /device:TPU:0, one launch (start us, length us, event | category | flops | bytes accessed | tf_op | source)
XLA Modules:
  0.0 103.8 jit_solution(16642407584707516356)
XLA Ops:
  0.7 27.0 %experts.1 = (f32[8,192,128]{2,1,0:T(8,128)}, f32[8,192,128]{2,1,0:T(8,128)}, f32[8,192,128]{2,1,0:T(8,128)}, f32[8,192,128]{2,1,0:T(8,128)}, f32[8,208,128]{2,1...) custom-call(s32[1]{0:T(128)} %bitcast.refs_0_, ...), custom_call_target="tpu_custom_call" | custom-call | flops 7247757312 | bytes 20971520 | tf_op jit(solution)/shard_map/experts/pallas_call | solution.py:515
  28.7 1.6 %collective-permute-done = f32[8,192,128]{2,1,0:T(8,128)S(1)} collective-permute-done((f32[8,192,128]{2,1,0:T(8,128)}, f32[8,192,128]{2,1,0:T(8,128)S(1)}, u32[]{:S(2)}, u32[]{:S(2)}) %collective-permute-start) | collective-permute-done | bytes 786464 | tf_op jit(solution)/shard_map/ppermute | solution.py:590
  30.3 1.2 %slice_add_fusion.3 = (f32[4,192,128]{2,1,0:T(8,128)S(1)}, f32[4,192,128]{2,1,0:T(8,128)S(1)}) fusion(f32[8,192,128]{2,1,0:T(8,128)S(1)} %collective-permute-done, f32[8,192,128]{2,1,0:T(8,128)} %get-tuple-element.63), kind=kLoop, calls=%fused_computation.7 | loop fusion | flops 196608 | bytes 2359296 | tf_op jit(solution)/shard_map/add | solution.py:605
  31.5 2.9 %collective-permute-start.1 = (f32[4,192,128]{2,1,0:T(8,128)S(1)}, f32[4,192,128]{2,1,0:T(8,128)S(1)}, u32[]{:S(2)}, u32[]{:S(2)}) collective-permute-start(f32[4,192,128]{2,1,0:T(8,128)S(1)} %get-tuple-element.114), channel_id=1, source_target_pairs={{0,2},{1,3},{2,0},{3,1},{4,6},{5,7},{6,4},{7,5},{8,10},{9,11},{10,... | collective-permute-start | bytes 1179656 | tf_op jit(solution)/shard_map/ppermute | solution.py:590
  34.8 1.6 %collective-permute-start.6 = (f32[4,192,128]{2,1,0:T(8,128)S(1)}, f32[4,192,128]{2,1,0:T(8,128)S(1)}, u32[]{:S(2)}, u32[]{:S(2)}) collective-permute-start(f32[4,192,128]{2,1,0:T(8,128)S(1)} %get-tuple-element.116), channel_id=1, source_target_pairs={{0,4},{1,5},{2,6},{3,7},{4,0},{5,1},{6,2},{7,3},{8,12},{9,13},{10,... | collective-permute-start | bytes 1179656 | tf_op jit(solution)/shard_map/ppermute | solution.py:590
  36.5 1.6 %collective-permute-start.5 = (f32[4,208,128]{2,1,0:T(8,128)S(1)}, f32[4,208,128]{2,1,0:T(8,128)S(1)}, u32[]{:S(2)}, u32[]{:S(2)}) collective-permute-start(f32[4,208,128]{2,1,0:T(8,128)S(1)} %get-tuple-element.111), channel_id=1, source_target_pairs={{0,8},{1,9},{2,10},{3,11},{4,12},{5,13},{6,14},{7,15},{8,0},{9,1},... | collective-permute-start | bytes 1277960 | tf_op jit(solution)/shard_map/ppermute | solution.py:590
  38.1 5.8 %collective-permute-done.1 = f32[4,192,128]{2,1,0:T(8,128)S(1)} collective-permute-done((f32[4,192,128]{2,1,0:T(8,128)S(1)}, f32[4,192,128]{2,1,0:T(8,128)S(1)}, u32[]{:S(2)}, u32[]{:S(2)}) %collective-permute-start.1) | collective-permute-done | bytes 393248 | tf_op jit(solution)/shard_map/ppermute | solution.py:590
  43.9 1.8 %collective-permute-start.4 = (f32[2,192,128]{2,1,0:T(8,128)S(1)}, f32[2,192,128]{2,1,0:T(8,128)S(1)}, u32[]{:S(2)}, u32[]{:S(2)}) collective-permute-start(f32[2,192,128]{2,1,0:T(8,128)S(1)} %get-tuple-element.120), channel_id=1, source_target_pairs={{0,4},{1,5},{2,6},{3,7},{4,0},{5,1},{6,2},{7,3},{8,12},{9,13},{10,... | collective-permute-start | bytes 589832 | tf_op jit(solution)/shard_map/ppermute | solution.py:590
  45.8 1.6 %collective-permute-start.9 = (f32[2,192,128]{2,1,0:T(8,128)S(1)}, f32[2,192,128]{2,1,0:T(8,128)S(1)}, u32[]{:S(2)}, u32[]{:S(2)}) collective-permute-start(f32[2,192,128]{2,1,0:T(8,128)S(1)} %get-tuple-element.122), channel_id=1, source_target_pairs={{0,8},{1,9},{2,10},{3,11},{4,12},{5,13},{6,14},{7,15},{8,0},{9,1},... | collective-permute-start | bytes 589832 | tf_op jit(solution)/shard_map/ppermute | solution.py:590
  49.1 1.3 %collective-permute-done.4 = f32[2,192,128]{2,1,0:T(8,128)S(1)} collective-permute-done((f32[2,192,128]{2,1,0:T(8,128)S(1)}, f32[2,192,128]{2,1,0:T(8,128)S(1)}, u32[]{:S(2)}, u32[]{:S(2)}) %collective-permute-start.4) | collective-permute-done | bytes 196640 | tf_op jit(solution)/shard_map/ppermute | solution.py:590
  50.4 1.6 %collective-permute-start.7 = (f32[1,192,128]{2,1,0:T(8,128)S(1)}, f32[1,192,128]{2,1,0:T(8,128)S(1)}, u32[]{:S(2)}, u32[]{:S(2)}) collective-permute-start(f32[1,192,128]{2,1,0:T(8,128)S(1)} %slice_add_fusion.16), channel_id=1, source_target_pairs={{0,8},{1,9},{2,10},{3,11},{4,12},{5,13},{6,14},{7,15},{8,0},{9,1},... | collective-permute-start | bytes 294920 | tf_op jit(solution)/shard_map/ppermute | solution.py:590
  52.2 1.3 %collective-permute-start.10 = (f32[1,192,128]{2,1,0:T(8,128)S(1)}, f32[1,192,128]{2,1,0:T(8,128)S(1)}, u32[]{:S(2)}, u32[]{:S(2)}) collective-permute-start(f32[1,192,128]{2,1,0:T(8,128)S(1)} %slice_add_fusion.15), channel_id=1, source_target_pairs={{0,2},{1,3},{2,0},{3,1},{4,6},{5,7},{6,4},{7,5},{8,10},{9,11},{10,... | collective-permute-start | bytes 294920 | tf_op jit(solution)/shard_map/ppermute | solution.py:590
  53.6 1.5 %collective-permute-done.8 = f32[2,208,128]{2,1,0:T(8,128)S(1)} collective-permute-done((f32[2,208,128]{2,1,0:T(8,128)S(1)}, f32[2,208,128]{2,1,0:T(8,128)S(1)}, u32[]{:S(2)}, u32[]{:S(2)}) %collective-permute-start.8) | collective-permute-done | bytes 213024 | tf_op jit(solution)/shard_map/ppermute | solution.py:590
  55.6 1.3 %collective-permute-done.10 = f32[1,192,128]{2,1,0:T(8,128)S(1)} collective-permute-done((f32[1,192,128]{2,1,0:T(8,128)S(1)}, f32[1,192,128]{2,1,0:T(8,128)S(1)}, u32[]{:S(2)}, u32[]{:S(2)}) %collective-permute-start.10) | collective-permute-done | bytes 98336 | tf_op jit(solution)/shard_map/ppermute | solution.py:590
  56.9 2.9 %collective-permute-done.11 = f32[1,208,128]{2,1,0:T(8,128)S(1)} collective-permute-done((f32[1,208,128]{2,1,0:T(8,128)S(1)}, f32[1,208,128]{2,1,0:T(8,128)S(1)}, u32[]{:S(2)}, u32[]{:S(2)}) %collective-permute-start.11) | collective-permute-done | bytes 106528 | tf_op jit(solution)/shard_map/ppermute | solution.py:590
  59.9 2.7 %collective-permute-start.12 = (f32[1,592,128]{2,1,0:T(8,128)S(1)}, f32[1,592,128]{2,1,0:T(8,128)S(1)}, u32[]{:S(2)}, u32[]{:S(2)}) collective-permute-start(f32[1,592,128]{2,1,0:T(8,128)S(1)} %pad_maximum_fusion.6), channel_id=1, source_target_pairs={{0,16},{1,17},{2,18},{3,19},{4,20},{5,21},{6,22},{7,23},{8,24},{9,... | collective-permute-start | bytes 909320 | tf_op jit(solution)/shard_map/ppermute | solution.py:590
  62.6 5.2 %outputs.1 = (bf16[3,1024,256]{2,1,0:T(8,128)(2,1)}, f32[1024,384]{1,0:T(8,128)}) custom-call(f32[1024,128]{1,0:T(8,128)S(1)} %copy-done.3, bf16[1024,128]{1,0:T(8,128)(2,1)S(1)} %copy-done.4, bf16[6,512,256]{2,1,0:T(8,128)(2,1)S(1)} %copy-done.2, bf16[6,256]{1,0:T(8,128)(2,1)S(1)} %copy-done.7, bf16[6,256]{1,0:T(8,128)(2,1)S(1)} %copy-done.8, ...), custom_call_target="tpu_custom_call" | custom-call | flops 1207959552 | bytes 11534336 | tf_op jit(solution)/shard_map/outputs/pallas_call | solution.py:534
  67.8 4.1 %collective-permute-done.12 = f32[1,592,128]{2,1,0:T(8,128)S(1)} collective-permute-done((f32[1,592,128]{2,1,0:T(8,128)S(1)}, f32[1,592,128]{2,1,0:T(8,128)S(1)}, u32[]{:S(2)}, u32[]{:S(2)}) %collective-permute-start.12) | collective-permute-done | bytes 303136 | tf_op jit(solution)/shard_map/ppermute | solution.py:590
  72.7 1.1 %collective-permute-start.14 = (f32[1,192,128]{2,1,0:T(8,128)S(1)}, f32[1,192,128]{2,1,0:T(8,128)S(1)}, u32[]{:S(2)}, u32[]{:S(2)}) collective-permute-start(f32[1,192,128]{2,1,0:T(8,128)S(1)} %get-tuple-element.124), channel_id=1, source_target_pairs={{0,2},{1,3},{2,0},{3,1},{4,6},{5,7},{6,4},{7,5},{8,10},{9,11},{10,... | collective-permute-start | bytes 294920 | tf_op jit(solution)/shard_map/ppermute | solution.py:590
  74.8 1.9 %collective-permute-done.15 = f32[1,192,128]{2,1,0:T(8,128)S(1)} collective-permute-done((f32[1,192,128]{2,1,0:T(8,128)S(1)}, f32[1,192,128]{2,1,0:T(8,128)S(1)}, u32[]{:S(2)}, u32[]{:S(2)}) %collective-permute-start.15) | collective-permute-done | bytes 98336 | tf_op jit(solution)/shard_map/ppermute | solution.py:590
  76.6 1.4 %collective-permute-start.18 = (f32[2,192,128]{2,1,0:T(8,128)S(1)}, f32[2,192,128]{2,1,0:T(8,128)S(1)}, u32[]{:S(2)}, u32[]{:S(2)}) collective-permute-start(f32[2,192,128]{2,1,0:T(8,128)S(1)} %pad_maximum_fusion.8), channel_id=1, source_target_pairs={{0,4},{1,5},{2,6},{3,7},{4,0},{5,1},{6,2},{7,3},{8,12},{9,13},{10,... | collective-permute-start | bytes 589832 | tf_op jit(solution)/shard_map/ppermute | solution.py:590
  80.7 1.7 %collective-permute-done.18 = f32[2,192,128]{2,1,0:T(8,128)S(1)} collective-permute-done((f32[2,192,128]{2,1,0:T(8,128)S(1)}, f32[2,192,128]{2,1,0:T(8,128)S(1)}, u32[]{:S(2)}, u32[]{:S(2)}) %collective-permute-start.18) | collective-permute-done | bytes 196640 | tf_op jit(solution)/shard_map/ppermute | solution.py:590
  82.4 1.4 %collective-permute-start.21 = (f32[4,192,128]{2,1,0:T(8,128)S(1)}, f32[4,192,128]{2,1,0:T(8,128)S(1)}, u32[]{:S(2)}, u32[]{:S(2)}) collective-permute-start(f32[4,192,128]{2,1,0:T(8,128)S(1)} %pad_maximum_fusion.4), channel_id=1, source_target_pairs={{0,2},{1,3},{2,0},{3,1},{4,6},{5,7},{6,4},{7,5},{8,10},{9,11},{10,... | collective-permute-start | bytes 1179656 | tf_op jit(solution)/shard_map/ppermute | solution.py:590
  83.9 1.1 %collective-permute-start.20 = (f32[4,192,128]{2,1,0:T(8,128)S(1)}, f32[4,192,128]{2,1,0:T(8,128)S(1)}, u32[]{:S(2)}, u32[]{:S(2)}) collective-permute-start(f32[4,192,128]{2,1,0:T(8,128)S(1)} %pad_maximum_fusion.5), channel_id=1, source_target_pairs={{0,4},{1,5},{2,6},{3,7},{4,0},{5,1},{6,2},{7,3},{8,12},{9,13},{10,... | collective-permute-start | bytes 1179656 | tf_op jit(solution)/shard_map/ppermute | solution.py:590
  84.9 2.9 %collective-permute-done.16 = f32[2,208,128]{2,1,0:T(8,128)S(1)} collective-permute-done((f32[2,208,128]{2,1,0:T(8,128)S(1)}, f32[2,208,128]{2,1,0:T(8,128)S(1)}, u32[]{:S(2)}, u32[]{:S(2)}) %collective-permute-start.16) | collective-permute-done | bytes 213024 | tf_op jit(solution)/shard_map/ppermute | solution.py:590
  87.9 1.4 %collective-permute-start.19 = (f32[4,208,128]{2,1,0:T(8,128)S(1)}, f32[4,208,128]{2,1,0:T(8,128)S(1)}, u32[]{:S(2)}, u32[]{:S(2)}) collective-permute-start(f32[4,208,128]{2,1,0:T(8,128)S(1)} %pad_maximum_fusion.3), channel_id=1, source_target_pairs={{0,8},{1,9},{2,10},{3,11},{4,12},{5,13},{6,14},{7,15},{8,0},{9,1},... | collective-permute-start | bytes 1277960 | tf_op jit(solution)/shard_map/ppermute | solution.py:590
  89.3 3.9 %collective-permute-done.21 = f32[4,192,128]{2,1,0:T(8,128)S(1)} collective-permute-done((f32[4,192,128]{2,1,0:T(8,128)S(1)}, f32[4,192,128]{2,1,0:T(8,128)S(1)}, u32[]{:S(2)}, u32[]{:S(2)}) %collective-permute-start.21) | collective-permute-done | bytes 393248 | tf_op jit(solution)/shard_map/ppermute | solution.py:590
  93.3 2.8 %collective-permute-done.19 = f32[4,208,128]{2,1,0:T(8,128)S(1)} collective-permute-done((f32[4,208,128]{2,1,0:T(8,128)S(1)}, f32[4,208,128]{2,1,0:T(8,128)S(1)}, u32[]{:S(2)}, u32[]{:S(2)}) %collective-permute-start.19) | collective-permute-done | bytes 426016 | tf_op jit(solution)/shard_map/ppermute | solution.py:590
  96.8 2.9 %collective-permute-done.24.refs_2_ = f32[8,192,128]{2,1,0:T(8,128)S(1)} collective-permute-done((f32[8,192,128]{2,1,0:T(8,128)S(1)}, f32[8,192,128]{2,1,0:T(8,128)S(1)}, u32[]{:S(2)}, u32[]{:S(2)}) %collective-permute-start.24) | collective-permute-done | bytes 786464 | tf_op jit(solution)/shard_map/ppermute | solution.py:590
  99.7 1.2 %unpack_0.1 = (f32[6,512,256]{2,1,0:T(8,128)}, f32[6,256,256]{2,1,0:T(8,128)}) custom-call(s32[1]{0:T(128)} %bitcast.refs_0_, f32[8,192,128]{2,1,0:T(8,128)S(1)} %pad_maximum_fusion.1.refs_1_, f32[8,192,128]{2,1,0:T(8,128)S(1)} %collective-permute-done.24.refs_2_), custom_call_target="tpu_custom_call" | custom-call | bytes 4194304 | tf_op jit(solution)/shard_map/unpack_0/pallas_call | solution.py:573
  101.0 1.2 %unpack_1.1 = (f32[6,512,256]{2,1,0:T(8,128)}, f32[6,256,256]{2,1,0:T(8,128)}) custom-call(s32[1]{0:T(128)} %bitcast.refs_0_, f32[8,192,128]{2,1,0:T(8,128)S(1)} %pad_maximum_fusion.2.refs_1_, f32[8,192,128]{2,1,0:T(8,128)S(1)} %collective-permute-done.23.refs_2_, ...), custom_call_target="tpu_custom_call", output_to_operand_aliasing={{0}: (3, {}), {1}: (4, {})} | custom-call | bytes 4194304 | tf_op jit(solution)/shard_map/unpack_1/pallas_call | solution.py:573
  102.2 1.5 %unpack_2.1 = (f32[6,512,256]{2,1,0:T(8,128)}, f32[6,256,256]{2,1,0:T(8,128)}, f32[16,1024]{1,0:T(8,128)}, f32[2,4,512]{2,1,0:T(4,128)}, f32[2,4]{1,0:T(2,128)},...) custom-call(s32[1]{0:T(128)} %bitcast.refs_0_, ...), custom_call_target="tpu_custom_call", output_to_operand_aliasing={{0}: (3, {}), {1}: (4, {})} | custom-call | bytes 4194304 | tf_op jit(solution)/shard_map/unpack_2/pallas_call | solution.py:573
  (69 shorter events, 9.3 us)
Async XLA Ops:
  27.7 2.6 %collective-permute-start = (f32[8,192,128]{2,1,0:T(8,128)}, f32[8,192,128]{2,1,0:T(8,128)S(1)}, u32[]{:S(2)}, u32[]{:S(2)}) collective-permute-start(f32[8,192,128]{2,1,0:T(8,128)} %get-tuple-element.64), channel_id=1, source_target_pairs={{0,1},{1,0},{2,3},{3,2},{4,5},{5,4},{6,7},{7,6},{8,9},{9,8},{10,11... | collective-permute-start | bytes 2359304 | tf_op jit(solution)/shard_map/ppermute | solution.py:590
  28.2 6.3 %collective-permute-start.3 = (f32[8,192,128]{2,1,0:T(8,128)}, f32[8,192,128]{2,1,0:T(8,128)S(1)}, u32[]{:S(2)}, u32[]{:S(2)}) collective-permute-start(f32[8,192,128]{2,1,0:T(8,128)} %get-tuple-element.68), channel_id=1, source_target_pairs={{0,1},{1,0},{2,3},{3,2},{4,5},{5,4},{6,7},{7,6},{8,9},{9,8},{10,11... | collective-permute-start | bytes 2359304 | tf_op jit(solution)/shard_map/ppermute | solution.py:590
  28.3 8.1 %collective-permute-start.2 = (f32[8,208,128]{2,1,0:T(8,128)}, f32[8,208,128]{2,1,0:T(8,128)S(1)}, u32[]{:S(2)}, u32[]{:S(2)}) collective-permute-start(f32[8,208,128]{2,1,0:T(8,128)} %get-tuple-element.66), channel_id=1, source_target_pairs={{0,1},{1,0},{2,3},{3,2},{4,5},{5,4},{6,7},{7,6},{8,9},{9,8},{10,11... | collective-permute-start | bytes 2555912 | tf_op jit(solution)/shard_map/ppermute | solution.py:590
  31.5 12.3 %collective-permute-start.1 = (f32[4,192,128]{2,1,0:T(8,128)S(1)}, f32[4,192,128]{2,1,0:T(8,128)S(1)}, u32[]{:S(2)}, u32[]{:S(2)}) collective-permute-start(f32[4,192,128]{2,1,0:T(8,128)S(1)} %get-tuple-element.114), channel_id=1, source_target_pairs={{0,2},{1,3},{2,0},{3,1},{4,6},{5,7},{6,4},{7,5},{8,10},{9,11},{10,... | collective-permute-start | bytes 1179656 | tf_op jit(solution)/shard_map/ppermute | solution.py:590
  34.8 11.0 %collective-permute-start.6 = (f32[4,192,128]{2,1,0:T(8,128)S(1)}, f32[4,192,128]{2,1,0:T(8,128)S(1)}, u32[]{:S(2)}, u32[]{:S(2)}) collective-permute-start(f32[4,192,128]{2,1,0:T(8,128)S(1)} %get-tuple-element.116), channel_id=1, source_target_pairs={{0,4},{1,5},{2,6},{3,7},{4,0},{5,1},{6,2},{7,3},{8,12},{9,13},{10,... | collective-permute-start | bytes 1179656 | tf_op jit(solution)/shard_map/ppermute | solution.py:590
  36.3 26.2 %copy-start.2 = (bf16[6,512,256]{2,1,0:T(8,128)(2,1)S(1)}, bf16[6,512,256]{2,1,0:T(8,128)(2,1)}, u32[]{:S(2)}) copy-start(bf16[6,512,256]{2,1,0:T(8,128)(2,1)} %refs_2_.1) | copy-start | bytes 4718596
  36.3 26.2 %copy-start.3 = (f32[1024,128]{1,0:T(8,128)S(1)}, f32[1024,128]{1,0:T(8,128)}, u32[]{:S(2)}) copy-start(f32[1024,128]{1,0:T(8,128)} %get-tuple-element.80.refs_0_) | copy-start | bytes 1572868
  36.3 26.2 %copy-start.4 = (bf16[1024,128]{1,0:T(8,128)(2,1)S(1)}, bf16[1024,128]{1,0:T(8,128)(2,1)}, u32[]{:S(2)}) copy-start(bf16[1024,128]{1,0:T(8,128)(2,1)} %get-tuple-element.81.refs_1_) | copy-start | bytes 786436
  36.5 11.6 %collective-permute-start.5 = (f32[4,208,128]{2,1,0:T(8,128)S(1)}, f32[4,208,128]{2,1,0:T(8,128)S(1)}, u32[]{:S(2)}, u32[]{:S(2)}) collective-permute-start(f32[4,208,128]{2,1,0:T(8,128)S(1)} %get-tuple-element.111), channel_id=1, source_target_pairs={{0,8},{1,9},{2,10},{3,11},{4,12},{5,13},{6,14},{7,15},{8,0},{9,1},... | collective-permute-start | bytes 1277960 | tf_op jit(solution)/shard_map/ppermute | solution.py:590
  43.9 18.7 %copy-start.1 = (bf16[6,1024,256]{2,1,0:T(8,128)(2,1)S(1)}, bf16[6,1024,256]{2,1,0:T(8,128)(2,1)}, u32[]{:S(2)}) copy-start(bf16[6,1024,256]{2,1,0:T(8,128)(2,1)} %get-tuple-element.83.refs_8_) | copy-start | bytes 9437188
  43.9 6.5 %collective-permute-start.4 = (f32[2,192,128]{2,1,0:T(8,128)S(1)}, f32[2,192,128]{2,1,0:T(8,128)S(1)}, u32[]{:S(2)}, u32[]{:S(2)}) collective-permute-start(f32[2,192,128]{2,1,0:T(8,128)S(1)} %get-tuple-element.120), channel_id=1, source_target_pairs={{0,4},{1,5},{2,6},{3,7},{4,0},{5,1},{6,2},{7,3},{8,12},{9,13},{10,... | collective-permute-start | bytes 589832 | tf_op jit(solution)/shard_map/ppermute | solution.py:590
  45.8 6.4 %collective-permute-start.9 = (f32[2,192,128]{2,1,0:T(8,128)S(1)}, f32[2,192,128]{2,1,0:T(8,128)S(1)}, u32[]{:S(2)}, u32[]{:S(2)}) collective-permute-start(f32[2,192,128]{2,1,0:T(8,128)S(1)} %get-tuple-element.122), channel_id=1, source_target_pairs={{0,8},{1,9},{2,10},{3,11},{4,12},{5,13},{6,14},{7,15},{8,0},{9,1},... | collective-permute-start | bytes 589832 | tf_op jit(solution)/shard_map/ppermute | solution.py:590
  48.1 14.4 %copy-start = (bf16[6,1024,256]{2,1,0:T(8,128)(2,1)S(1)}, bf16[6,1024,256]{2,1,0:T(8,128)(2,1)}, u32[]{:S(2)}) copy-start(bf16[6,1024,256]{2,1,0:T(8,128)(2,1)} %get-tuple-element.82.refs_7_) | copy-start | bytes 9437188
  48.2 14.4 %copy-start.5 = (bf16[2,512,4]{1,2,0:T(4,128)(2,1)S(1)}, bf16[2,512,4]{1,2,0:T(4,128)(2,1)}, u32[]{:S(2)}) copy-start(bf16[2,512,4]{1,2,0:T(4,128)(2,1)} %param.25) | copy-start | bytes 24580
  48.2 14.4 %copy-start.6 = (bf16[512,6]{0,1:T(8,128)(2,1)S(1)}, bf16[512,6]{0,1:T(8,128)(2,1)}, u32[]{:S(2)}) copy-start(bf16[512,6]{0,1:T(8,128)(2,1)} %param.27) | copy-start | bytes 18436
  48.2 6.8 %collective-permute-start.8 = (f32[2,208,128]{2,1,0:T(8,128)S(1)}, f32[2,208,128]{2,1,0:T(8,128)S(1)}, u32[]{:S(2)}, u32[]{:S(2)}) collective-permute-start(f32[2,208,128]{2,1,0:T(8,128)S(1)} %get-tuple-element.117), channel_id=1, source_target_pairs={{0,2},{1,3},{2,0},{3,1},{4,6},{5,7},{6,4},{7,5},{8,10},{9,11},{10,... | collective-permute-start | bytes 638984 | tf_op jit(solution)/shard_map/ppermute | solution.py:590
  50.4 5.2 %collective-permute-start.7 = (f32[1,192,128]{2,1,0:T(8,128)S(1)}, f32[1,192,128]{2,1,0:T(8,128)S(1)}, u32[]{:S(2)}, u32[]{:S(2)}) collective-permute-start(f32[1,192,128]{2,1,0:T(8,128)S(1)} %slice_add_fusion.16), channel_id=1, source_target_pairs={{0,8},{1,9},{2,10},{3,11},{4,12},{5,13},{6,14},{7,15},{8,0},{9,1},... | collective-permute-start | bytes 294920 | tf_op jit(solution)/shard_map/ppermute | solution.py:590
  52.2 4.7 %collective-permute-start.10 = (f32[1,192,128]{2,1,0:T(8,128)S(1)}, f32[1,192,128]{2,1,0:T(8,128)S(1)}, u32[]{:S(2)}, u32[]{:S(2)}) collective-permute-start(f32[1,192,128]{2,1,0:T(8,128)S(1)} %slice_add_fusion.15), channel_id=1, source_target_pairs={{0,2},{1,3},{2,0},{3,1},{4,6},{5,7},{6,4},{7,5},{8,10},{9,11},{10,... | collective-permute-start | bytes 294920 | tf_op jit(solution)/shard_map/ppermute | solution.py:590
  55.0 4.8 %collective-permute-start.11 = (f32[1,208,128]{2,1,0:T(8,128)S(1)}, f32[1,208,128]{2,1,0:T(8,128)S(1)}, u32[]{:S(2)}, u32[]{:S(2)}) collective-permute-start(f32[1,208,128]{2,1,0:T(8,128)S(1)} %slice_add_fusion.13), channel_id=1, source_target_pairs={{0,4},{1,5},{2,6},{3,7},{4,0},{5,1},{6,2},{7,3},{8,12},{9,13},{10,... | collective-permute-start | bytes 319496 | tf_op jit(solution)/shard_map/ppermute | solution.py:590
  59.9 12.0 %collective-permute-start.12 = (f32[1,592,128]{2,1,0:T(8,128)S(1)}, f32[1,592,128]{2,1,0:T(8,128)S(1)}, u32[]{:S(2)}, u32[]{:S(2)}) collective-permute-start(f32[1,592,128]{2,1,0:T(8,128)S(1)} %pad_maximum_fusion.6), channel_id=1, source_target_pairs={{0,16},{1,17},{2,18},{3,19},{4,20},{5,21},{6,22},{7,23},{8,24},{9,... | collective-permute-start | bytes 909320 | tf_op jit(solution)/shard_map/ppermute | solution.py:590
  71.9 4.7 %collective-permute-start.15 = (f32[1,192,128]{2,1,0:T(8,128)S(1)}, f32[1,192,128]{2,1,0:T(8,128)S(1)}, u32[]{:S(2)}, u32[]{:S(2)}) collective-permute-start(f32[1,192,128]{2,1,0:T(8,128)S(1)} %get-tuple-element.123), channel_id=1, source_target_pairs={{0,8},{1,9},{2,10},{3,11},{4,12},{5,13},{6,14},{7,15},{8,0},{9,1},... | collective-permute-start | bytes 294920 | tf_op jit(solution)/shard_map/ppermute | solution.py:590
  72.7 5.4 %collective-permute-start.14 = (f32[1,192,128]{2,1,0:T(8,128)S(1)}, f32[1,192,128]{2,1,0:T(8,128)S(1)}, u32[]{:S(2)}, u32[]{:S(2)}) collective-permute-start(f32[1,192,128]{2,1,0:T(8,128)S(1)} %get-tuple-element.124), channel_id=1, source_target_pairs={{0,2},{1,3},{2,0},{3,1},{4,6},{5,7},{6,4},{7,5},{8,10},{9,11},{10,... | collective-permute-start | bytes 294920 | tf_op jit(solution)/shard_map/ppermute | solution.py:590
  73.8 5.8 %collective-permute-start.13 = (f32[1,208,128]{2,1,0:T(8,128)S(1)}, f32[1,208,128]{2,1,0:T(8,128)S(1)}, u32[]{:S(2)}, u32[]{:S(2)}) collective-permute-start(f32[1,208,128]{2,1,0:T(8,128)S(1)} %slice.170), channel_id=1, source_target_pairs={{0,4},{1,5},{2,6},{3,7},{4,0},{5,1},{6,2},{7,3},{8,12},{9,13},{10,... | collective-permute-start | bytes 319496 | tf_op jit(solution)/shard_map/ppermute | solution.py:590
  76.6 5.7 %collective-permute-start.18 = (f32[2,192,128]{2,1,0:T(8,128)S(1)}, f32[2,192,128]{2,1,0:T(8,128)S(1)}, u32[]{:S(2)}, u32[]{:S(2)}) collective-permute-start(f32[2,192,128]{2,1,0:T(8,128)S(1)} %pad_maximum_fusion.8), channel_id=1, source_target_pairs={{0,4},{1,5},{2,6},{3,7},{4,0},{5,1},{6,2},{7,3},{8,12},{9,13},{10,... | collective-permute-start | bytes 589832 | tf_op jit(solution)/shard_map/ppermute | solution.py:590
  78.1 5.7 %collective-permute-start.17 = (f32[2,192,128]{2,1,0:T(8,128)S(1)}, f32[2,192,128]{2,1,0:T(8,128)S(1)}, u32[]{:S(2)}, u32[]{:S(2)}) collective-permute-start(f32[2,192,128]{2,1,0:T(8,128)S(1)} %pad_maximum_fusion.9), channel_id=1, source_target_pairs={{0,8},{1,9},{2,10},{3,11},{4,12},{5,13},{6,14},{7,15},{8,0},{9,1},... | collective-permute-start | bytes 589832 | tf_op jit(solution)/shard_map/ppermute | solution.py:590
  79.7 8.2 %collective-permute-start.16 = (f32[2,208,128]{2,1,0:T(8,128)S(1)}, f32[2,208,128]{2,1,0:T(8,128)S(1)}, u32[]{:S(2)}, u32[]{:S(2)}) collective-permute-start(f32[2,208,128]{2,1,0:T(8,128)S(1)} %pad_maximum_fusion.7), channel_id=1, source_target_pairs={{0,2},{1,3},{2,0},{3,1},{4,6},{5,7},{6,4},{7,5},{8,10},{9,11},{10,... | collective-permute-start | bytes 638984 | tf_op jit(solution)/shard_map/ppermute | solution.py:590
  82.4 10.8 %collective-permute-start.21 = (f32[4,192,128]{2,1,0:T(8,128)S(1)}, f32[4,192,128]{2,1,0:T(8,128)S(1)}, u32[]{:S(2)}, u32[]{:S(2)}) collective-permute-start(f32[4,192,128]{2,1,0:T(8,128)S(1)} %pad_maximum_fusion.4), channel_id=1, source_target_pairs={{0,2},{1,3},{2,0},{3,1},{4,6},{5,7},{6,4},{7,5},{8,10},{9,11},{10,... | collective-permute-start | bytes 1179656 | tf_op jit(solution)/shard_map/ppermute | solution.py:590
  83.9 9.4 %collective-permute-start.20 = (f32[4,192,128]{2,1,0:T(8,128)S(1)}, f32[4,192,128]{2,1,0:T(8,128)S(1)}, u32[]{:S(2)}, u32[]{:S(2)}) collective-permute-start(f32[4,192,128]{2,1,0:T(8,128)S(1)} %pad_maximum_fusion.5), channel_id=1, source_target_pairs={{0,4},{1,5},{2,6},{3,7},{4,0},{5,1},{6,2},{7,3},{8,12},{9,13},{10,... | collective-permute-start | bytes 1179656 | tf_op jit(solution)/shard_map/ppermute | solution.py:590
  87.9 8.2 %collective-permute-start.19 = (f32[4,208,128]{2,1,0:T(8,128)S(1)}, f32[4,208,128]{2,1,0:T(8,128)S(1)}, u32[]{:S(2)}, u32[]{:S(2)}) collective-permute-start(f32[4,208,128]{2,1,0:T(8,128)S(1)} %pad_maximum_fusion.3), channel_id=1, source_target_pairs={{0,8},{1,9},{2,10},{3,11},{4,12},{5,13},{6,14},{7,15},{8,0},{9,1},... | collective-permute-start | bytes 1277960 | tf_op jit(solution)/shard_map/ppermute | solution.py:590
  96.2 6.0 %collective-permute-start.22 = (f32[8,208,128]{2,1,0:T(8,128)S(1)}, f32[8,208,128]{2,1,0:T(8,128)S(1)}, u32[]{:S(2)}, u32[]{:S(2)}) collective-permute-start(f32[8,208,128]{2,1,0:T(8,128)S(1)} %pad_maximum_fusion.refs_1_), channel_id=1, source_target_pairs={{0,1},{1,0},{2,3},{3,2},{4,5},{5,4},{6,7},{7,6},{8,9},{9,8},{10,11... | collective-permute-start | bytes 2555912 | tf_op jit(solution)/shard_map/ppermute | solution.py:590
  96.2 3.5 %collective-permute-start.24 = (f32[8,192,128]{2,1,0:T(8,128)S(1)}, f32[8,192,128]{2,1,0:T(8,128)S(1)}, u32[]{:S(2)}, u32[]{:S(2)}) collective-permute-start(f32[8,192,128]{2,1,0:T(8,128)S(1)} %pad_maximum_fusion.1.refs_1_), channel_id=1, source_target_pairs={{0,1},{1,0},{2,3},{3,2},{4,5},{5,4},{6,7},{7,6},{8,9},{9,8},{10,11... | collective-permute-start | bytes 2359304 | tf_op jit(solution)/shard_map/ppermute | solution.py:590
  96.7 4.2 %collective-permute-start.23 = (f32[8,192,128]{2,1,0:T(8,128)S(1)}, f32[8,192,128]{2,1,0:T(8,128)S(1)}, u32[]{:S(2)}, u32[]{:S(2)}) collective-permute-start(f32[8,192,128]{2,1,0:T(8,128)S(1)} %pad_maximum_fusion.2.refs_1_), channel_id=1, source_target_pairs={{0,1},{1,0},{2,3},{3,2},{4,5},{5,4},{6,7},{7,6},{8,9},{9,8},{10,11... | collective-permute-start | bytes 2359304 | tf_op jit(solution)/shard_map/ppermute | solution.py:590
  (4 other events, 40.4 us)

commit v2 on v1

--- a/solution.py
+++ b/solution.py
@@ -271,77 +271,108 @@
         part = dot_nt(cot_ref[k], column_matrix(z, k, bias_ref))
         along = part if along is None else along + part
         bias_sums.append(dot_tn(few, cot_ref[k]))
-    embed = jnp.zeros((z.rows, LANES), f32)
+    held = {"along": along, "embed": jnp.zeros((z.rows, LANES), f32)}
     scale = 1.0 / z.out
-    for index, span in enumerate(SPANS):
-        for e in range(*span):
-
-            def row(ref):
-                return ref[e : e + 1, :].astype(f32)
-
-            def mean(v):
-                return jnp.sum(v, axis=1, keepdims=True) * scale
-
-            def keep(q, v):
+
+    def expert(index, e):
+        span = SPANS[index]
+
+        def row(ref):
+            return ref[e : e + 1, :].astype(f32)
+
+        def mean(v):
+            return jnp.sum(v, axis=1, keepdims=True) * scale
+
+        def keep(q, v):
+            for h in range(z.halves):
+                line = z.sums_at + e * z.sum_rows + q * z.halves + h
+                small_s[line : line + 1, :] = v[:, h * LANES : (h + 1) * LANES]
+
+        def total(v):
+            return jnp.sum(v, axis=0, keepdims=True)
+
+        gain = row(gain_ref)
+        half = dot(features_s[...], w_first_ref[e]) + 0.5 * row(b_first_ref)
+        yield
+        turn = jnp.tanh(half)
+        up = 1.0 + turn
+        smooth = half * up
+        hidden = smooth.astype(bf16)
+        yield
+        second = dot(hidden, w_second_ref[e]) + row(b_second_ref)
+        yield
+        center = second - mean(second)
+        inverse = lax.rsqrt(mean(center * center) + epsilon)
+        normed = center * inverse
+        normed_s[e] = normed.astype(bf16)
+        send(normed_s.at[e], normed_ref.at[e])
+        low = normed.astype(bf16)
+        low_gain = gain_ref[e : e + 1, :]
+        gained = low * low_gain
+        upstream = None
+        along = held["along"]
+        for k, column in z.columns[e]:
+            cot = cot_ref[k]
+            part = few[:, column : column + 1] * cot
+            upstream = part if upstream is None else upstream + part
+            found = jnp.sum((cot * gained).astype(f32), axis=1, keepdims=True)
+            along = jnp.where(lane == column, along + found, along)
+        held["along"] = along
+        product = upstream * low
+        scaled = upstream * low_gain
+        average = jnp.full((z.out, LANES), scale, bf16)
+        first_mean = dot(scaled, average).astype(bf16)
+        second_mean = dot(product * low_gain, average).astype(bf16)
+        first_mean = jnp.concatenate([first_mean] * z.halves, axis=1)
+        second_mean = jnp.concatenate([second_mean] * z.halves, axis=1)
+        second_grad = inverse.astype(bf16) * (scaled - first_mean - low * second_mean)
+        ones = jnp.ones((16, z.rows), bf16)
+        keep(1, dot(ones, second_grad)[:1])
+        keep(2, dot(ones, product)[:1])
+        yield
+        hidden_grad = dot_nt(second_grad, w_second_ref[e])
+        second_total = dot_tn(hidden, second_grad) * grad_scale
+        yield
+        first_grad = hidden_grad * (up + smooth * (1.0 - turn))
+        keep(0, 0.5 * total(first_grad))
+        first_s[e] = first_grad.astype(bf16)
+        send(first_s.at[e], first_ref.at[e])
+        yield
+        first_total = dot_tn(features_s[...], first_s[e]) * grad_scale
+        held["embed"] = held["embed"] + dot_nt(first_s[e], w_first_ref[e, z.dense :, :])
+        found = None
+        for k, column in z.columns[e]:
+            part = bias_sums[k][column : column + 1, :]
+            found = part if found is None else found + part
+        keep(3, found)
+        line = (e - span[0]) * z.expert_rows
+        lines = pl.ds(line, z.expert_rows)
+        for shard in range(BLOCKS):
+            at = block_of(shard, ORDERS[index], core, own)
+            begin = line
+            for v, count in ((first_total, z.first_rows), (second_total, z.second_rows)):
                 for h in range(z.halves):
-                    line = z.sums_at + e * z.sum_rows + q * z.halves + h
-                    small_s[line : line + 1, :] = v[:, h * LANES : (h + 1) * LANES]
-
-            def total(v):
-                return jnp.sum(v, axis=0, keepdims=True)
-
-            gain = row(gain_ref)
-            half = dot(features_s[...], w_first_ref[e]) + 0.5 * row(b_first_ref)
-            turn = jnp.tanh(half)
-            up = 1.0 + turn
-            smooth = half * up
-            hidden = smooth.astype(bf16)
-            second = dot(hidden, w_second_ref[e]) + row(b_second_ref)
-            center = second - mean(second)
-            inverse = lax.rsqrt(mean(center * center) + epsilon)
-            normed = center * inverse
-            normed_s[e] = normed.astype(bf16)
-            send(normed_s.at[e], normed_ref.at[e])
-            gained = normed * gain
-            upstream = None
-            for k, column in z.columns[e]:
-                cot = cot_ref[k].astype(f32)
-                part = weights_s[:, column : column + 1] * cot
-                upstream = part if upstream is None else upstream + part
-                found = jnp.sum(cot * gained, axis=1, keepdims=True)
-                along = jnp.where(lane == column, along + found, along)
-            product = upstream * normed
-            scaled = upstream * gain
-            second_grad = inverse * (scaled - mean(scaled) - normed * mean(product * gain))
-            keep(1, total(second_grad))
-            keep(2, total(product))
-            second_grad = second_grad.astype(bf16)
-            second_total = dot_tn(hidden, second_grad) * grad_scale
-            first_grad = dot_nt(second_grad, w_second_ref[e]) * (up + smooth * (1.0 - turn))
-            keep(0, 0.5 * total(first_grad))
-            first_s[e] = first_grad.astype(bf16)
-            send(first_s.at[e], first_ref.at[e])
-            first_total = dot_tn(features_s[...], first_s[e]) * grad_scale
-            embed = embed + dot_nt(first_s[e], w_first_ref[e, z.dense :, :])
-            found = None
-            for k, column in z.columns[e]:
-                part = bias_sums[k][column : column + 1, :]
-                found = part if found is None else found + part
-            keep(3, found)
-            line = (e - span[0]) * z.expert_rows
-            lines = pl.ds(line, z.expert_rows)
-            for shard in range(BLOCKS):
-                at = block_of(shard, ORDERS[index], core, own)
-                begin = line
-                for v, count in ((first_total, z.first_rows), (second_total, z.second_rows)):
-                    for h in range(z.halves):
-                        packed_s[index][at, begin : begin + count, :] = v[
-                            shard * count : (shard + 1) * count, h * LANES : (h + 1) * LANES
-                        ]
-                        begin += count
-            for side in range(2):
-                blocks = pl.ds(side * (BLOCKS // 2), BLOCKS // 2)
-                send(packed_s[index].at[blocks, lines, :], piece_refs[index][side].at[:, lines, :])
+                    packed_s[index][at, begin : begin + count, :] = v[
+                        shard * count : (shard + 1) * count, h * LANES : (h + 1) * LANES
+                    ]
+                    begin += count
+        for side in range(2):
+            blocks = pl.ds(side * (BLOCKS // 2), BLOCKS // 2)
+            send(packed_s[index].at[blocks, lines, :], piece_refs[index][side].at[:, lines, :])
+        yield
+
+    chains = [expert(index, e) for index, span in enumerate(SPANS) for e in range(*span)]
+    for _ in range(3):
+        next(chains[0])
+    for this, then in zip(chains, chains[1:] + [iter([None] * 7)]):
+        next(then)
+        next(this)
+        next(this)
+        next(then)
+        next(then)
+        next(this)
+        next(this)
+    along, embed = held["along"], held["embed"]
     logit_grad = logit_part(z, weights_s[...], along)
     logit_s[...] = logit_grad
     send(logit_s, logit_ref)
@@ -390,40 +421,33 @@
     dense_ref[...] = 0.5 * dense + dot(logit_ref[...], gates[:, : z.dense])
 
 
-def unpack_kernel(z, index, *refs):
-    last = index == len(SPANS) - 1
+def unpack_kernel(z, index, side, place_ref, device_ref, piece_ref, *refs):
+    last = index == len(SPANS) - 1 and side == 1
     refs = list(refs)
 
     def take(count):
         return [refs.pop(0) for _ in range(count)]
 
-    device_ref, near_ref, far_ref = take(3)
-    if index:
+    if last:
+        small_refs = take(2)
+    if index or side:
         take(2)
     w_first_ref, w_second_ref = take(2)
     core, own = device_bits(device_ref[0])
-    base = pl.program_id(0) * z.expert_rows
     count = BLOCKS // 2
 
-    def unpack(shard, side, from_ref):
-        at = lax.bitwise_and(block_of(shard, ORDERS[index], core, own), count - 1)
+    def at(shard):
+        return lax.bitwise_and(block_of(shard, ORDERS[index], core, own), count - 1)
+
+    for shard in range(count):
+        block = at(shard)
         line = 0
         for ref, rows in ((w_first_ref, z.first_rows), (w_second_ref, z.second_rows)):
             for h in range(z.halves):
-                lines = pl.ds(pl.multiple_of(base + line, 8), rows)
-                ref[0, shard * rows : (shard + 1) * rows, h * LANES : (h + 1) * LANES] = from_ref[
-                    at, lines, :
-                ]
+                ref[0, shard * rows : (shard + 1) * rows, h * LANES : (h + 1) * LANES] = (
+                    piece_ref[block, line : line + rows, :]
+                )
                 line += rows
-
-    for side, from_ref in enumerate((near_ref, far_ref)):
-        for owner in range(2):
-
-            @pl.when(lax.bitwise_xor(core, owner) == side)
-            def _():
-                for shard in range(owner * count, (owner + 1) * count):
-                    unpack(shard, side, from_ref)
-
     if not last:
         return
     table_ref, gate_task_ref, gate_task_bias_ref, gate_shared_ref, gate_shared_bias_ref = take(5)
@@ -432,18 +456,11 @@
 
     @pl.when(pl.program_id(0) == 0)
     def _():
-        start = (SPANS[index][1] - SPANS[index][0]) * z.expert_rows
-        for side, from_ref in enumerate((near_ref, far_ref)):
-            for owner in range(2):
-
-                @pl.when(lax.bitwise_xor(core, owner) == side)
-                def _():
-                    for shard in range(owner * count, (owner + 1) * count):
-                        at = block_of(shard, ORDERS[index], core, own)
-                        small_s[shard * z.small_rows : (shard + 1) * z.small_rows, :] = from_ref[
-                            lax.bitwise_and(at, count - 1), start:, :
-                        ]
-
+        for half, from_ref in enumerate(small_refs):
+            start = lax.bitwise_xor(core, half) * (count * z.small_rows)
+            for shard in range(count):
+                lines = pl.ds(pl.multiple_of(start + shard * z.small_rows, 8), z.small_rows)
+                small_s[lines, :] = from_ref[at(shard)]
         for low in range(z.low):
             table_ref[:, low * z.high : (low + 1) * z.high] = small_s[
                 low * z.emb : (low + 1) * z.emb, :
@@ -549,15 +566,35 @@
     )(weights, logit_grad, w_first, gain, bias, *gates, normed, firsts)
 
 
-def run_unpack(z, index, device, near, far, earlier):
-    last = index == len(SPANS) - 1
+def run_unpack(z, index, side, device, pieces, earlier):
+    last = index == len(SPANS) - 1 and side == 1
     lo, hi = SPANS[index]
+    half = BLOCKS // 2
     out_shape = [
         shape_of((z.experts, z.d_in, z.hidden)),
         shape_of((z.experts, z.hidden, z.out)),
     ]
-    out_specs = [pl.BlockSpec((1,) + v.shape[1:], lambda at: (lo + at, 0, 0)) for v in out_shape]
+
+    def half_spec(array):
+        shape = (1, array.shape[1] // 2, array.shape[2])
+        return pl.BlockSpec(shape, lambda at, place: (lo + at, lax.bitwise_xor(place[0], side), 0))
+
+    def fixed(array):
+        return pl.BlockSpec(array.shape, lambda at, place: (0,) * len(array.shape))
+
+    out_specs = [half_spec(v) for v in out_shape]
+    operands = [pieces[side]]
+    in_specs = [SMEM, pl.BlockSpec((half, z.expert_rows, LANES), lambda at, place: (0, at, 0))]
     scratch = []
+    if last:
+        start = (hi - lo) * z.expert_rows // z.small_rows
+        operands += list(pieces)
+        in_specs += [
+            pl.BlockSpec((half, z.small_rows, LANES), lambda at, place: (0, start, 0))
+        ] * 2
+    aliases = {2 + len(operands): 0, 3 + len(operands): 1} if earlier else {}
+    operands += list(earlier)
+    in_specs += [ANY] * len(earlier)
     if last:
         small = [
             shape_of((z.emb, z.vocab)),
@@ -567,21 +604,24 @@
             shape_of((1, z.experts)),
         ] + [shape_of((z.experts, z.out))] * 4
         out_shape += small
-        out_specs += [whole(v) for v in small]
+        out_specs += [fixed(v) for v in small]
         scratch = [pltpu.VMEM((z.small_rows * BLOCKS, LANES), f32)]
-    operands = [device, near, far] + list(earlier)
+    core = lax.bitwise_and(device, 1)
     return pl.pallas_call(
-        functools.partial(unpack_kernel, z, index),
-        grid=(hi - lo,),
-        in_specs=[SMEM, whole(near), whole(far)] + [ANY] * len(earlier),
-        out_specs=out_specs,
+        functools.partial(unpack_kernel, z, index, side),
+        grid_spec=pltpu.PrefetchScalarGridSpec(
+            num_scalar_prefetch=1,
+            grid=(hi - lo,),
+            in_specs=in_specs,
+            out_specs=out_specs,
+            scratch_shapes=scratch,
+        ),
         out_shape=out_shape,
-        scratch_shapes=scratch,
-        input_output_aliases={3: 0, 4: 1} if earlier else {},
+        input_output_aliases=aliases,
         compiler_params=pltpu.CompilerParams(vmem_limit_bytes=24 * MIB),
         cost_estimate=pl.CostEstimate(flops=0, bytes_accessed=4 * MIB, transcendentals=0),
-        name="unpack_%d" % index,
-    )(*operands)
+        name="unpack_%d_%d" % (index, side),
+    )(core, device, *operands)
 
 
 def exchange(value, axis):
@@ -594,7 +634,7 @@
     return lax.optimization_barrier((value, other))[0]
 
 
-def sum_pieces(near, far, outputs):
+def sum_pieces(near, far, outputs, unpack):
     count = len(near)
     got = [exchange(v, "c") for v in far]
     sent = None
@@ -622,11 +662,17 @@
             got[i] = exchange(near[i], ORDERS[i][step])
             sent = near[i]
     far = []
+    grads = ()
     for i in range(count):
         near[i] = jnp.concatenate([near[i], after(got[i], sent)], axis=0)
+        if i:
+            near[i] = after(near[i], grads[0])
         sent = near[i]
         far.append(exchange(near[i], "c"))
-    return near, far, results
+        grads = unpack(i, 0, near[i], None, grads)
+    for i in range(count):
+        grads = unpack(i, 1, near[i], far[i], grads)
+    return grads, results
 
 
 def local(
@@ -688,15 +734,19 @@
             z, first, logit_grad, w_first, ln_gain, ln_bias, gates, normed, firsts
         )
 
+    def unpack(index, side, near, far, earlier):
+        return run_unpack(z, index, side, device, (near, far), earlier)
+
     if fits:
-        near, far, results = sum_pieces(near, far, outputs)
+        grads, results = sum_pieces(near, far, outputs, unpack)
     else:
         results = outputs(None)
         near, far = lax.psum((near, far), BOTH)
+        grads = ()
+        for side in range(2):
+            for index in range(len(SPANS)):
+                grads = unpack(index, side, near[index], far[index], grads)
     mixed, dense_grad = results
-    grads = ()
-    for index in range(len(SPANS)):
-        grads = run_unpack(z, index, device, near[index], far[index], grads[:2])
     w_first_grad, w_second_grad, table_grad = grads[:3]
     gate_task_grad, gate_task_bias_grad, gate_shared_grad, gate_shared_bias_grad = grads[3:7]
     b_first_grad, b_second_grad, gain_grad, bias_grad = grads[7:]

time: 104 us -> 96.1 us (0.924)
  Pallas kernels: 36.1 us -> 31.6 us
  waiting for transfers between devices: 36.2 us -> 32 us
  starting transfers between devices: 28.1 us -> 29.3 us
    pallas_call x1, Pallas kernels: 27 us -> 20 us  [run_main(): pl.pallas_call(functools.partial(main_kernel, z, grad_scale), in_specs=[S...]
    ppermute x25, waiting for transfers between devices: 36.2 us -> 32 us  [exchange(): return lax.ppermute(value, BOTH, [(i, i ^ flip) for i in range(count)])]
    pallas_call x3 -> x6, Pallas kernels: 3.92 us -> 6.39 us  [run_unpack(): pl.pallas_call(functools.partial(unpack_kernel, z, index, side), grid_spe...]
    ppermute x25, starting transfers between devices: 28.1 us -> 29.3 us  [exchange(): return lax.ppermute(value, BOTH, [(i, i ^ flip) for i in range(count)])]
  transfers between devices with their start and end apart: 25 -> 25, of which waited for: 16 -> 16; matrix products, arithmetic and copies ran while one was open for 2% -> 2% of each run, Pallas kernels for 7% -> 11%
where the time goes in v2:
time: 96.1 us; the launch traced here: 95.9 us
  waiting for transfers between devices  32 us (33%)
  Pallas kernels  31.6 us (33%)
  starting transfers between devices  29.3 us (30%)
  other arithmetic  1.94 us (2%)
  between operations  1.07 us (1%)
    ppermute x25, waiting for transfers between devices, exchange(): return lax.ppermute(value, BOTH, [(i, i ^ flip) for i in range(count)])  32 us
    ppermute x25, starting transfers between devices, exchange(): return lax.ppermute(value, BOTH, [(i, i ^ flip) for i in range(count)])  29.3 us
    pallas_call x1, Pallas kernels, run_main(): pl.pallas_call(functools.partial(main_kernel, z, grad_scale), in_specs=[S...  20 us
    pallas_call x6, Pallas kernels, run_unpack(): pl.pallas_call(functools.partial(unpack_kernel, z, index, side), grid_spe...  6.39 us
    pallas_call x1, Pallas kernels, run_outputs(): pl.pallas_call(functools.partial(outputs_kernel, z), grid=(z.rows // bloc...  5.19 us
  transfers between devices with their start and end apart: 25, of which 16 were waited for; matrix products, arithmetic and copies ran while one was open for 2% of the time, Pallas kernels for 11%

profile of v2, /device:TPU:0, one launch (start us, length us, event | category | flops | bytes accessed | tf_op | source)
XLA Modules:
  0.0 95.9 jit_solution(6523599723858028755)
XLA Ops:
  0.7 20.0 %experts.1 = (f32[8,192,128]{2,1,0:T(8,128)}, f32[8,192,128]{2,1,0:T(8,128)}, f32[8,192,128]{2,1,0:T(8,128)}, f32[8,192,128]{2,1,0:T(8,128)}, f32[8,208,128]{2,1...) custom-call(s32[1]{0:T(128)} %bitcast.refs_0_.device_ref, ...), custom_call_target="tpu_custom_call" | custom-call | flops 7247757312 | bytes 20971520 | tf_op jit(solution)/shard_map/experts/pallas_call | solution.py:532
  21.7 1.6 %collective-permute-done = f32[8,192,128]{2,1,0:T(8,128)S(1)} collective-permute-done((f32[8,192,128]{2,1,0:T(8,128)}, f32[8,192,128]{2,1,0:T(8,128)S(1)}, u32[]{:S(2)}, u32[]{:S(2)}) %collective-permute-start) | collective-permute-done | bytes 786464 | tf_op jit(solution)/shard_map/ppermute | solution.py:630
  23.3 1.2 %slice_add_fusion.3 = (f32[4,192,128]{2,1,0:T(8,128)S(1)}, f32[4,192,128]{2,1,0:T(8,128)S(1)}) fusion(f32[8,192,128]{2,1,0:T(8,128)S(1)} %collective-permute-done, f32[8,192,128]{2,1,0:T(8,128)} %get-tuple-element.71), kind=kLoop, calls=%fused_computation.7 | loop fusion | flops 196608 | bytes 2359296 | tf_op jit(solution)/shard_map/add | solution.py:645
  24.5 2.9 %collective-permute-start.1 = (f32[4,192,128]{2,1,0:T(8,128)S(1)}, f32[4,192,128]{2,1,0:T(8,128)S(1)}, u32[]{:S(2)}, u32[]{:S(2)}) collective-permute-start(f32[4,192,128]{2,1,0:T(8,128)S(1)} %get-tuple-element.130), channel_id=1, source_target_pairs={{0,2},{1,3},{2,0},{3,1},{4,6},{5,7},{6,4},{7,5},{8,10},{9,11},{10,... | collective-permute-start | bytes 1179656 | tf_op jit(solution)/shard_map/ppermute | solution.py:630
  27.5 1.6 %collective-permute-start.6 = (f32[4,192,128]{2,1,0:T(8,128)S(1)}, f32[4,192,128]{2,1,0:T(8,128)S(1)}, u32[]{:S(2)}, u32[]{:S(2)}) collective-permute-start(f32[4,192,128]{2,1,0:T(8,128)S(1)} %get-tuple-element.132), channel_id=1, source_target_pairs={{0,4},{1,5},{2,6},{3,7},{4,0},{5,1},{6,2},{7,3},{8,12},{9,13},{10,... | collective-permute-start | bytes 1179656 | tf_op jit(solution)/shard_map/ppermute | solution.py:630
  29.2 1.6 %collective-permute-start.5 = (f32[4,208,128]{2,1,0:T(8,128)S(1)}, f32[4,208,128]{2,1,0:T(8,128)S(1)}, u32[]{:S(2)}, u32[]{:S(2)}) collective-permute-start(f32[4,208,128]{2,1,0:T(8,128)S(1)} %get-tuple-element.127), channel_id=1, source_target_pairs={{0,8},{1,9},{2,10},{3,11},{4,12},{5,13},{6,14},{7,15},{8,0},{9,1},... | collective-permute-start | bytes 1277960 | tf_op jit(solution)/shard_map/ppermute | solution.py:630
  30.9 6.0 %collective-permute-done.1 = f32[4,192,128]{2,1,0:T(8,128)S(1)} collective-permute-done((f32[4,192,128]{2,1,0:T(8,128)S(1)}, f32[4,192,128]{2,1,0:T(8,128)S(1)}, u32[]{:S(2)}, u32[]{:S(2)}) %collective-permute-start.1) | collective-permute-done | bytes 393248 | tf_op jit(solution)/shard_map/ppermute | solution.py:630
  36.9 1.8 %collective-permute-start.4 = (f32[2,192,128]{2,1,0:T(8,128)S(1)}, f32[2,192,128]{2,1,0:T(8,128)S(1)}, u32[]{:S(2)}, u32[]{:S(2)}) collective-permute-start(f32[2,192,128]{2,1,0:T(8,128)S(1)} %get-tuple-element.136), channel_id=1, source_target_pairs={{0,4},{1,5},{2,6},{3,7},{4,0},{5,1},{6,2},{7,3},{8,12},{9,13},{10,... | collective-permute-start | bytes 589832 | tf_op jit(solution)/shard_map/ppermute | solution.py:630
  38.8 1.6 %collective-permute-start.9 = (f32[2,192,128]{2,1,0:T(8,128)S(1)}, f32[2,192,128]{2,1,0:T(8,128)S(1)}, u32[]{:S(2)}, u32[]{:S(2)}) collective-permute-start(f32[2,192,128]{2,1,0:T(8,128)S(1)} %get-tuple-element.138), channel_id=1, source_target_pairs={{0,8},{1,9},{2,10},{3,11},{4,12},{5,13},{6,14},{7,15},{8,0},{9,1},... | collective-permute-start | bytes 589832 | tf_op jit(solution)/shard_map/ppermute | solution.py:630
  40.7 1.3 %collective-permute-start.8 = (f32[2,208,128]{2,1,0:T(8,128)S(1)}, f32[2,208,128]{2,1,0:T(8,128)S(1)}, u32[]{:S(2)}, u32[]{:S(2)}) collective-permute-start(f32[2,208,128]{2,1,0:T(8,128)S(1)} %get-tuple-element.133), channel_id=1, source_target_pairs={{0,2},{1,3},{2,0},{3,1},{4,6},{5,7},{6,4},{7,5},{8,10},{9,11},{10,... | collective-permute-start | bytes 638984 | tf_op jit(solution)/shard_map/ppermute | solution.py:630
  42.1 1.3 %collective-permute-done.4 = f32[2,192,128]{2,1,0:T(8,128)S(1)} collective-permute-done((f32[2,192,128]{2,1,0:T(8,128)S(1)}, f32[2,192,128]{2,1,0:T(8,128)S(1)}, u32[]{:S(2)}, u32[]{:S(2)}) %collective-permute-start.4) | collective-permute-done | bytes 196640 | tf_op jit(solution)/shard_map/ppermute | solution.py:630
  43.4 1.6 %collective-permute-start.7 = (f32[1,192,128]{2,1,0:T(8,128)S(1)}, f32[1,192,128]{2,1,0:T(8,128)S(1)}, u32[]{:S(2)}, u32[]{:S(2)}) collective-permute-start(f32[1,192,128]{2,1,0:T(8,128)S(1)} %slice_add_fusion.16), channel_id=1, source_target_pairs={{0,8},{1,9},{2,10},{3,11},{4,12},{5,13},{6,14},{7,15},{8,0},{9,1},... | collective-permute-start | bytes 294920 | tf_op jit(solution)/shard_map/ppermute | solution.py:630
  45.0 1.6 %collective-permute-start.10 = (f32[1,192,128]{2,1,0:T(8,128)S(1)}, f32[1,192,128]{2,1,0:T(8,128)S(1)}, u32[]{:S(2)}, u32[]{:S(2)}) collective-permute-start(f32[1,192,128]{2,1,0:T(8,128)S(1)} %slice_add_fusion.15), channel_id=1, source_target_pairs={{0,2},{1,3},{2,0},{3,1},{4,6},{5,7},{6,4},{7,5},{8,10},{9,11},{10,... | collective-permute-start | bytes 294920 | tf_op jit(solution)/shard_map/ppermute | solution.py:630
  48.2 1.5 %collective-permute-done.10 = f32[1,192,128]{2,1,0:T(8,128)S(1)} collective-permute-done((f32[1,192,128]{2,1,0:T(8,128)S(1)}, f32[1,192,128]{2,1,0:T(8,128)S(1)}, u32[]{:S(2)}, u32[]{:S(2)}) %collective-permute-start.10) | collective-permute-done | bytes 98336 | tf_op jit(solution)/shard_map/ppermute | solution.py:630
  49.7 2.6 %collective-permute-done.11 = f32[1,208,128]{2,1,0:T(8,128)S(1)} collective-permute-done((f32[1,208,128]{2,1,0:T(8,128)S(1)}, f32[1,208,128]{2,1,0:T(8,128)S(1)}, u32[]{:S(2)}, u32[]{:S(2)}) %collective-permute-start.11) | collective-permute-done | bytes 106528 | tf_op jit(solution)/shard_map/ppermute | solution.py:630
  52.3 2.7 %collective-permute-start.12 = (f32[1,592,128]{2,1,0:T(8,128)S(1)}, f32[1,592,128]{2,1,0:T(8,128)S(1)}, u32[]{:S(2)}, u32[]{:S(2)}) collective-permute-start(f32[1,592,128]{2,1,0:T(8,128)S(1)} %pad_maximum_fusion.6), channel_id=1, source_target_pairs={{0,16},{1,17},{2,18},{3,19},{4,20},{5,21},{6,22},{7,23},{8,24},{9,... | collective-permute-start | bytes 909320 | tf_op jit(solution)/shard_map/ppermute | solution.py:630
  55.1 5.2 %outputs.1 = (bf16[3,1024,256]{2,1,0:T(8,128)(2,1)}, f32[1024,384]{1,0:T(8,128)}) custom-call(f32[1024,128]{1,0:T(8,128)S(1)} %copy-done.3, bf16[1024,128]{1,0:T(8,128)(2,1)S(1)} %copy-done.4, bf16[6,512,256]{2,1,0:T(8,128)(2,1)S(1)} %copy-done.2, bf16[6,256]{1,0:T(8,128)(2,1)S(1)} %copy-done.7, bf16[6,256]{1,0:T(8,128)(2,1)S(1)} %copy-done.8, ...), custom_call_target="tpu_custom_call" | custom-call | flops 1207959552 | bytes 11534336 | tf_op jit(solution)/shard_map/outputs/pallas_call | solution.py:551
  60.3 4.5 %collective-permute-done.12 = f32[1,592,128]{2,1,0:T(8,128)S(1)} collective-permute-done((f32[1,592,128]{2,1,0:T(8,128)S(1)}, f32[1,592,128]{2,1,0:T(8,128)S(1)}, u32[]{:S(2)}, u32[]{:S(2)}) %collective-permute-start.12) | collective-permute-done | bytes 303136 | tf_op jit(solution)/shard_map/ppermute | solution.py:630
  66.5 1.3 %collective-permute-start.13 = (f32[1,208,128]{2,1,0:T(8,128)S(1)}, f32[1,208,128]{2,1,0:T(8,128)S(1)}, u32[]{:S(2)}, u32[]{:S(2)}) collective-permute-start(f32[1,208,128]{2,1,0:T(8,128)S(1)} %slice.170), channel_id=1, source_target_pairs={{0,4},{1,5},{2,6},{3,7},{4,0},{5,1},{6,2},{7,3},{8,12},{9,13},{10,... | collective-permute-start | bytes 319496 | tf_op jit(solution)/shard_map/ppermute | solution.py:630
  67.8 1.7 %collective-permute-done.15 = f32[1,192,128]{2,1,0:T(8,128)S(1)} collective-permute-done((f32[1,192,128]{2,1,0:T(8,128)S(1)}, f32[1,192,128]{2,1,0:T(8,128)S(1)}, u32[]{:S(2)}, u32[]{:S(2)}) %collective-permute-start.15) | collective-permute-done | bytes 98336 | tf_op jit(solution)/shard_map/ppermute | solution.py:630
  69.6 1.5 %collective-permute-start.18 = (f32[2,192,128]{2,1,0:T(8,128)S(1)}, f32[2,192,128]{2,1,0:T(8,128)S(1)}, u32[]{:S(2)}, u32[]{:S(2)}) collective-permute-start(f32[2,192,128]{2,1,0:T(8,128)S(1)} %pad_maximum_fusion.8), channel_id=1, source_target_pairs={{0,4},{1,5},{2,6},{3,7},{4,0},{5,1},{6,2},{7,3},{8,12},{9,13},{10,... | collective-permute-start | bytes 589832 | tf_op jit(solution)/shard_map/ppermute | solution.py:630
  72.4 1.1 %collective-permute-start.16 = (f32[2,208,128]{2,1,0:T(8,128)S(1)}, f32[2,208,128]{2,1,0:T(8,128)S(1)}, u32[]{:S(2)}, u32[]{:S(2)}) collective-permute-start(f32[2,208,128]{2,1,0:T(8,128)S(1)} %pad_maximum_fusion.7), channel_id=1, source_target_pairs={{0,2},{1,3},{2,0},{3,1},{4,6},{5,7},{6,4},{7,5},{8,10},{9,11},{10,... | collective-permute-start | bytes 638984 | tf_op jit(solution)/shard_map/ppermute | solution.py:630
  73.5 1.8 %collective-permute-done.18 = f32[2,192,128]{2,1,0:T(8,128)S(1)} collective-permute-done((f32[2,192,128]{2,1,0:T(8,128)S(1)}, f32[2,192,128]{2,1,0:T(8,128)S(1)}, u32[]{:S(2)}, u32[]{:S(2)}) %collective-permute-start.18) | collective-permute-done | bytes 196640 | tf_op jit(solution)/shard_map/ppermute | solution.py:630
  75.3 1.5 %collective-permute-start.21 = (f32[4,192,128]{2,1,0:T(8,128)S(1)}, f32[4,192,128]{2,1,0:T(8,128)S(1)}, u32[]{:S(2)}, u32[]{:S(2)}) collective-permute-start(f32[4,192,128]{2,1,0:T(8,128)S(1)} %pad_maximum_fusion.4), channel_id=1, source_target_pairs={{0,2},{1,3},{2,0},{3,1},{4,6},{5,7},{6,4},{7,5},{8,10},{9,11},{10,... | collective-permute-start | bytes 1179656 | tf_op jit(solution)/shard_map/ppermute | solution.py:630
  76.9 1.1 %collective-permute-start.20 = (f32[4,192,128]{2,1,0:T(8,128)S(1)}, f32[4,192,128]{2,1,0:T(8,128)S(1)}, u32[]{:S(2)}, u32[]{:S(2)}) collective-permute-start(f32[4,192,128]{2,1,0:T(8,128)S(1)} %pad_maximum_fusion.5), channel_id=1, source_target_pairs={{0,4},{1,5},{2,6},{3,7},{4,0},{5,1},{6,2},{7,3},{8,12},{9,13},{10,... | collective-permute-start | bytes 1179656 | tf_op jit(solution)/shard_map/ppermute | solution.py:630
  77.9 2.6 %collective-permute-done.16 = f32[2,208,128]{2,1,0:T(8,128)S(1)} collective-permute-done((f32[2,208,128]{2,1,0:T(8,128)S(1)}, f32[2,208,128]{2,1,0:T(8,128)S(1)}, u32[]{:S(2)}, u32[]{:S(2)}) %collective-permute-start.16) | collective-permute-done | bytes 213024 | tf_op jit(solution)/shard_map/ppermute | solution.py:630
  80.5 1.4 %collective-permute-start.19 = (f32[4,208,128]{2,1,0:T(8,128)S(1)}, f32[4,208,128]{2,1,0:T(8,128)S(1)}, u32[]{:S(2)}, u32[]{:S(2)}) collective-permute-start(f32[4,208,128]{2,1,0:T(8,128)S(1)} %pad_maximum_fusion.3), channel_id=1, source_target_pairs={{0,8},{1,9},{2,10},{3,11},{4,12},{5,13},{6,14},{7,15},{8,0},{9,1},... | collective-permute-start | bytes 1277960 | tf_op jit(solution)/shard_map/ppermute | solution.py:630
  81.9 4.5 %collective-permute-done.21 = f32[4,192,128]{2,1,0:T(8,128)S(1)} collective-permute-done((f32[4,192,128]{2,1,0:T(8,128)S(1)}, f32[4,192,128]{2,1,0:T(8,128)S(1)}, u32[]{:S(2)}, u32[]{:S(2)}) %collective-permute-start.21) | collective-permute-done | bytes 393248 | tf_op jit(solution)/shard_map/ppermute | solution.py:630
  87.5 1.0 %unpack_1_0.1 = (f32[6,512,256]{2,1,0:T(8,128)}, f32[6,256,256]{2,1,0:T(8,128)}) custom-call(s32[1]{0:T(128)S(6)} %and.4.place_ref, s32[1]{0:T(128)} %bitcast.refs_0_.device_ref, f32[8,192,128]{2,1,0:T(8,128)S(1)} %pad_maximum_fusion.2.piece_ref, f32[6,512,256]{2,1,0:T(8,128)} %get-tuple-element.103.refs_0_, ...), custom_call_target="tpu_custom_call", output_to_operand_aliasing={{0}: (3, {}), {1}: (4, {})} | custom-call | bytes 4194304 | tf_op jit(solution)/shard_map/unpack_1_0/pallas_call | solution.py:610
  89.4 1.0 %unpack_2_0.1 = (f32[6,512,256]{2,1,0:T(8,128)}, f32[6,256,256]{2,1,0:T(8,128)}) custom-call(s32[1]{0:T(128)S(6)} %and.4.place_ref, s32[1]{0:T(128)} %bitcast.refs_0_.device_ref, f32[8,208,128]{2,1,0:T(8,128)S(1)} %pad_maximum_fusion.piece_ref.refs_0_, f32[6,512,256]{2,1,0:T(8,128)} %get-tuple-element.107.refs_0_, ...), custom_call_target="tpu_custom_call", output_to_operand_aliasing={{0}: (3, {}), {1}: (4, {})} | custom-call | bytes 4194304 | tf_op jit(solution)/shard_map/unpack_2_0/pallas_call | solution.py:610
  90.5 1.9 %collective-permute-done.24.piece_ref = f32[8,192,128]{2,1,0:T(8,128)S(1)} collective-permute-done((f32[8,192,128]{2,1,0:T(8,128)S(1)}, f32[8,192,128]{2,1,0:T(8,128)S(1)}, u32[]{:S(2)}, u32[]{:S(2)}) %collective-permute-start.24) | collective-permute-done | bytes 786464 | tf_op jit(solution)/shard_map/ppermute | solution.py:630
  94.5 1.3 %unpack_2_1.1 = (f32[6,512,256]{2,1,0:T(8,128)}, f32[6,256,256]{2,1,0:T(8,128)}, f32[16,1024]{1,0:T(8,128)}, f32[2,4,512]{2,1,0:T(4,128)}, f32[2,4]{1,0:T(2,128)...) custom-call(s32[1]{0:T(128)S(6)} %and.4.place_ref, ...), custom_call_target="tpu_custom_call", output_to_operand_aliasing={{0}: (5, {}), {1}: (6, {})} | custom-call | bytes 4194304 | tf_op jit(solution)/shard_map/unpack_2_1/pallas_call | solution.py:610
  (72 shorter events, 10.6 us)
Async XLA Ops:
  20.7 2.6 %collective-permute-start = (f32[8,192,128]{2,1,0:T(8,128)}, f32[8,192,128]{2,1,0:T(8,128)S(1)}, u32[]{:S(2)}, u32[]{:S(2)}) collective-permute-start(f32[8,192,128]{2,1,0:T(8,128)} %get-tuple-element.72), channel_id=1, source_target_pairs={{0,1},{1,0},{2,3},{3,2},{4,5},{5,4},{6,7},{7,6},{8,9},{9,8},{10,11... | collective-permute-start | bytes 2359304 | tf_op jit(solution)/shard_map/ppermute | solution.py:630
  21.2 6.3 %collective-permute-start.3 = (f32[8,192,128]{2,1,0:T(8,128)}, f32[8,192,128]{2,1,0:T(8,128)S(1)}, u32[]{:S(2)}, u32[]{:S(2)}) collective-permute-start(f32[8,192,128]{2,1,0:T(8,128)} %get-tuple-element.76), channel_id=1, source_target_pairs={{0,1},{1,0},{2,3},{3,2},{4,5},{5,4},{6,7},{7,6},{8,9},{9,8},{10,11... | collective-permute-start | bytes 2359304 | tf_op jit(solution)/shard_map/ppermute | solution.py:630
  21.2 7.9 %collective-permute-start.2 = (f32[8,208,128]{2,1,0:T(8,128)}, f32[8,208,128]{2,1,0:T(8,128)S(1)}, u32[]{:S(2)}, u32[]{:S(2)}) collective-permute-start(f32[8,208,128]{2,1,0:T(8,128)} %get-tuple-element.74), channel_id=1, source_target_pairs={{0,1},{1,0},{2,3},{3,2},{4,5},{5,4},{6,7},{7,6},{8,9},{9,8},{10,11... | collective-permute-start | bytes 2555912 | tf_op jit(solution)/shard_map/ppermute | solution.py:630
  24.5 12.3 %collective-permute-start.1 = (f32[4,192,128]{2,1,0:T(8,128)S(1)}, f32[4,192,128]{2,1,0:T(8,128)S(1)}, u32[]{:S(2)}, u32[]{:S(2)}) collective-permute-start(f32[4,192,128]{2,1,0:T(8,128)S(1)} %get-tuple-element.130), channel_id=1, source_target_pairs={{0,2},{1,3},{2,0},{3,1},{4,6},{5,7},{6,4},{7,5},{8,10},{9,11},{10,... | collective-permute-start | bytes 1179656 | tf_op jit(solution)/shard_map/ppermute | solution.py:630
  27.5 11.2 %collective-permute-start.6 = (f32[4,192,128]{2,1,0:T(8,128)S(1)}, f32[4,192,128]{2,1,0:T(8,128)S(1)}, u32[]{:S(2)}, u32[]{:S(2)}) collective-permute-start(f32[4,192,128]{2,1,0:T(8,128)S(1)} %get-tuple-element.132), channel_id=1, source_target_pairs={{0,4},{1,5},{2,6},{3,7},{4,0},{5,1},{6,2},{7,3},{8,12},{9,13},{10,... | collective-permute-start | bytes 1179656 | tf_op jit(solution)/shard_map/ppermute | solution.py:630
  29.1 25.9 %copy-start.2 = (bf16[6,512,256]{2,1,0:T(8,128)(2,1)S(1)}, bf16[6,512,256]{2,1,0:T(8,128)(2,1)}, u32[]{:S(2)}) copy-start(bf16[6,512,256]{2,1,0:T(8,128)(2,1)} %refs_2_.1) | copy-start | bytes 4718596
  29.1 25.9 %copy-start.3 = (f32[1024,128]{1,0:T(8,128)S(1)}, f32[1024,128]{1,0:T(8,128)}, u32[]{:S(2)}) copy-start(f32[1024,128]{1,0:T(8,128)} %get-tuple-element.88.refs_0_) | copy-start | bytes 1572868
  29.1 25.9 %copy-start.4 = (bf16[1024,128]{1,0:T(8,128)(2,1)S(1)}, bf16[1024,128]{1,0:T(8,128)(2,1)}, u32[]{:S(2)}) copy-start(bf16[1024,128]{1,0:T(8,128)(2,1)} %get-tuple-element.89.refs_1_) | copy-start | bytes 786436
  29.2 11.4 %collective-permute-start.5 = (f32[4,208,128]{2,1,0:T(8,128)S(1)}, f32[4,208,128]{2,1,0:T(8,128)S(1)}, u32[]{:S(2)}, u32[]{:S(2)}) collective-permute-start(f32[4,208,128]{2,1,0:T(8,128)S(1)} %get-tuple-element.127), channel_id=1, source_target_pairs={{0,8},{1,9},{2,10},{3,11},{4,12},{5,13},{6,14},{7,15},{8,0},{9,1},... | collective-permute-start | bytes 1277960 | tf_op jit(solution)/shard_map/ppermute | solution.py:630
  36.8 18.2 %copy-start.1 = (bf16[6,1024,256]{2,1,0:T(8,128)(2,1)S(1)}, bf16[6,1024,256]{2,1,0:T(8,128)(2,1)}, u32[]{:S(2)}) copy-start(bf16[6,1024,256]{2,1,0:T(8,128)(2,1)} %get-tuple-element.91.refs_8_) | copy-start | bytes 9437188
  36.9 6.5 %collective-permute-start.4 = (f32[2,192,128]{2,1,0:T(8,128)S(1)}, f32[2,192,128]{2,1,0:T(8,128)S(1)}, u32[]{:S(2)}, u32[]{:S(2)}) collective-permute-start(f32[2,192,128]{2,1,0:T(8,128)S(1)} %get-tuple-element.136), channel_id=1, source_target_pairs={{0,4},{1,5},{2,6},{3,7},{4,0},{5,1},{6,2},{7,3},{8,12},{9,13},{10,... | collective-permute-start | bytes 589832 | tf_op jit(solution)/shard_map/ppermute | solution.py:630
  38.8 6.2 %collective-permute-start.9 = (f32[2,192,128]{2,1,0:T(8,128)S(1)}, f32[2,192,128]{2,1,0:T(8,128)S(1)}, u32[]{:S(2)}, u32[]{:S(2)}) collective-permute-start(f32[2,192,128]{2,1,0:T(8,128)S(1)} %get-tuple-element.138), channel_id=1, source_target_pairs={{0,8},{1,9},{2,10},{3,11},{4,12},{5,13},{6,14},{7,15},{8,0},{9,1},... | collective-permute-start | bytes 589832 | tf_op jit(solution)/shard_map/ppermute | solution.py:630
  40.6 14.4 %copy-start = (bf16[6,1024,256]{2,1,0:T(8,128)(2,1)S(1)}, bf16[6,1024,256]{2,1,0:T(8,128)(2,1)}, u32[]{:S(2)}) copy-start(bf16[6,1024,256]{2,1,0:T(8,128)(2,1)} %get-tuple-element.90.refs_7_) | copy-start | bytes 9437188
  40.7 14.4 %copy-start.5 = (bf16[2,512,4]{1,2,0:T(4,128)(2,1)S(1)}, bf16[2,512,4]{1,2,0:T(4,128)(2,1)}, u32[]{:S(2)}) copy-start(bf16[2,512,4]{1,2,0:T(4,128)(2,1)} %param.25) | copy-start | bytes 24580
  40.7 14.4 %copy-start.6 = (bf16[512,6]{0,1:T(8,128)(2,1)S(1)}, bf16[512,6]{0,1:T(8,128)(2,1)}, u32[]{:S(2)}) copy-start(bf16[512,6]{0,1:T(8,128)(2,1)} %param.27) | copy-start | bytes 18436
  40.7 6.8 %collective-permute-start.8 = (f32[2,208,128]{2,1,0:T(8,128)S(1)}, f32[2,208,128]{2,1,0:T(8,128)S(1)}, u32[]{:S(2)}, u32[]{:S(2)}) collective-permute-start(f32[2,208,128]{2,1,0:T(8,128)S(1)} %get-tuple-element.133), channel_id=1, source_target_pairs={{0,2},{1,3},{2,0},{3,1},{4,6},{5,7},{6,4},{7,5},{8,10},{9,11},{10,... | collective-permute-start | bytes 638984 | tf_op jit(solution)/shard_map/ppermute | solution.py:630
  43.4 6.3 %collective-permute-start.7 = (f32[1,192,128]{2,1,0:T(8,128)S(1)}, f32[1,192,128]{2,1,0:T(8,128)S(1)}, u32[]{:S(2)}, u32[]{:S(2)}) collective-permute-start(f32[1,192,128]{2,1,0:T(8,128)S(1)} %slice_add_fusion.16), channel_id=1, source_target_pairs={{0,8},{1,9},{2,10},{3,11},{4,12},{5,13},{6,14},{7,15},{8,0},{9,1},... | collective-permute-start | bytes 294920 | tf_op jit(solution)/shard_map/ppermute | solution.py:630
  45.0 4.7 %collective-permute-start.10 = (f32[1,192,128]{2,1,0:T(8,128)S(1)}, f32[1,192,128]{2,1,0:T(8,128)S(1)}, u32[]{:S(2)}, u32[]{:S(2)}) collective-permute-start(f32[1,192,128]{2,1,0:T(8,128)S(1)} %slice_add_fusion.15), channel_id=1, source_target_pairs={{0,2},{1,3},{2,0},{3,1},{4,6},{5,7},{6,4},{7,5},{8,10},{9,11},{10,... | collective-permute-start | bytes 294920 | tf_op jit(solution)/shard_map/ppermute | solution.py:630
  47.5 4.8 %collective-permute-start.11 = (f32[1,208,128]{2,1,0:T(8,128)S(1)}, f32[1,208,128]{2,1,0:T(8,128)S(1)}, u32[]{:S(2)}, u32[]{:S(2)}) collective-permute-start(f32[1,208,128]{2,1,0:T(8,128)S(1)} %slice_add_fusion.13), channel_id=1, source_target_pairs={{0,4},{1,5},{2,6},{3,7},{4,0},{5,1},{6,2},{7,3},{8,12},{9,13},{10,... | collective-permute-start | bytes 319496 | tf_op jit(solution)/shard_map/ppermute | solution.py:630
  52.3 12.5 %collective-permute-start.12 = (f32[1,592,128]{2,1,0:T(8,128)S(1)}, f32[1,592,128]{2,1,0:T(8,128)S(1)}, u32[]{:S(2)}, u32[]{:S(2)}) collective-permute-start(f32[1,592,128]{2,1,0:T(8,128)S(1)} %pad_maximum_fusion.6), channel_id=1, source_target_pairs={{0,16},{1,17},{2,18},{3,19},{4,20},{5,21},{6,22},{7,23},{8,24},{9,... | collective-permute-start | bytes 909320 | tf_op jit(solution)/shard_map/ppermute | solution.py:630
  64.9 4.7 %collective-permute-start.15 = (f32[1,192,128]{2,1,0:T(8,128)S(1)}, f32[1,192,128]{2,1,0:T(8,128)S(1)}, u32[]{:S(2)}, u32[]{:S(2)}) collective-permute-start(f32[1,192,128]{2,1,0:T(8,128)S(1)} %get-tuple-element.139), channel_id=1, source_target_pairs={{0,8},{1,9},{2,10},{3,11},{4,12},{5,13},{6,14},{7,15},{8,0},{9,1},... | collective-permute-start | bytes 294920 | tf_op jit(solution)/shard_map/ppermute | solution.py:630
  65.5 5.5 %collective-permute-start.14 = (f32[1,192,128]{2,1,0:T(8,128)S(1)}, f32[1,192,128]{2,1,0:T(8,128)S(1)}, u32[]{:S(2)}, u32[]{:S(2)}) collective-permute-start(f32[1,192,128]{2,1,0:T(8,128)S(1)} %get-tuple-element.140), channel_id=1, source_target_pairs={{0,2},{1,3},{2,0},{3,1},{4,6},{5,7},{6,4},{7,5},{8,10},{9,11},{10,... | collective-permute-start | bytes 294920 | tf_op jit(solution)/shard_map/ppermute | solution.py:630
  66.5 5.8 %collective-permute-start.13 = (f32[1,208,128]{2,1,0:T(8,128)S(1)}, f32[1,208,128]{2,1,0:T(8,128)S(1)}, u32[]{:S(2)}, u32[]{:S(2)}) collective-permute-start(f32[1,208,128]{2,1,0:T(8,128)S(1)} %slice.170), channel_id=1, source_target_pairs={{0,4},{1,5},{2,6},{3,7},{4,0},{5,1},{6,2},{7,3},{8,12},{9,13},{10,... | collective-permute-start | bytes 319496 | tf_op jit(solution)/shard_map/ppermute | solution.py:630
  69.6 5.7 %collective-permute-start.18 = (f32[2,192,128]{2,1,0:T(8,128)S(1)}, f32[2,192,128]{2,1,0:T(8,128)S(1)}, u32[]{:S(2)}, u32[]{:S(2)}) collective-permute-start(f32[2,192,128]{2,1,0:T(8,128)S(1)} %pad_maximum_fusion.8), channel_id=1, source_target_pairs={{0,4},{1,5},{2,6},{3,7},{4,0},{5,1},{6,2},{7,3},{8,12},{9,13},{10,... | collective-permute-start | bytes 589832 | tf_op jit(solution)/shard_map/ppermute | solution.py:630
  71.1 5.7 %collective-permute-start.17 = (f32[2,192,128]{2,1,0:T(8,128)S(1)}, f32[2,192,128]{2,1,0:T(8,128)S(1)}, u32[]{:S(2)}, u32[]{:S(2)}) collective-permute-start(f32[2,192,128]{2,1,0:T(8,128)S(1)} %pad_maximum_fusion.9), channel_id=1, source_target_pairs={{0,8},{1,9},{2,10},{3,11},{4,12},{5,13},{6,14},{7,15},{8,0},{9,1},... | collective-permute-start | bytes 589832 | tf_op jit(solution)/shard_map/ppermute | solution.py:630
  72.4 8.1 %collective-permute-start.16 = (f32[2,208,128]{2,1,0:T(8,128)S(1)}, f32[2,208,128]{2,1,0:T(8,128)S(1)}, u32[]{:S(2)}, u32[]{:S(2)}) collective-permute-start(f32[2,208,128]{2,1,0:T(8,128)S(1)} %pad_maximum_fusion.7), channel_id=1, source_target_pairs={{0,2},{1,3},{2,0},{3,1},{4,6},{5,7},{6,4},{7,5},{8,10},{9,11},{10,... | collective-permute-start | bytes 638984 | tf_op jit(solution)/shard_map/ppermute | solution.py:630
  75.3 11.1 %collective-permute-start.21 = (f32[4,192,128]{2,1,0:T(8,128)S(1)}, f32[4,192,128]{2,1,0:T(8,128)S(1)}, u32[]{:S(2)}, u32[]{:S(2)}) collective-permute-start(f32[4,192,128]{2,1,0:T(8,128)S(1)} %pad_maximum_fusion.4), channel_id=1, source_target_pairs={{0,2},{1,3},{2,0},{3,1},{4,6},{5,7},{6,4},{7,5},{8,10},{9,11},{10,... | collective-permute-start | bytes 1179656 | tf_op jit(solution)/shard_map/ppermute | solution.py:630
  76.9 9.6 %collective-permute-start.20 = (f32[4,192,128]{2,1,0:T(8,128)S(1)}, f32[4,192,128]{2,1,0:T(8,128)S(1)}, u32[]{:S(2)}, u32[]{:S(2)}) collective-permute-start(f32[4,192,128]{2,1,0:T(8,128)S(1)} %pad_maximum_fusion.5), channel_id=1, source_target_pairs={{0,4},{1,5},{2,6},{3,7},{4,0},{5,1},{6,2},{7,3},{8,12},{9,13},{10,... | collective-permute-start | bytes 1179656 | tf_op jit(solution)/shard_map/ppermute | solution.py:630
  80.5 8.2 %collective-permute-start.19 = (f32[4,208,128]{2,1,0:T(8,128)S(1)}, f32[4,208,128]{2,1,0:T(8,128)S(1)}, u32[]{:S(2)}, u32[]{:S(2)}) collective-permute-start(f32[4,208,128]{2,1,0:T(8,128)S(1)} %pad_maximum_fusion.3), channel_id=1, source_target_pairs={{0,8},{1,9},{2,10},{3,11},{4,12},{5,13},{6,14},{7,15},{8,0},{9,1},... | collective-permute-start | bytes 1277960 | tf_op jit(solution)/shard_map/ppermute | solution.py:630
  88.8 5.7 %collective-permute-start.22 = (f32[8,208,128]{2,1,0:T(8,128)S(1)}, f32[8,208,128]{2,1,0:T(8,128)S(1)}, u32[]{:S(2)}, u32[]{:S(2)}) collective-permute-start(f32[8,208,128]{2,1,0:T(8,128)S(1)} %pad_maximum_fusion.piece_ref.refs_0_), channel_id=1, source_target_pairs={{0,1},{1,0},{2,3},{3,2},{4,5},{5,4},{6,7},{7,6},{8,9},{9,8},{10,11... | collective-permute-start | bytes 2555912 | tf_op jit(solution)/shard_map/ppermute | solution.py:630
  88.9 3.5 %collective-permute-start.24 = (f32[8,192,128]{2,1,0:T(8,128)S(1)}, f32[8,192,128]{2,1,0:T(8,128)S(1)}, u32[]{:S(2)}, u32[]{:S(2)}) collective-permute-start(f32[8,192,128]{2,1,0:T(8,128)S(1)} %pad_maximum_fusion.1.piece_ref), channel_id=1, source_target_pairs={{0,1},{1,0},{2,3},{3,2},{4,5},{5,4},{6,7},{7,6},{8,9},{9,8},{10,11... | collective-permute-start | bytes 2359304 | tf_op jit(solution)/shard_map/ppermute | solution.py:630
  89.4 4.1 %collective-permute-start.23 = (f32[8,192,128]{2,1,0:T(8,128)S(1)}, f32[8,192,128]{2,1,0:T(8,128)S(1)}, u32[]{:S(2)}, u32[]{:S(2)}) collective-permute-start(f32[8,192,128]{2,1,0:T(8,128)S(1)} %pad_maximum_fusion.2.piece_ref), channel_id=1, source_target_pairs={{0,1},{1,0},{2,3},{3,2},{4,5},{5,4},{6,7},{7,6},{8,9},{9,8},{10,11... | collective-permute-start | bytes 2359304 | tf_op jit(solution)/shard_map/ppermute | solution.py:630
  (4 other events, 40.2 us)

commit v3 on v2

--- a/solution.py
+++ b/solution.py
@@ -18,9 +18,8 @@
 BOTH = ("wide", "narrow")
 SPANS = ((0, 2), (2, 4), (4, 6))
 FLIPS = {"c": 1, "x": 2, "y": 4, "1": 8, "2": 16}
-AXES = "xy1"
-ORDERS = ("xy1", "y1x", "1xy")
-HALVED = len(AXES)
+ORDERS = ("xy12", "y1x2", "1xy2")
+HALVED = 3
 BLOCKS = 2 << HALVED
 
 
@@ -190,21 +189,16 @@
     return dot(jnp.concatenate(hots, axis=1), jnp.concatenate(kept, axis=0))
 
 
-def device_bits(device):
+def device_bits(device, order):
     own = jnp.int32(0)
-    for axis in AXES:
+    for axis in order[:HALVED]:
         own = own * 2 + lax.bitwise_and(lax.div(device, FLIPS[axis]), 1)
     return lax.bitwise_and(device, 1), own
 
 
-def block_of(shard, order, core, own):
+def block_of(shard, core, own):
     count = BLOCKS // 2
-    flips = lax.bitwise_xor(own, shard % count)
-    q = jnp.int32(0)
-    for axis in order:
-        bit = lax.bitwise_and(lax.shift_right_logical(flips, HALVED - 1 - AXES.index(axis)), 1)
-        q = q * 2 + bit
-    return lax.bitwise_xor(core, shard // count) * count + q
+    return lax.bitwise_xor(core, shard // count) * count + lax.bitwise_xor(own, shard % count)
 
 
 def column_matrix(z, k, ref):
@@ -243,7 +237,7 @@
         copy.start()
         sent.append(copy)
 
-    core, own = device_bits(device_ref[0])
+    places = [device_bits(device_ref[0], order) for order in ORDERS]
     ids_ref, presence_ref, table_ref, gate_task_ref, gate_task_bias_ref = here[:5]
     gate_shared_ref, gate_shared_bias_ref, dense_ref, w_first_ref, b_first_ref = here[5:10]
     w_second_ref, b_second_ref, gain_ref, bias_ref, cot_ref = here[10:]
@@ -348,7 +342,7 @@
         line = (e - span[0]) * z.expert_rows
         lines = pl.ds(line, z.expert_rows)
         for shard in range(BLOCKS):
-            at = block_of(shard, ORDERS[index], core, own)
+            at = block_of(shard, *places[index])
             begin = line
             for v, count in ((first_total, z.first_rows), (second_total, z.second_rows)):
                 for h in range(z.halves):
@@ -387,7 +381,7 @@
     small_s[z.bias_at : z.bias_at + 1, :] = jnp.sum(logit_grad.astype(f32), axis=0, keepdims=True)
     lines = pl.ds((SPANS[-1][1] - SPANS[-1][0]) * z.expert_rows, z.small_rows)
     for shard in range(BLOCKS):
-        at = block_of(shard, ORDERS[-1], core, own)
+        at = block_of(shard, *places[-1])
         packed_s[-1][at, lines, :] = (
             small_s[shard * z.small_rows : (shard + 1) * z.small_rows, :] * grad_scale
         )
@@ -421,69 +415,105 @@
     dense_ref[...] = 0.5 * dense + dot(logit_ref[...], gates[:, : z.dense])
 
 
-def unpack_kernel(z, index, side, place_ref, device_ref, piece_ref, *refs):
-    last = index == len(SPANS) - 1 and side == 1
+def unpack_kernel(z, side, device_ref, *refs):
     refs = list(refs)
 
     def take(count):
         return [refs.pop(0) for _ in range(count)]
 
-    if last:
-        small_refs = take(2)
-    if index or side:
+    far_refs = take(2 * (len(SPANS) + side))
+    if side:
         take(2)
     w_first_ref, w_second_ref = take(2)
-    core, own = device_bits(device_ref[0])
+    small_outs = take(9 * side)
+    here = list(zip(far_refs[::2], far_refs[1::2]))
+    w_first_s, w_second_s, out_sems = take(3)
+    places = [device_bits(device_ref[0], order) for order in ORDERS]
+    core = places[0][0]
     count = BLOCKS // 2
-
-    def at(shard):
-        return lax.bitwise_and(block_of(shard, ORDERS[index], core, own), count - 1)
-
-    for shard in range(count):
-        block = at(shard)
-        line = 0
-        for ref, rows in ((w_first_ref, z.first_rows), (w_second_ref, z.second_rows)):
+    owner = lax.bitwise_xor(core, side)
+    sent = []
+
+    first = HALVED - 1
+    for parts, span, (_, own) in zip(here, SPANS, places):
+        bit = lax.bitwise_and(lax.shift_right_logical(own, first), 1)
+        for e in range(*span):
+            for half in range(2):
+
+                @pl.when(bit == half)
+                def _():
+                    for shard in range(count):
+                        part_ref = parts[(shard >> first & 1) ^ half]
+                        block = lax.bitwise_and(lax.bitwise_xor(own, shard), count // 2 - 1)
+                        line = (e - span[0]) * z.expert_rows
+                        for ref, rows in ((w_first_s, z.first_rows), (w_second_s, z.second_rows)):
+                            lines = slice(shard * rows, (shard + 1) * rows)
+                            for h in range(z.halves):
+                                ref[e, lines, h * LANES : (h + 1) * LANES] = part_ref[
+                                    block, line : line + rows, :
+                                ]
+                                line += rows
+
+            for ref, out_ref in ((w_first_s, w_first_ref), (w_second_s, w_second_ref)):
+                rows = ref.shape[1]
+                lines = pl.ds(pl.multiple_of(owner * rows, rows), rows)
+                copy = pltpu.make_async_copy(
+                    ref.at[e], out_ref.at[e, lines, :], out_sems.at[len(sent)]
+                )
+                copy.start()
+                sent.append(copy)
+
+    def finish():
+        for copy in sent:
+            copy.wait()
+
+    if not side:
+        finish()
+        return
+    table_ref, gate_task_ref, gate_task_bias_ref, gate_shared_ref, gate_shared_bias_ref = (
+        small_outs[:5]
+    )
+    sum_refs = small_outs[5:]
+    (small_s,) = take(1)
+
+    own = places[-1][1]
+    bit = lax.bitwise_and(lax.shift_right_logical(own, first), 1)
+    for half, parts in enumerate((here[-1], here[len(SPANS) - 1])):
+        start = lax.bitwise_xor(core, half) * (count * z.small_rows)
+        for side_bit in range(2):
+
+            @pl.when(bit == side_bit)
+            def _():
+                for shard in range(count):
+                    lines = pl.ds(pl.multiple_of(start + shard * z.small_rows, 8), z.small_rows)
+                    part_ref = parts[(shard >> first & 1) ^ side_bit]
+                    block = lax.bitwise_and(lax.bitwise_xor(own, shard), count // 2 - 1)
+                    small_s[lines, :] = part_ref[block, part_ref.shape[1] - z.small_rows :, :]
+
+    for low in range(z.low):
+        table_ref[:, low * z.high : (low + 1) * z.high] = small_s[
+            low * z.emb : (low + 1) * z.emb, :
+        ]
+    for q in range(z.d_in // LANES):
+        line = z.gate_at + q * 16
+        lanes = slice(q * LANES, (q + 1) * LANES)
+        for k in range(z.tasks):
+            gate_task_ref[k, :, lanes] = small_s[
+                line + k * z.gate : line + (k + 1) * z.gate, :
+            ]
+        gate_shared_ref[:, lanes] = small_s[line + z.tasks * z.gate : line + z.width, :]
+    bias_row = small_s[z.bias_at : z.bias_at + 1, :]
+    for k in range(z.tasks):
+        gate_task_bias_ref[k : k + 1, :] = bias_row[:, k * z.gate : (k + 1) * z.gate]
+    gate_shared_bias_ref[...] = bias_row[:, z.tasks * z.gate : z.width]
+    for e in range(z.experts):
+        for q in range(4):
             for h in range(z.halves):
-                ref[0, shard * rows : (shard + 1) * rows, h * LANES : (h + 1) * LANES] = (
-                    piece_ref[block, line : line + rows, :]
-                )
-                line += rows
-    if not last:
-        return
-    table_ref, gate_task_ref, gate_task_bias_ref, gate_shared_ref, gate_shared_bias_ref = take(5)
-    sum_refs = take(4)
-    (small_s,) = take(1)
-
-    @pl.when(pl.program_id(0) == 0)
-    def _():
-        for half, from_ref in enumerate(small_refs):
-            start = lax.bitwise_xor(core, half) * (count * z.small_rows)
-            for shard in range(count):
-                lines = pl.ds(pl.multiple_of(start + shard * z.small_rows, 8), z.small_rows)
-                small_s[lines, :] = from_ref[at(shard)]
-        for low in range(z.low):
-            table_ref[:, low * z.high : (low + 1) * z.high] = small_s[
-                low * z.emb : (low + 1) * z.emb, :
-            ]
-        for q in range(z.d_in // LANES):
-            line = z.gate_at + q * 16
-            lanes = slice(q * LANES, (q + 1) * LANES)
-            for k in range(z.tasks):
-                gate_task_ref[k, :, lanes] = small_s[
-                    line + k * z.gate : line + (k + 1) * z.gate, :
+                line = z.sums_at + e * z.sum_rows + q * z.halves + h
+                sum_refs[q][e : e + 1, h * LANES : (h + 1) * LANES] = small_s[
+                    line : line + 1, :
                 ]
-            gate_shared_ref[:, lanes] = small_s[line + z.tasks * z.gate : line + z.width, :]
-        bias_row = small_s[z.bias_at : z.bias_at + 1, :]
-        for k in range(z.tasks):
-            gate_task_bias_ref[k : k + 1, :] = bias_row[:, k * z.gate : (k + 1) * z.gate]
-        gate_shared_bias_ref[...] = bias_row[:, z.tasks * z.gate : z.width]
-        for e in range(z.experts):
-            for q in range(4):
-                for h in range(z.halves):
-                    line = z.sums_at + e * z.sum_rows + q * z.halves + h
-                    sum_refs[q][e : e + 1, h * LANES : (h + 1) * LANES] = small_s[
-                        line : line + 1, :
-                    ]
+    finish()
 
 
 SMEM = pl.BlockSpec(memory_space=pltpu.SMEM)
@@ -566,36 +596,20 @@
     )(weights, logit_grad, w_first, gain, bias, *gates, normed, firsts)
 
 
-def run_unpack(z, index, side, device, pieces, earlier):
-    last = index == len(SPANS) - 1 and side == 1
-    lo, hi = SPANS[index]
-    half = BLOCKS // 2
+def run_unpack(z, side, device, near, far, earlier):
     out_shape = [
         shape_of((z.experts, z.d_in, z.hidden)),
         shape_of((z.experts, z.hidden, z.out)),
     ]
-
-    def half_spec(array):
-        shape = (1, array.shape[1] // 2, array.shape[2])
-        return pl.BlockSpec(shape, lambda at, place: (lo + at, lax.bitwise_xor(place[0], side), 0))
-
-    def fixed(array):
-        return pl.BlockSpec(array.shape, lambda at, place: (0,) * len(array.shape))
-
-    out_specs = [half_spec(v) for v in out_shape]
-    operands = [pieces[side]]
-    in_specs = [SMEM, pl.BlockSpec((half, z.expert_rows, LANES), lambda at, place: (0, at, 0))]
-    scratch = []
-    if last:
-        start = (hi - lo) * z.expert_rows // z.small_rows
-        operands += list(pieces)
-        in_specs += [
-            pl.BlockSpec((half, z.small_rows, LANES), lambda at, place: (0, start, 0))
-        ] * 2
-    aliases = {2 + len(operands): 0, 3 + len(operands): 1} if earlier else {}
-    operands += list(earlier)
-    in_specs += [ANY] * len(earlier)
-    if last:
+    halves = [pltpu.VMEM((v.shape[0], v.shape[1] // 2, v.shape[2]), f32) for v in out_shape]
+    out_specs = [ANY] * 2
+    pieces = list(far if side else near)
+    if side:
+        pieces.append(near[-1])
+    operands = [v for piece in pieces for v in piece]
+    aliases = {}
+    if side:
+        aliases = {1 + len(operands): 0, 2 + len(operands): 1}
         small = [
             shape_of((z.emb, z.vocab)),
             shape_of((z.tasks, z.gate, z.d_in)),
@@ -604,24 +618,25 @@
             shape_of((1, z.experts)),
         ] + [shape_of((z.experts, z.out))] * 4
         out_shape += small
-        out_specs += [fixed(v) for v in small]
-        scratch = [pltpu.VMEM((z.small_rows * BLOCKS, LANES), f32)]
-    core = lax.bitwise_and(device, 1)
+        out_specs += [pl.BlockSpec(memory_space=pltpu.VMEM)] * len(small)
+    vmem = pl.BlockSpec(memory_space=pltpu.VMEM)
+    in_specs = [SMEM] + [vmem] * len(operands) + [ANY] * len(earlier)
+    scratch = halves
+    scratch += [pltpu.SemaphoreType.DMA((2 * z.experts,))]
+    if side:
+        scratch += [pltpu.VMEM((z.small_rows * BLOCKS, LANES), f32)]
+    operands += list(earlier)
     return pl.pallas_call(
-        functools.partial(unpack_kernel, z, index, side),
-        grid_spec=pltpu.PrefetchScalarGridSpec(
-            num_scalar_prefetch=1,
-            grid=(hi - lo,),
-            in_specs=in_specs,
-            out_specs=out_specs,
-            scratch_shapes=scratch,
-        ),
+        functools.partial(unpack_kernel, z, side),
+        in_specs=in_specs,
+        out_specs=out_specs,
         out_shape=out_shape,
+        scratch_shapes=scratch,
         input_output_aliases=aliases,
         compiler_params=pltpu.CompilerParams(vmem_limit_bytes=24 * MIB),
         cost_estimate=pl.CostEstimate(flops=0, bytes_accessed=4 * MIB, transcendentals=0),
-        name="unpack_%d_%d" % (index, side),
-    )(core, device, *operands)
+        name="unpack_%d" % side,
+    )(device, *operands)
 
 
 def exchange(value, axis):
@@ -634,7 +649,7 @@
     return lax.optimization_barrier((value, other))[0]
 
 
-def sum_pieces(near, far, outputs, unpack):
+def sum_pieces(near, far, outputs):
     count = len(near)
     got = [exchange(v, "c") for v in far]
     sent = None
@@ -648,31 +663,29 @@
             sent = high
     for i in range(count):
         near[i] = near[i] + after(got[i], sent)
-    rows = [v.shape[1] for v in near]
-    joined = jnp.concatenate(near, axis=1)
-    results = outputs(joined)
-    joined = joined + after(exchange(joined, "2"), results[0])
-    near = []
-    for i in range(count):
-        near.append(joined[:, sum(rows[:i]) : sum(rows[: i + 1])])
+        got[i] = exchange(near[i], ORDERS[i][HALVED])
+        sent = near[i]
+    results = outputs(sent)
+    sent = results[0]
+    early = []
     for step in reversed(range(HALVED)):
         for i in range(count):
             if step < HALVED - 1:
                 near[i] = jnp.concatenate([near[i], after(got[i], sent)], axis=0)
+            else:
+                near[i] = near[i] + after(got[i], sent)
             got[i] = exchange(near[i], ORDERS[i][step])
             sent = near[i]
-    far = []
-    grads = ()
+            if step == 0:
+                early.append(exchange(near[i], "c"))
+    near_parts, far_parts = [], []
     for i in range(count):
-        near[i] = jnp.concatenate([near[i], after(got[i], sent)], axis=0)
-        if i:
-            near[i] = after(near[i], grads[0])
-        sent = near[i]
-        far.append(exchange(near[i], "c"))
-        grads = unpack(i, 0, near[i], None, grads)
-    for i in range(count):
-        grads = unpack(i, 1, near[i], far[i], grads)
-    return grads, results
+        found = after(got[i], sent)
+        sent = found
+        near_parts.append((near[i], found))
+        far_parts.append((early[i], exchange(found, "c")))
+    near, far = near_parts, far_parts
+    return near, far, results
 
 
 def local(
@@ -734,18 +747,15 @@
             z, first, logit_grad, w_first, ln_gain, ln_bias, gates, normed, firsts
         )
 
-    def unpack(index, side, near, far, earlier):
-        return run_unpack(z, index, side, device, (near, far), earlier)
-
     if fits:
-        grads, results = sum_pieces(near, far, outputs, unpack)
+        near, far, results = sum_pieces(near, far, outputs)
     else:
         results = outputs(None)
         near, far = lax.psum((near, far), BOTH)
-        grads = ()
-        for side in range(2):
-            for index in range(len(SPANS)):
-                grads = unpack(index, side, near[index], far[index], grads)
+        half = BLOCKS // 4
+        near, far = [[(v[:half], v[half:]) for v in side] for side in (near, far)]
+    grads = run_unpack(z, 0, device, near, far, ())
+    grads = run_unpack(z, 1, device, near, far, grads)
     mixed, dense_grad = results
     w_first_grad, w_second_grad, table_grad = grads[:3]
     gate_task_grad, gate_task_bias_grad, gate_shared_grad, gate_shared_bias_grad = grads[3:7]

time: 96.1 us -> 90.7 us (0.944)
  waiting for transfers between devices: 32 us -> 25.2 us
  starting transfers between devices: 29.3 us -> 33.6 us
  Pallas kernels: 31.6 us -> 28.9 us
    ppermute x25 -> x30, waiting for transfers between devices: 32 us -> 25.2 us  [exchange(): return lax.ppermute(value, BOTH, [(i, i ^ flip) for i in range(count)])]
    ppermute x25 -> x30, starting transfers between devices: 29.3 us -> 33.6 us  [exchange(): return lax.ppermute(value, BOTH, [(i, i ^ flip) for i in range(count)])]
    pallas_call x6 -> x2, Pallas kernels: 6.39 us -> 3.69 us  [run_unpack(): pl.pallas_call(functools.partial(unpack_kernel, z, side), in_specs=in_spe...]
  transfers between devices with their start and end apart: 25 -> 30, of which waited for: 16 -> 15; matrix products, arithmetic and copies ran while one was open for 2% -> 2% of each run, Pallas kernels for 11% -> 7%
where the time goes in v3:
time: 90.7 us; the launch traced here: 90.6 us
  starting transfers between devices  33.6 us (37%)
  Pallas kernels  28.9 us (32%)
  waiting for transfers between devices  25.2 us (28%)
  other arithmetic  1.82 us (2%)
  between operations  1.01 us (1%)
    ppermute x30, starting transfers between devices, exchange(): return lax.ppermute(value, BOTH, [(i, i ^ flip) for i in range(count)])  33.6 us
    ppermute x30, waiting for transfers between devices, exchange(): return lax.ppermute(value, BOTH, [(i, i ^ flip) for i in range(count)])  25.2 us
    pallas_call x1, Pallas kernels, run_main(): pl.pallas_call(functools.partial(main_kernel, z, grad_scale), in_specs=[S...  20 us
    pallas_call x1, Pallas kernels, run_outputs(): pl.pallas_call(functools.partial(outputs_kernel, z), grid=(z.rows // bloc...  5.2 us
    pallas_call x2, Pallas kernels, run_unpack(): pl.pallas_call(functools.partial(unpack_kernel, z, side), in_specs=in_spe...  3.69 us
  transfers between devices with their start and end apart: 30, of which 15 were waited for; matrix products, arithmetic and copies ran while one was open for 2% of the time, Pallas kernels for 7%

profile of v3, /device:TPU:0, one launch (start us, length us, event | category | flops | bytes accessed | tf_op | source)
XLA Modules:
  0.0 90.6 jit_solution(11227639813513294702)
XLA Ops:
  0.7 20.0 %experts.1 = (f32[8,192,128]{2,1,0:T(8,128)}, f32[8,192,128]{2,1,0:T(8,128)}, f32[8,192,128]{2,1,0:T(8,128)}, f32[8,192,128]{2,1,0:T(8,128)}, f32[8,208,128]{2,1...) custom-call(s32[1]{0:T(128)} %bitcast.refs_0_.device_ref, ...), custom_call_target="tpu_custom_call" | custom-call | flops 7247757312 | bytes 20971520 | tf_op jit(solution)/shard_map/experts/pallas_call | solution.py:562
  21.7 1.6 %collective-permute-done.2 = f32[8,192,128]{2,1,0:T(8,128)S(1)} collective-permute-done((f32[8,192,128]{2,1,0:T(8,128)}, f32[8,192,128]{2,1,0:T(8,128)S(1)}, u32[]{:S(2)}, u32[]{:S(2)}) %collective-permute-start.2) | collective-permute-done | bytes 786464 | tf_op jit(solution)/shard_map/ppermute | solution.py:645
  23.3 1.2 %slice_add_fusion.2 = (f32[4,192,128]{2,1,0:T(8,128)S(1)}, f32[4,192,128]{2,1,0:T(8,128)S(1)}) fusion(f32[8,192,128]{2,1,0:T(8,128)S(1)} %collective-permute-done.2, f32[8,192,128]{2,1,0:T(8,128)} %get-tuple-element.67), kind=kLoop, calls=%fused_computation.3 | loop fusion | flops 196608 | bytes 2359296 | tf_op jit(solution)/shard_map/add | solution.py:660
  24.5 2.9 %collective-permute-start.5 = (f32[4,192,128]{2,1,0:T(8,128)S(1)}, f32[4,192,128]{2,1,0:T(8,128)S(1)}, u32[]{:S(2)}, u32[]{:S(2)}) collective-permute-start(f32[4,192,128]{2,1,0:T(8,128)S(1)} %get-tuple-element.114), channel_id=1, source_target_pairs={{0,2},{1,3},{2,0},{3,1},{4,6},{5,7},{6,4},{7,5},{8,10},{9,11},{10,... | collective-permute-start | bytes 1179656 | tf_op jit(solution)/shard_map/ppermute | solution.py:645
  27.5 1.6 %collective-permute-start.4 = (f32[4,192,128]{2,1,0:T(8,128)S(1)}, f32[4,192,128]{2,1,0:T(8,128)S(1)}, u32[]{:S(2)}, u32[]{:S(2)}) collective-permute-start(f32[4,192,128]{2,1,0:T(8,128)S(1)} %get-tuple-element.116), channel_id=1, source_target_pairs={{0,4},{1,5},{2,6},{3,7},{4,0},{5,1},{6,2},{7,3},{8,12},{9,13},{10,... | collective-permute-start | bytes 1179656 | tf_op jit(solution)/shard_map/ppermute | solution.py:645
  29.2 1.6 %collective-permute-start.3 = (f32[4,208,128]{2,1,0:T(8,128)S(1)}, f32[4,208,128]{2,1,0:T(8,128)S(1)}, u32[]{:S(2)}, u32[]{:S(2)}) collective-permute-start(f32[4,208,128]{2,1,0:T(8,128)S(1)} %get-tuple-element.111), channel_id=1, source_target_pairs={{0,8},{1,9},{2,10},{3,11},{4,12},{5,13},{6,14},{7,15},{8,0},{9,1},... | collective-permute-start | bytes 1277960 | tf_op jit(solution)/shard_map/ppermute | solution.py:645
  30.9 6.0 %collective-permute-done.5 = f32[4,192,128]{2,1,0:T(8,128)S(1)} collective-permute-done((f32[4,192,128]{2,1,0:T(8,128)S(1)}, f32[4,192,128]{2,1,0:T(8,128)S(1)}, u32[]{:S(2)}, u32[]{:S(2)}) %collective-permute-start.5) | collective-permute-done | bytes 393248 | tf_op jit(solution)/shard_map/ppermute | solution.py:645
  36.9 1.8 %collective-permute-start.8 = (f32[2,192,128]{2,1,0:T(8,128)S(1)}, f32[2,192,128]{2,1,0:T(8,128)S(1)}, u32[]{:S(2)}, u32[]{:S(2)}) collective-permute-start(f32[2,192,128]{2,1,0:T(8,128)S(1)} %get-tuple-element.120), channel_id=1, source_target_pairs={{0,4},{1,5},{2,6},{3,7},{4,0},{5,1},{6,2},{7,3},{8,12},{9,13},{10,... | collective-permute-start | bytes 589832 | tf_op jit(solution)/shard_map/ppermute | solution.py:645
  38.8 1.6 %collective-permute-start.7 = (f32[2,192,128]{2,1,0:T(8,128)S(1)}, f32[2,192,128]{2,1,0:T(8,128)S(1)}, u32[]{:S(2)}, u32[]{:S(2)}) collective-permute-start(f32[2,192,128]{2,1,0:T(8,128)S(1)} %get-tuple-element.122), channel_id=1, source_target_pairs={{0,8},{1,9},{2,10},{3,11},{4,12},{5,13},{6,14},{7,15},{8,0},{9,1},... | collective-permute-start | bytes 589832 | tf_op jit(solution)/shard_map/ppermute | solution.py:645
  40.7 1.4 %collective-permute-start.6 = (f32[2,208,128]{2,1,0:T(8,128)S(1)}, f32[2,208,128]{2,1,0:T(8,128)S(1)}, u32[]{:S(2)}, u32[]{:S(2)}) collective-permute-start(f32[2,208,128]{2,1,0:T(8,128)S(1)} %get-tuple-element.117), channel_id=1, source_target_pairs={{0,2},{1,3},{2,0},{3,1},{4,6},{5,7},{6,4},{7,5},{8,10},{9,11},{10,... | collective-permute-start | bytes 638984 | tf_op jit(solution)/shard_map/ppermute | solution.py:645
  42.1 1.3 %collective-permute-done.8 = f32[2,192,128]{2,1,0:T(8,128)S(1)} collective-permute-done((f32[2,192,128]{2,1,0:T(8,128)S(1)}, f32[2,192,128]{2,1,0:T(8,128)S(1)}, u32[]{:S(2)}, u32[]{:S(2)}) %collective-permute-start.8) | collective-permute-done | bytes 196640 | tf_op jit(solution)/shard_map/ppermute | solution.py:645
  43.4 1.6 %collective-permute-start.11 = (f32[1,192,128]{2,1,0:T(8,128)S(1)}, f32[1,192,128]{2,1,0:T(8,128)S(1)}, u32[]{:S(2)}, u32[]{:S(2)}) collective-permute-start(f32[1,192,128]{2,1,0:T(8,128)S(1)} %slice_add_fusion.16), channel_id=1, source_target_pairs={{0,8},{1,9},{2,10},{3,11},{4,12},{5,13},{6,14},{7,15},{8,0},{9,1},... | collective-permute-start | bytes 294920 | tf_op jit(solution)/shard_map/ppermute | solution.py:645
  45.0 1.6 %collective-permute-start.10 = (f32[1,192,128]{2,1,0:T(8,128)S(1)}, f32[1,192,128]{2,1,0:T(8,128)S(1)}, u32[]{:S(2)}, u32[]{:S(2)}) collective-permute-start(f32[1,192,128]{2,1,0:T(8,128)S(1)} %slice_add_fusion.17), channel_id=1, source_target_pairs={{0,2},{1,3},{2,0},{3,1},{4,6},{5,7},{6,4},{7,5},{8,10},{9,11},{10,... | collective-permute-start | bytes 294920 | tf_op jit(solution)/shard_map/ppermute | solution.py:645
  46.6 0.7 collective-permute-done.6
  47.3 0.9 collective-permute-start.9
  48.2 2.7 %collective-permute-start.12 = (f32[1,192,128]{2,1,0:T(8,128)S(1)}, f32[1,192,128]{2,1,0:T(8,128)S(1)}, u32[]{:S(2)}, u32[]{:S(2)}) collective-permute-start(f32[1,192,128]{2,1,0:T(8,128)S(1)} %fusion.1), channel_id=1, source_target_pairs={{0,16},{1,17},{2,18},{3,19},{4,20},{5,21},{6,22},{7,23},{8,24},{9,... | collective-permute-start | bytes 294920 | tf_op jit(solution)/shard_map/ppermute | solution.py:645
  50.9 1.6 %collective-permute-start.15 = (f32[1,192,128]{2,1,0:T(8,128)S(1)}, f32[1,192,128]{2,1,0:T(8,128)S(1)}, u32[]{:S(2)}, u32[]{:S(2)}) collective-permute-start(f32[1,192,128]{2,1,0:T(8,128)S(1)} %fusion.2), channel_id=1, source_target_pairs={{0,16},{1,17},{2,18},{3,19},{4,20},{5,21},{6,22},{7,23},{8,24},{9,... | collective-permute-start | bytes 294920 | tf_op jit(solution)/shard_map/ppermute | solution.py:645
  52.5 2.3 %collective-permute-start.14 = (f32[1,208,128]{2,1,0:T(8,128)S(1)}, f32[1,208,128]{2,1,0:T(8,128)S(1)}, u32[]{:S(2)}, u32[]{:S(2)}) collective-permute-start(f32[1,208,128]{2,1,0:T(8,128)S(1)} %fusion), channel_id=1, source_target_pairs={{0,16},{1,17},{2,18},{3,19},{4,20},{5,21},{6,22},{7,23},{8,24},{9,... | collective-permute-start | bytes 319496 | tf_op jit(solution)/shard_map/ppermute | solution.py:645
  54.8 5.2 %outputs.1 = (bf16[3,1024,256]{2,1,0:T(8,128)(2,1)}, f32[1024,384]{1,0:T(8,128)}) custom-call(f32[1024,128]{1,0:T(8,128)S(1)} %copy-done.3, bf16[1024,128]{1,0:T(8,128)(2,1)S(1)} %copy-done.4, bf16[6,512,256]{2,1,0:T(8,128)(2,1)S(1)} %copy-done.2, bf16[6,256]{1,0:T(8,128)(2,1)S(1)} %copy-done.7, bf16[6,256]{1,0:T(8,128)(2,1)S(1)} %copy-done.8, ...), custom_call_target="tpu_custom_call" | custom-call | flops 1207959552 | bytes 11534336 | tf_op jit(solution)/shard_map/outputs/pallas_call | solution.py:581
  60.4 1.5 %collective-permute-start.13 = (f32[1,192,128]{2,1,0:T(8,128)S(1)}, f32[1,192,128]{2,1,0:T(8,128)S(1)}, u32[]{:S(2)}, u32[]{:S(2)}) collective-permute-start(f32[1,192,128]{2,1,0:T(8,128)S(1)} %add.97), channel_id=1, source_target_pairs={{0,8},{1,9},{2,10},{3,11},{4,12},{5,13},{6,14},{7,15},{8,0},{9,1},... | collective-permute-start | bytes 294920 | tf_op jit(solution)/shard_map/ppermute | solution.py:645
  61.9 1.4 %collective-permute-start.18 = (f32[1,192,128]{2,1,0:T(8,128)S(1)}, f32[1,192,128]{2,1,0:T(8,128)S(1)}, u32[]{:S(2)}, u32[]{:S(2)}) collective-permute-start(f32[1,192,128]{2,1,0:T(8,128)S(1)} %add.98), channel_id=1, source_target_pairs={{0,2},{1,3},{2,0},{3,1},{4,6},{5,7},{6,4},{7,5},{8,10},{9,11},{10,... | collective-permute-start | bytes 294920 | tf_op jit(solution)/shard_map/ppermute | solution.py:645
  63.3 1.3 %collective-permute-start.17 = (f32[1,208,128]{2,1,0:T(8,128)S(1)}, f32[1,208,128]{2,1,0:T(8,128)S(1)}, u32[]{:S(2)}, u32[]{:S(2)}) collective-permute-start(f32[1,208,128]{2,1,0:T(8,128)S(1)} %add.99), channel_id=1, source_target_pairs={{0,4},{1,5},{2,6},{3,7},{4,0},{5,1},{6,2},{7,3},{8,12},{9,13},{10,... | collective-permute-start | bytes 319496 | tf_op jit(solution)/shard_map/ppermute | solution.py:645
  65.1 1.4 %collective-permute-start.16 = (f32[2,192,128]{2,1,0:T(8,128)S(1)}, f32[2,192,128]{2,1,0:T(8,128)S(1)}, u32[]{:S(2)}, u32[]{:S(2)}) collective-permute-start(f32[2,192,128]{2,1,0:T(8,128)S(1)} %pad_maximum_fusion.4), channel_id=1, source_target_pairs={{0,4},{1,5},{2,6},{3,7},{4,0},{5,1},{6,2},{7,3},{8,12},{9,13},{10,... | collective-permute-start | bytes 589832 | tf_op jit(solution)/shard_map/ppermute | solution.py:645
  67.2 1.9 %collective-permute-done.17 = f32[1,208,128]{2,1,0:T(8,128)S(1)} collective-permute-done((f32[1,208,128]{2,1,0:T(8,128)S(1)}, f32[1,208,128]{2,1,0:T(8,128)S(1)}, u32[]{:S(2)}, u32[]{:S(2)}) %collective-permute-start.17) | collective-permute-done | bytes 106528 | tf_op jit(solution)/shard_map/ppermute | solution.py:645
  69.2 1.1 %collective-permute-start.21 = (f32[2,208,128]{2,1,0:T(8,128)S(1)}, f32[2,208,128]{2,1,0:T(8,128)S(1)}, u32[]{:S(2)}, u32[]{:S(2)}) collective-permute-start(f32[2,208,128]{2,1,0:T(8,128)S(1)} %pad_maximum_fusion.3), channel_id=1, source_target_pairs={{0,2},{1,3},{2,0},{3,1},{4,6},{5,7},{6,4},{7,5},{8,10},{9,11},{10,... | collective-permute-start | bytes 638984 | tf_op jit(solution)/shard_map/ppermute | solution.py:645
  70.3 0.9 %collective-permute-done.16 = f32[2,192,128]{2,1,0:T(8,128)S(1)} collective-permute-done((f32[2,192,128]{2,1,0:T(8,128)S(1)}, f32[2,192,128]{2,1,0:T(8,128)S(1)}, u32[]{:S(2)}, u32[]{:S(2)}) %collective-permute-start.16) | collective-permute-done | bytes 196640 | tf_op jit(solution)/shard_map/ppermute | solution.py:645
  71.3 1.0 %collective-permute-done.22 = f32[2,192,128]{2,1,0:T(8,128)S(1)} collective-permute-done((f32[2,192,128]{2,1,0:T(8,128)S(1)}, f32[2,192,128]{2,1,0:T(8,128)S(1)}, u32[]{:S(2)}, u32[]{:S(2)}) %collective-permute-start.22) | collective-permute-done | bytes 196640 | tf_op jit(solution)/shard_map/ppermute | solution.py:645
  72.3 3.9 %collective-permute-done.21 = f32[2,208,128]{2,1,0:T(8,128)S(1)} collective-permute-done((f32[2,208,128]{2,1,0:T(8,128)S(1)}, f32[2,208,128]{2,1,0:T(8,128)S(1)}, u32[]{:S(2)}, u32[]{:S(2)}) %collective-permute-start.21) | collective-permute-done | bytes 213024 | tf_op jit(solution)/shard_map/ppermute | solution.py:645
  77.0 1.3 %collective-permute-start.25 = (f32[4,192,128]{2,1,0:T(8,128)S(1)}, f32[4,192,128]{2,1,0:T(8,128)S(1)}, u32[]{:S(2)}, u32[]{:S(2)}) collective-permute-start(f32[4,192,128]{2,1,0:T(8,128)S(1)} %pad_maximum_fusion.2.refs_2_), channel_id=1, source_target_pairs={{0,4},{1,5},{2,6},{3,7},{4,0},{5,1},{6,2},{7,3},{8,12},{9,13},{10,... | collective-permute-start | bytes 1179656 | tf_op jit(solution)/shard_map/ppermute | solution.py:645
  78.8 5.4 %collective-permute-done.20.refs_1_ = f32[4,192,128]{2,1,0:T(8,128)S(1)} collective-permute-done((f32[4,192,128]{2,1,0:T(8,128)S(1)}, f32[4,192,128]{2,1,0:T(8,128)S(1)}, u32[]{:S(2)}, u32[]{:S(2)}) %collective-permute-start.20) | collective-permute-done | bytes 393248 | tf_op jit(solution)/shard_map/ppermute | solution.py:645
  85.8 1.5 %unpack_0.1 = (f32[6,512,256]{2,1,0:T(8,128)}, f32[6,256,256]{2,1,0:T(8,128)}) custom-call(s32[1]{0:T(128)} %bitcast.refs_0_.device_ref, f32[4,192,128]{2,1,0:T(8,128)S(1)} %pad_maximum_fusion.1.refs_0_, f32[4,192,128]{2,1,0:T(8,128)S(1)} %collective-permute-done.20.refs_1_, f32[4,192,128]{2,1,0:T(8,128)S(1)} %pad_maximum_fusion.2.refs_2_, ...), custom_call_target="tpu_custom_call" | custom-call | bytes 4194304 | tf_op jit(solution)/shard_map/unpack_0/pallas_call | solution.py:629
  88.2 2.2 %unpack_1.1 = (f32[6,512,256]{2,1,0:T(8,128)}, f32[6,256,256]{2,1,0:T(8,128)}, f32[16,1024]{1,0:T(8,128)}, f32[2,4,512]{2,1,0:T(4,128)}, f32[2,4]{1,0:T(2,128)},...) custom-call(s32[1]{0:T(128)} %bitcast.refs_0_.device_ref, ...), custom_call_target="tpu_custom_call", output_to_operand_aliasing={{0}: (9, {}), {1}: (10, {})} | custom-call | bytes 4194304 | tf_op jit(solution)/shard_map/unpack_1/pallas_call | solution.py:629
  (75 shorter events, 7.2 us)
Async XLA Ops:
  20.6 2.6 %collective-permute-start.2 = (f32[8,192,128]{2,1,0:T(8,128)}, f32[8,192,128]{2,1,0:T(8,128)S(1)}, u32[]{:S(2)}, u32[]{:S(2)}) collective-permute-start(f32[8,192,128]{2,1,0:T(8,128)} %get-tuple-element.68), channel_id=1, source_target_pairs={{0,1},{1,0},{2,3},{3,2},{4,5},{5,4},{6,7},{7,6},{8,9},{9,8},{10,11... | collective-permute-start | bytes 2359304 | tf_op jit(solution)/shard_map/ppermute | solution.py:645
  21.2 6.3 %collective-permute-start.1 = (f32[8,192,128]{2,1,0:T(8,128)}, f32[8,192,128]{2,1,0:T(8,128)S(1)}, u32[]{:S(2)}, u32[]{:S(2)}) collective-permute-start(f32[8,192,128]{2,1,0:T(8,128)} %get-tuple-element.66), channel_id=1, source_target_pairs={{0,1},{1,0},{2,3},{3,2},{4,5},{5,4},{6,7},{7,6},{8,9},{9,8},{10,11... | collective-permute-start | bytes 2359304 | tf_op jit(solution)/shard_map/ppermute | solution.py:645
  21.2 7.9 %collective-permute-start = (f32[8,208,128]{2,1,0:T(8,128)}, f32[8,208,128]{2,1,0:T(8,128)S(1)}, u32[]{:S(2)}, u32[]{:S(2)}) collective-permute-start(f32[8,208,128]{2,1,0:T(8,128)} %get-tuple-element.64), channel_id=1, source_target_pairs={{0,1},{1,0},{2,3},{3,2},{4,5},{5,4},{6,7},{7,6},{8,9},{9,8},{10,11... | collective-permute-start | bytes 2555912 | tf_op jit(solution)/shard_map/ppermute | solution.py:645
  24.5 12.3 %collective-permute-start.5 = (f32[4,192,128]{2,1,0:T(8,128)S(1)}, f32[4,192,128]{2,1,0:T(8,128)S(1)}, u32[]{:S(2)}, u32[]{:S(2)}) collective-permute-start(f32[4,192,128]{2,1,0:T(8,128)S(1)} %get-tuple-element.114), channel_id=1, source_target_pairs={{0,2},{1,3},{2,0},{3,1},{4,6},{5,7},{6,4},{7,5},{8,10},{9,11},{10,... | collective-permute-start | bytes 1179656 | tf_op jit(solution)/shard_map/ppermute | solution.py:645
  27.5 27.3 %copy-start.3 = (f32[1024,128]{1,0:T(8,128)S(1)}, f32[1024,128]{1,0:T(8,128)}, u32[]{:S(2)}) copy-start(f32[1024,128]{1,0:T(8,128)} %get-tuple-element.80.refs_0_) | copy-start | bytes 1572868
  27.5 11.2 %collective-permute-start.4 = (f32[4,192,128]{2,1,0:T(8,128)S(1)}, f32[4,192,128]{2,1,0:T(8,128)S(1)}, u32[]{:S(2)}, u32[]{:S(2)}) collective-permute-start(f32[4,192,128]{2,1,0:T(8,128)S(1)} %get-tuple-element.116), channel_id=1, source_target_pairs={{0,4},{1,5},{2,6},{3,7},{4,0},{5,1},{6,2},{7,3},{8,12},{9,13},{10,... | collective-permute-start | bytes 1179656 | tf_op jit(solution)/shard_map/ppermute | solution.py:645
  29.1 25.6 %copy-start.1 = (bf16[6,1024,256]{2,1,0:T(8,128)(2,1)S(1)}, bf16[6,1024,256]{2,1,0:T(8,128)(2,1)}, u32[]{:S(2)}) copy-start(bf16[6,1024,256]{2,1,0:T(8,128)(2,1)} %get-tuple-element.83.refs_8_) | copy-start | bytes 9437188
  29.2 11.4 %collective-permute-start.3 = (f32[4,208,128]{2,1,0:T(8,128)S(1)}, f32[4,208,128]{2,1,0:T(8,128)S(1)}, u32[]{:S(2)}, u32[]{:S(2)}) collective-permute-start(f32[4,208,128]{2,1,0:T(8,128)S(1)} %get-tuple-element.111), channel_id=1, source_target_pairs={{0,8},{1,9},{2,10},{3,11},{4,12},{5,13},{6,14},{7,15},{8,0},{9,1},... | collective-permute-start | bytes 1277960 | tf_op jit(solution)/shard_map/ppermute | solution.py:645
  36.9 6.5 %collective-permute-start.8 = (f32[2,192,128]{2,1,0:T(8,128)S(1)}, f32[2,192,128]{2,1,0:T(8,128)S(1)}, u32[]{:S(2)}, u32[]{:S(2)}) collective-permute-start(f32[2,192,128]{2,1,0:T(8,128)S(1)} %get-tuple-element.120), channel_id=1, source_target_pairs={{0,4},{1,5},{2,6},{3,7},{4,0},{5,1},{6,2},{7,3},{8,12},{9,13},{10,... | collective-permute-start | bytes 589832 | tf_op jit(solution)/shard_map/ppermute | solution.py:645
  38.8 6.2 %collective-permute-start.7 = (f32[2,192,128]{2,1,0:T(8,128)S(1)}, f32[2,192,128]{2,1,0:T(8,128)S(1)}, u32[]{:S(2)}, u32[]{:S(2)}) collective-permute-start(f32[2,192,128]{2,1,0:T(8,128)S(1)} %get-tuple-element.122), channel_id=1, source_target_pairs={{0,8},{1,9},{2,10},{3,11},{4,12},{5,13},{6,14},{7,15},{8,0},{9,1},... | collective-permute-start | bytes 589832 | tf_op jit(solution)/shard_map/ppermute | solution.py:645
  40.7 6.6 %collective-permute-start.6 = (f32[2,208,128]{2,1,0:T(8,128)S(1)}, f32[2,208,128]{2,1,0:T(8,128)S(1)}, u32[]{:S(2)}, u32[]{:S(2)}) collective-permute-start(f32[2,208,128]{2,1,0:T(8,128)S(1)} %get-tuple-element.117), channel_id=1, source_target_pairs={{0,2},{1,3},{2,0},{3,1},{4,6},{5,7},{6,4},{7,5},{8,10},{9,11},{10,... | collective-permute-start | bytes 638984 | tf_op jit(solution)/shard_map/ppermute | solution.py:645
  43.4 4.8 %collective-permute-start.11 = (f32[1,192,128]{2,1,0:T(8,128)S(1)}, f32[1,192,128]{2,1,0:T(8,128)S(1)}, u32[]{:S(2)}, u32[]{:S(2)}) collective-permute-start(f32[1,192,128]{2,1,0:T(8,128)S(1)} %slice_add_fusion.16), channel_id=1, source_target_pairs={{0,8},{1,9},{2,10},{3,11},{4,12},{5,13},{6,14},{7,15},{8,0},{9,1},... | collective-permute-start | bytes 294920 | tf_op jit(solution)/shard_map/ppermute | solution.py:645
  45.0 5.8 %collective-permute-start.10 = (f32[1,192,128]{2,1,0:T(8,128)S(1)}, f32[1,192,128]{2,1,0:T(8,128)S(1)}, u32[]{:S(2)}, u32[]{:S(2)}) collective-permute-start(f32[1,192,128]{2,1,0:T(8,128)S(1)} %slice_add_fusion.17), channel_id=1, source_target_pairs={{0,2},{1,3},{2,0},{3,1},{4,6},{5,7},{6,4},{7,5},{8,10},{9,11},{10,... | collective-permute-start | bytes 294920 | tf_op jit(solution)/shard_map/ppermute | solution.py:645
  47.3 5.2 %collective-permute-start.9 = (f32[1,208,128]{2,1,0:T(8,128)S(1)}, f32[1,208,128]{2,1,0:T(8,128)S(1)}, u32[]{:S(2)}, u32[]{:S(2)}) collective-permute-start(f32[1,208,128]{2,1,0:T(8,128)S(1)} %slice_add_fusion.12), channel_id=1, source_target_pairs={{0,4},{1,5},{2,6},{3,7},{4,0},{5,1},{6,2},{7,3},{8,12},{9,13},{10,... | collective-permute-start | bytes 319496 | tf_op jit(solution)/shard_map/ppermute | solution.py:645
  48.2 12.1 %collective-permute-start.12 = (f32[1,192,128]{2,1,0:T(8,128)S(1)}, f32[1,192,128]{2,1,0:T(8,128)S(1)}, u32[]{:S(2)}, u32[]{:S(2)}) collective-permute-start(f32[1,192,128]{2,1,0:T(8,128)S(1)} %fusion.1), channel_id=1, source_target_pairs={{0,16},{1,17},{2,18},{3,19},{4,20},{5,21},{6,22},{7,23},{8,24},{9,... | collective-permute-start | bytes 294920 | tf_op jit(solution)/shard_map/ppermute | solution.py:645
  50.9 10.9 %collective-permute-start.15 = (f32[1,192,128]{2,1,0:T(8,128)S(1)}, f32[1,192,128]{2,1,0:T(8,128)S(1)}, u32[]{:S(2)}, u32[]{:S(2)}) collective-permute-start(f32[1,192,128]{2,1,0:T(8,128)S(1)} %fusion.2), channel_id=1, source_target_pairs={{0,16},{1,17},{2,18},{3,19},{4,20},{5,21},{6,22},{7,23},{8,24},{9,... | collective-permute-start | bytes 294920 | tf_op jit(solution)/shard_map/ppermute | solution.py:645
  52.5 10.8 %collective-permute-start.14 = (f32[1,208,128]{2,1,0:T(8,128)S(1)}, f32[1,208,128]{2,1,0:T(8,128)S(1)}, u32[]{:S(2)}, u32[]{:S(2)}) collective-permute-start(f32[1,208,128]{2,1,0:T(8,128)S(1)} %fusion), channel_id=1, source_target_pairs={{0,16},{1,17},{2,18},{3,19},{4,20},{5,21},{6,22},{7,23},{8,24},{9,... | collective-permute-start | bytes 319496 | tf_op jit(solution)/shard_map/ppermute | solution.py:645
  60.4 4.7 %collective-permute-start.13 = (f32[1,192,128]{2,1,0:T(8,128)S(1)}, f32[1,192,128]{2,1,0:T(8,128)S(1)}, u32[]{:S(2)}, u32[]{:S(2)}) collective-permute-start(f32[1,192,128]{2,1,0:T(8,128)S(1)} %add.97), channel_id=1, source_target_pairs={{0,8},{1,9},{2,10},{3,11},{4,12},{5,13},{6,14},{7,15},{8,0},{9,1},... | collective-permute-start | bytes 294920 | tf_op jit(solution)/shard_map/ppermute | solution.py:645
  61.9 4.7 %collective-permute-start.18 = (f32[1,192,128]{2,1,0:T(8,128)S(1)}, f32[1,192,128]{2,1,0:T(8,128)S(1)}, u32[]{:S(2)}, u32[]{:S(2)}) collective-permute-start(f32[1,192,128]{2,1,0:T(8,128)S(1)} %add.98), channel_id=1, source_target_pairs={{0,2},{1,3},{2,0},{3,1},{4,6},{5,7},{6,4},{7,5},{8,10},{9,11},{10,... | collective-permute-start | bytes 294920 | tf_op jit(solution)/shard_map/ppermute | solution.py:645
  63.3 5.8 %collective-permute-start.17 = (f32[1,208,128]{2,1,0:T(8,128)S(1)}, f32[1,208,128]{2,1,0:T(8,128)S(1)}, u32[]{:S(2)}, u32[]{:S(2)}) collective-permute-start(f32[1,208,128]{2,1,0:T(8,128)S(1)} %add.99), channel_id=1, source_target_pairs={{0,4},{1,5},{2,6},{3,7},{4,0},{5,1},{6,2},{7,3},{8,12},{9,13},{10,... | collective-permute-start | bytes 319496 | tf_op jit(solution)/shard_map/ppermute | solution.py:645
  65.1 6.2 %collective-permute-start.16 = (f32[2,192,128]{2,1,0:T(8,128)S(1)}, f32[2,192,128]{2,1,0:T(8,128)S(1)}, u32[]{:S(2)}, u32[]{:S(2)}) collective-permute-start(f32[2,192,128]{2,1,0:T(8,128)S(1)} %pad_maximum_fusion.4), channel_id=1, source_target_pairs={{0,4},{1,5},{2,6},{3,7},{4,0},{5,1},{6,2},{7,3},{8,12},{9,13},{10,... | collective-permute-start | bytes 589832 | tf_op jit(solution)/shard_map/ppermute | solution.py:645
  66.5 5.7 %collective-permute-start.22 = (f32[2,192,128]{2,1,0:T(8,128)S(1)}, f32[2,192,128]{2,1,0:T(8,128)S(1)}, u32[]{:S(2)}, u32[]{:S(2)}) collective-permute-start(f32[2,192,128]{2,1,0:T(8,128)S(1)} %pad_maximum_fusion.5), channel_id=1, source_target_pairs={{0,8},{1,9},{2,10},{3,11},{4,12},{5,13},{6,14},{7,15},{8,0},{9,1},... | collective-permute-start | bytes 589832 | tf_op jit(solution)/shard_map/ppermute | solution.py:645
  69.2 7.0 %collective-permute-start.21 = (f32[2,208,128]{2,1,0:T(8,128)S(1)}, f32[2,208,128]{2,1,0:T(8,128)S(1)}, u32[]{:S(2)}, u32[]{:S(2)}) collective-permute-start(f32[2,208,128]{2,1,0:T(8,128)S(1)} %pad_maximum_fusion.3), channel_id=1, source_target_pairs={{0,2},{1,3},{2,0},{3,1},{4,6},{5,7},{6,4},{7,5},{8,10},{9,11},{10,... | collective-permute-start | bytes 638984 | tf_op jit(solution)/shard_map/ppermute | solution.py:645
  76.2 8.5 %collective-permute-start.28 = (f32[4,208,128]{2,1,0:T(8,128)S(1)}, f32[4,208,128]{2,1,0:T(8,128)S(1)}, u32[]{:S(2)}, u32[]{:S(2)}) collective-permute-start(f32[4,208,128]{2,1,0:T(8,128)S(1)} %pad_maximum_fusion.refs_4_.refs_6_), channel_id=1, source_target_pairs={{0,8},{1,9},{2,10},{3,11},{4,12},{5,13},{6,14},{7,15},{8,0},{9,1},... | collective-permute-start | bytes 1277960 | tf_op jit(solution)/shard_map/ppermute | solution.py:645
  76.4 7.8 %collective-permute-start.20 = (f32[4,192,128]{2,1,0:T(8,128)S(1)}, f32[4,192,128]{2,1,0:T(8,128)S(1)}, u32[]{:S(2)}, u32[]{:S(2)}) collective-permute-start(f32[4,192,128]{2,1,0:T(8,128)S(1)} %pad_maximum_fusion.1.refs_0_), channel_id=1, source_target_pairs={{0,2},{1,3},{2,0},{3,1},{4,6},{5,7},{6,4},{7,5},{8,10},{9,11},{10,... | collective-permute-start | bytes 1179656 | tf_op jit(solution)/shard_map/ppermute | solution.py:645
  77.0 7.8 %collective-permute-start.25 = (f32[4,192,128]{2,1,0:T(8,128)S(1)}, f32[4,192,128]{2,1,0:T(8,128)S(1)}, u32[]{:S(2)}, u32[]{:S(2)}) collective-permute-start(f32[4,192,128]{2,1,0:T(8,128)S(1)} %pad_maximum_fusion.2.refs_2_), channel_id=1, source_target_pairs={{0,4},{1,5},{2,6},{3,7},{4,0},{5,1},{6,2},{7,3},{8,12},{9,13},{10,... | collective-permute-start | bytes 1179656 | tf_op jit(solution)/shard_map/ppermute | solution.py:645
  78.2 7.0 %collective-permute-start.24 = (f32[4,192,128]{2,1,0:T(8,128)S(1)}, f32[4,192,128]{2,1,0:T(8,128)S(1)}, u32[]{:S(2)}, u32[]{:S(2)}) collective-permute-start(f32[4,192,128]{2,1,0:T(8,128)S(1)} %pad_maximum_fusion.2.refs_2_), channel_id=1, source_target_pairs={{0,1},{1,0},{2,3},{3,2},{4,5},{5,4},{6,7},{7,6},{8,9},{9,8},{10,11... | collective-permute-start | bytes 1179656 | tf_op jit(solution)/shard_map/ppermute | solution.py:645
  78.2 9.1 %collective-permute-start.27 = (f32[4,208,128]{2,1,0:T(8,128)S(1)}, f32[4,208,128]{2,1,0:T(8,128)S(1)}, u32[]{:S(2)}, u32[]{:S(2)}) collective-permute-start(f32[4,208,128]{2,1,0:T(8,128)S(1)} %pad_maximum_fusion.refs_4_.refs_6_), channel_id=1, source_target_pairs={{0,1},{1,0},{2,3},{3,2},{4,5},{5,4},{6,7},{7,6},{8,9},{9,8},{10,11... | collective-permute-start | bytes 1277960 | tf_op jit(solution)/shard_map/ppermute | solution.py:645
  84.8 3.5 %collective-permute-start.29 = (f32[4,208,128]{2,1,0:T(8,128)S(1)}, f32[4,208,128]{2,1,0:T(8,128)S(1)}, u32[]{:S(2)}, u32[]{:S(2)}) collective-permute-start(f32[4,208,128]{2,1,0:T(8,128)S(1)} %collective-permute-done.28.refs_5_.refs_7_), channel_id=1, source_target_pairs={{0,1},{1,0},{2,3},{3,2},{4,5},{5,4},{6,7},{7,6},{8,9},{9,8},{10,11... | collective-permute-start | bytes 1277960 | tf_op jit(solution)/shard_map/ppermute | solution.py:645
  84.8 2.6 %collective-permute-start.19 = (f32[4,192,128]{2,1,0:T(8,128)S(1)}, f32[4,192,128]{2,1,0:T(8,128)S(1)}, u32[]{:S(2)}, u32[]{:S(2)}) collective-permute-start(f32[4,192,128]{2,1,0:T(8,128)S(1)} %pad_maximum_fusion.1.refs_0_), channel_id=1, source_target_pairs={{0,1},{1,0},{2,3},{3,2},{4,5},{5,4},{6,7},{7,6},{8,9},{9,8},{10,11... | collective-permute-start | bytes 1179656 | tf_op jit(solution)/shard_map/ppermute | solution.py:645
  85.3 2.4 %collective-permute-start.26 = (f32[4,192,128]{2,1,0:T(8,128)S(1)}, f32[4,192,128]{2,1,0:T(8,128)S(1)}, u32[]{:S(2)}, u32[]{:S(2)}) collective-permute-start(f32[4,192,128]{2,1,0:T(8,128)S(1)} %collective-permute-done.25.refs_3_), channel_id=1, source_target_pairs={{0,1},{1,0},{2,3},{3,2},{4,5},{5,4},{6,7},{7,6},{8,9},{9,8},{10,11... | collective-permute-start | bytes 1179656 | tf_op jit(solution)/shard_map/ppermute | solution.py:645
  85.3 2.9 %collective-permute-start.23 = (f32[4,192,128]{2,1,0:T(8,128)S(1)}, f32[4,192,128]{2,1,0:T(8,128)S(1)}, u32[]{:S(2)}, u32[]{:S(2)}) collective-permute-start(f32[4,192,128]{2,1,0:T(8,128)S(1)} %collective-permute-done.20.refs_1_), channel_id=1, source_target_pairs={{0,1},{1,0},{2,3},{3,2},{4,5},{5,4},{6,7},{7,6},{8,9},{9,8},{10,11... | collective-permute-start | bytes 1179656 | tf_op jit(solution)/shard_map/ppermute | solution.py:645
  (9 other events, 120.1 us)

commit v4 on v3

--- a/solution.py
+++ b/solution.py
@@ -576,7 +576,7 @@
 
 
 def run_outputs(z, weights, logit_grad, w_first, gain, bias, gates, normed, firsts):
-    block = z.rows // 4
+    block = z.rows // 2
     out_shape = [shape_of((z.tasks + 1, z.rows, z.out), bf16), shape_of((z.rows, z.dense))]
     return pl.pallas_call(
         functools.partial(outputs_kernel, z),

time: 90.7 us -> 90.7 us (level)
  no operation moved by 1% of the time
where the time goes in v4:
time: 90.7 us; the launch traced here: 90.6 us
  starting transfers between devices  33.8 us (37%)
  Pallas kernels  28.8 us (32%)
  waiting for transfers between devices  25.1 us (28%)
  other arithmetic  1.82 us (2%)
  between operations  1.01 us (1%)
    ppermute x30, starting transfers between devices, exchange(): return lax.ppermute(value, BOTH, [(i, i ^ flip) for i in range(count)])  33.8 us
    ppermute x30, waiting for transfers between devices, exchange(): return lax.ppermute(value, BOTH, [(i, i ^ flip) for i in range(count)])  25.1 us
    pallas_call x1, Pallas kernels, run_main(): pl.pallas_call(functools.partial(main_kernel, z, grad_scale), in_specs=[S...  20 us
    pallas_call x1, Pallas kernels, run_outputs(): pl.pallas_call(functools.partial(outputs_kernel, z), grid=(z.rows // bloc...  5.16 us
    pallas_call x2, Pallas kernels, run_unpack(): pl.pallas_call(functools.partial(unpack_kernel, z, side), in_specs=in_spe...  3.69 us
  transfers between devices with their start and end apart: 30, of which 15 were waited for; matrix products, arithmetic and copies ran while one was open for 2% of the time, Pallas kernels for 7%

profile of v4, /device:TPU:0, one launch (start us, length us, event | category | flops | bytes accessed | tf_op | source)
XLA Modules:
  0.0 90.6 jit_solution(13427111941652831355)
XLA Ops:
  0.7 20.0 %experts.1 = (f32[8,192,128]{2,1,0:T(8,128)}, f32[8,192,128]{2,1,0:T(8,128)}, f32[8,192,128]{2,1,0:T(8,128)}, f32[8,192,128]{2,1,0:T(8,128)}, f32[8,208,128]{2,1...) custom-call(s32[1]{0:T(128)} %bitcast.refs_0_.device_ref, ...), custom_call_target="tpu_custom_call" | custom-call | flops 7247757312 | bytes 20971520 | tf_op jit(solution)/shard_map/experts/pallas_call | solution.py:562
  21.7 1.6 %collective-permute-done.2 = f32[8,192,128]{2,1,0:T(8,128)S(1)} collective-permute-done((f32[8,192,128]{2,1,0:T(8,128)}, f32[8,192,128]{2,1,0:T(8,128)S(1)}, u32[]{:S(2)}, u32[]{:S(2)}) %collective-permute-start.2) | collective-permute-done | bytes 786464 | tf_op jit(solution)/shard_map/ppermute | solution.py:645
  23.3 1.2 %slice_add_fusion.2 = (f32[4,192,128]{2,1,0:T(8,128)S(1)}, f32[4,192,128]{2,1,0:T(8,128)S(1)}) fusion(f32[8,192,128]{2,1,0:T(8,128)S(1)} %collective-permute-done.2, f32[8,192,128]{2,1,0:T(8,128)} %get-tuple-element.67), kind=kLoop, calls=%fused_computation.3 | loop fusion | flops 196608 | bytes 2359296 | tf_op jit(solution)/shard_map/add | solution.py:660
  24.5 2.9 %collective-permute-start.5 = (f32[4,192,128]{2,1,0:T(8,128)S(1)}, f32[4,192,128]{2,1,0:T(8,128)S(1)}, u32[]{:S(2)}, u32[]{:S(2)}) collective-permute-start(f32[4,192,128]{2,1,0:T(8,128)S(1)} %get-tuple-element.114), channel_id=1, source_target_pairs={{0,2},{1,3},{2,0},{3,1},{4,6},{5,7},{6,4},{7,5},{8,10},{9,11},{10,... | collective-permute-start | bytes 1179656 | tf_op jit(solution)/shard_map/ppermute | solution.py:645
  27.5 1.6 %collective-permute-start.4 = (f32[4,192,128]{2,1,0:T(8,128)S(1)}, f32[4,192,128]{2,1,0:T(8,128)S(1)}, u32[]{:S(2)}, u32[]{:S(2)}) collective-permute-start(f32[4,192,128]{2,1,0:T(8,128)S(1)} %get-tuple-element.116), channel_id=1, source_target_pairs={{0,4},{1,5},{2,6},{3,7},{4,0},{5,1},{6,2},{7,3},{8,12},{9,13},{10,... | collective-permute-start | bytes 1179656 | tf_op jit(solution)/shard_map/ppermute | solution.py:645
  29.2 1.6 %collective-permute-start.3 = (f32[4,208,128]{2,1,0:T(8,128)S(1)}, f32[4,208,128]{2,1,0:T(8,128)S(1)}, u32[]{:S(2)}, u32[]{:S(2)}) collective-permute-start(f32[4,208,128]{2,1,0:T(8,128)S(1)} %get-tuple-element.111), channel_id=1, source_target_pairs={{0,8},{1,9},{2,10},{3,11},{4,12},{5,13},{6,14},{7,15},{8,0},{9,1},... | collective-permute-start | bytes 1277960 | tf_op jit(solution)/shard_map/ppermute | solution.py:645
  30.9 6.0 %collective-permute-done.5 = f32[4,192,128]{2,1,0:T(8,128)S(1)} collective-permute-done((f32[4,192,128]{2,1,0:T(8,128)S(1)}, f32[4,192,128]{2,1,0:T(8,128)S(1)}, u32[]{:S(2)}, u32[]{:S(2)}) %collective-permute-start.5) | collective-permute-done | bytes 393248 | tf_op jit(solution)/shard_map/ppermute | solution.py:645
  36.9 1.8 %collective-permute-start.8 = (f32[2,192,128]{2,1,0:T(8,128)S(1)}, f32[2,192,128]{2,1,0:T(8,128)S(1)}, u32[]{:S(2)}, u32[]{:S(2)}) collective-permute-start(f32[2,192,128]{2,1,0:T(8,128)S(1)} %get-tuple-element.120), channel_id=1, source_target_pairs={{0,4},{1,5},{2,6},{3,7},{4,0},{5,1},{6,2},{7,3},{8,12},{9,13},{10,... | collective-permute-start | bytes 589832 | tf_op jit(solution)/shard_map/ppermute | solution.py:645
  38.8 1.6 %collective-permute-start.7 = (f32[2,192,128]{2,1,0:T(8,128)S(1)}, f32[2,192,128]{2,1,0:T(8,128)S(1)}, u32[]{:S(2)}, u32[]{:S(2)}) collective-permute-start(f32[2,192,128]{2,1,0:T(8,128)S(1)} %get-tuple-element.122), channel_id=1, source_target_pairs={{0,8},{1,9},{2,10},{3,11},{4,12},{5,13},{6,14},{7,15},{8,0},{9,1},... | collective-permute-start | bytes 589832 | tf_op jit(solution)/shard_map/ppermute | solution.py:645
  40.7 1.4 %collective-permute-start.6 = (f32[2,208,128]{2,1,0:T(8,128)S(1)}, f32[2,208,128]{2,1,0:T(8,128)S(1)}, u32[]{:S(2)}, u32[]{:S(2)}) collective-permute-start(f32[2,208,128]{2,1,0:T(8,128)S(1)} %get-tuple-element.117), channel_id=1, source_target_pairs={{0,2},{1,3},{2,0},{3,1},{4,6},{5,7},{6,4},{7,5},{8,10},{9,11},{10,... | collective-permute-start | bytes 638984 | tf_op jit(solution)/shard_map/ppermute | solution.py:645
  42.1 1.3 %collective-permute-done.8 = f32[2,192,128]{2,1,0:T(8,128)S(1)} collective-permute-done((f32[2,192,128]{2,1,0:T(8,128)S(1)}, f32[2,192,128]{2,1,0:T(8,128)S(1)}, u32[]{:S(2)}, u32[]{:S(2)}) %collective-permute-start.8) | collective-permute-done | bytes 196640 | tf_op jit(solution)/shard_map/ppermute | solution.py:645
  43.4 1.6 %collective-permute-start.11 = (f32[1,192,128]{2,1,0:T(8,128)S(1)}, f32[1,192,128]{2,1,0:T(8,128)S(1)}, u32[]{:S(2)}, u32[]{:S(2)}) collective-permute-start(f32[1,192,128]{2,1,0:T(8,128)S(1)} %slice_add_fusion.16), channel_id=1, source_target_pairs={{0,8},{1,9},{2,10},{3,11},{4,12},{5,13},{6,14},{7,15},{8,0},{9,1},... | collective-permute-start | bytes 294920 | tf_op jit(solution)/shard_map/ppermute | solution.py:645
  45.0 1.6 %collective-permute-start.10 = (f32[1,192,128]{2,1,0:T(8,128)S(1)}, f32[1,192,128]{2,1,0:T(8,128)S(1)}, u32[]{:S(2)}, u32[]{:S(2)}) collective-permute-start(f32[1,192,128]{2,1,0:T(8,128)S(1)} %slice_add_fusion.17), channel_id=1, source_target_pairs={{0,2},{1,3},{2,0},{3,1},{4,6},{5,7},{6,4},{7,5},{8,10},{9,11},{10,... | collective-permute-start | bytes 294920 | tf_op jit(solution)/shard_map/ppermute | solution.py:645
  47.3 0.9 collective-permute-start.9
  48.2 2.7 %collective-permute-start.12 = (f32[1,192,128]{2,1,0:T(8,128)S(1)}, f32[1,192,128]{2,1,0:T(8,128)S(1)}, u32[]{:S(2)}, u32[]{:S(2)}) collective-permute-start(f32[1,192,128]{2,1,0:T(8,128)S(1)} %fusion.1), channel_id=1, source_target_pairs={{0,16},{1,17},{2,18},{3,19},{4,20},{5,21},{6,22},{7,23},{8,24},{9,... | collective-permute-start | bytes 294920 | tf_op jit(solution)/shard_map/ppermute | solution.py:645
  50.9 1.6 %collective-permute-start.15 = (f32[1,192,128]{2,1,0:T(8,128)S(1)}, f32[1,192,128]{2,1,0:T(8,128)S(1)}, u32[]{:S(2)}, u32[]{:S(2)}) collective-permute-start(f32[1,192,128]{2,1,0:T(8,128)S(1)} %fusion.2), channel_id=1, source_target_pairs={{0,16},{1,17},{2,18},{3,19},{4,20},{5,21},{6,22},{7,23},{8,24},{9,... | collective-permute-start | bytes 294920 | tf_op jit(solution)/shard_map/ppermute | solution.py:645
  52.5 2.3 %collective-permute-start.14 = (f32[1,208,128]{2,1,0:T(8,128)S(1)}, f32[1,208,128]{2,1,0:T(8,128)S(1)}, u32[]{:S(2)}, u32[]{:S(2)}) collective-permute-start(f32[1,208,128]{2,1,0:T(8,128)S(1)} %fusion), channel_id=1, source_target_pairs={{0,16},{1,17},{2,18},{3,19},{4,20},{5,21},{6,22},{7,23},{8,24},{9,... | collective-permute-start | bytes 319496 | tf_op jit(solution)/shard_map/ppermute | solution.py:645
  54.8 5.2 %outputs.1 = (bf16[3,1024,256]{2,1,0:T(8,128)(2,1)}, f32[1024,384]{1,0:T(8,128)}) custom-call(f32[1024,128]{1,0:T(8,128)S(1)} %copy-done.3, bf16[1024,128]{1,0:T(8,128)(2,1)S(1)} %copy-done.4, bf16[6,512,256]{2,1,0:T(8,128)(2,1)S(1)} %copy-done.2, bf16[6,256]{1,0:T(8,128)(2,1)S(1)} %copy-done.7, bf16[6,256]{1,0:T(8,128)(2,1)S(1)} %copy-done.8, ...), custom_call_target="tpu_custom_call" | custom-call | flops 1207959552 | bytes 11534336 | tf_op jit(solution)/shard_map/outputs/pallas_call | solution.py:581
  60.4 1.4 %collective-permute-start.13 = (f32[1,192,128]{2,1,0:T(8,128)S(1)}, f32[1,192,128]{2,1,0:T(8,128)S(1)}, u32[]{:S(2)}, u32[]{:S(2)}) collective-permute-start(f32[1,192,128]{2,1,0:T(8,128)S(1)} %add.97), channel_id=1, source_target_pairs={{0,8},{1,9},{2,10},{3,11},{4,12},{5,13},{6,14},{7,15},{8,0},{9,1},... | collective-permute-start | bytes 294920 | tf_op jit(solution)/shard_map/ppermute | solution.py:645
  61.8 1.5 %collective-permute-start.18 = (f32[1,192,128]{2,1,0:T(8,128)S(1)}, f32[1,192,128]{2,1,0:T(8,128)S(1)}, u32[]{:S(2)}, u32[]{:S(2)}) collective-permute-start(f32[1,192,128]{2,1,0:T(8,128)S(1)} %add.98), channel_id=1, source_target_pairs={{0,2},{1,3},{2,0},{3,1},{4,6},{5,7},{6,4},{7,5},{8,10},{9,11},{10,... | collective-permute-start | bytes 294920 | tf_op jit(solution)/shard_map/ppermute | solution.py:645
  63.3 1.3 %collective-permute-start.17 = (f32[1,208,128]{2,1,0:T(8,128)S(1)}, f32[1,208,128]{2,1,0:T(8,128)S(1)}, u32[]{:S(2)}, u32[]{:S(2)}) collective-permute-start(f32[1,208,128]{2,1,0:T(8,128)S(1)} %add.99), channel_id=1, source_target_pairs={{0,4},{1,5},{2,6},{3,7},{4,0},{5,1},{6,2},{7,3},{8,12},{9,13},{10,... | collective-permute-start | bytes 319496 | tf_op jit(solution)/shard_map/ppermute | solution.py:645
  65.1 1.4 %collective-permute-start.16 = (f32[2,192,128]{2,1,0:T(8,128)S(1)}, f32[2,192,128]{2,1,0:T(8,128)S(1)}, u32[]{:S(2)}, u32[]{:S(2)}) collective-permute-start(f32[2,192,128]{2,1,0:T(8,128)S(1)} %pad_maximum_fusion.4), channel_id=1, source_target_pairs={{0,4},{1,5},{2,6},{3,7},{4,0},{5,1},{6,2},{7,3},{8,12},{9,13},{10,... | collective-permute-start | bytes 589832 | tf_op jit(solution)/shard_map/ppermute | solution.py:645
  66.5 0.7 collective-permute-start.22
  67.2 1.9 %collective-permute-done.17 = f32[1,208,128]{2,1,0:T(8,128)S(1)} collective-permute-done((f32[1,208,128]{2,1,0:T(8,128)S(1)}, f32[1,208,128]{2,1,0:T(8,128)S(1)}, u32[]{:S(2)}, u32[]{:S(2)}) %collective-permute-start.17) | collective-permute-done | bytes 106528 | tf_op jit(solution)/shard_map/ppermute | solution.py:645
  69.1 1.2 %collective-permute-start.21 = (f32[2,208,128]{2,1,0:T(8,128)S(1)}, f32[2,208,128]{2,1,0:T(8,128)S(1)}, u32[]{:S(2)}, u32[]{:S(2)}) collective-permute-start(f32[2,208,128]{2,1,0:T(8,128)S(1)} %pad_maximum_fusion.3), channel_id=1, source_target_pairs={{0,2},{1,3},{2,0},{3,1},{4,6},{5,7},{6,4},{7,5},{8,10},{9,11},{10,... | collective-permute-start | bytes 638984 | tf_op jit(solution)/shard_map/ppermute | solution.py:645
  70.3 0.9 collective-permute-done.16
  71.2 1.0 %collective-permute-done.22 = f32[2,192,128]{2,1,0:T(8,128)S(1)} collective-permute-done((f32[2,192,128]{2,1,0:T(8,128)S(1)}, f32[2,192,128]{2,1,0:T(8,128)S(1)}, u32[]{:S(2)}, u32[]{:S(2)}) %collective-permute-start.22) | collective-permute-done | bytes 196640 | tf_op jit(solution)/shard_map/ppermute | solution.py:645
  72.3 3.8 %collective-permute-done.21 = f32[2,208,128]{2,1,0:T(8,128)S(1)} collective-permute-done((f32[2,208,128]{2,1,0:T(8,128)S(1)}, f32[2,208,128]{2,1,0:T(8,128)S(1)}, u32[]{:S(2)}, u32[]{:S(2)}) %collective-permute-start.21) | collective-permute-done | bytes 213024 | tf_op jit(solution)/shard_map/ppermute | solution.py:645
  77.0 1.3 %collective-permute-start.25 = (f32[4,192,128]{2,1,0:T(8,128)S(1)}, f32[4,192,128]{2,1,0:T(8,128)S(1)}, u32[]{:S(2)}, u32[]{:S(2)}) collective-permute-start(f32[4,192,128]{2,1,0:T(8,128)S(1)} %pad_maximum_fusion.2.refs_2_), channel_id=1, source_target_pairs={{0,4},{1,5},{2,6},{3,7},{4,0},{5,1},{6,2},{7,3},{8,12},{9,13},{10,... | collective-permute-start | bytes 1179656 | tf_op jit(solution)/shard_map/ppermute | solution.py:645
  78.8 5.4 %collective-permute-done.20.refs_1_ = f32[4,192,128]{2,1,0:T(8,128)S(1)} collective-permute-done((f32[4,192,128]{2,1,0:T(8,128)S(1)}, f32[4,192,128]{2,1,0:T(8,128)S(1)}, u32[]{:S(2)}, u32[]{:S(2)}) %collective-permute-start.20) | collective-permute-done | bytes 393248 | tf_op jit(solution)/shard_map/ppermute | solution.py:645
  85.8 1.5 %unpack_0.1 = (f32[6,512,256]{2,1,0:T(8,128)}, f32[6,256,256]{2,1,0:T(8,128)}) custom-call(s32[1]{0:T(128)} %bitcast.refs_0_.device_ref, f32[4,192,128]{2,1,0:T(8,128)S(1)} %pad_maximum_fusion.1.refs_0_, f32[4,192,128]{2,1,0:T(8,128)S(1)} %collective-permute-done.20.refs_1_, f32[4,192,128]{2,1,0:T(8,128)S(1)} %pad_maximum_fusion.2.refs_2_, ...), custom_call_target="tpu_custom_call" | custom-call | bytes 4194304 | tf_op jit(solution)/shard_map/unpack_0/pallas_call | solution.py:629
  88.2 2.2 %unpack_1.1 = (f32[6,512,256]{2,1,0:T(8,128)}, f32[6,256,256]{2,1,0:T(8,128)}, f32[16,1024]{1,0:T(8,128)}, f32[2,4,512]{2,1,0:T(4,128)}, f32[2,4]{1,0:T(2,128)},...) custom-call(s32[1]{0:T(128)} %bitcast.refs_0_.device_ref, ...), custom_call_target="tpu_custom_call", output_to_operand_aliasing={{0}: (9, {}), {1}: (10, {})} | custom-call | bytes 4194304 | tf_op jit(solution)/shard_map/unpack_1/pallas_call | solution.py:629
  (75 shorter events, 7.3 us)
Async XLA Ops:
  20.6 2.6 %collective-permute-start.2 = (f32[8,192,128]{2,1,0:T(8,128)}, f32[8,192,128]{2,1,0:T(8,128)S(1)}, u32[]{:S(2)}, u32[]{:S(2)}) collective-permute-start(f32[8,192,128]{2,1,0:T(8,128)} %get-tuple-element.68), channel_id=1, source_target_pairs={{0,1},{1,0},{2,3},{3,2},{4,5},{5,4},{6,7},{7,6},{8,9},{9,8},{10,11... | collective-permute-start | bytes 2359304 | tf_op jit(solution)/shard_map/ppermute | solution.py:645
  21.2 6.3 %collective-permute-start.1 = (f32[8,192,128]{2,1,0:T(8,128)}, f32[8,192,128]{2,1,0:T(8,128)S(1)}, u32[]{:S(2)}, u32[]{:S(2)}) collective-permute-start(f32[8,192,128]{2,1,0:T(8,128)} %get-tuple-element.66), channel_id=1, source_target_pairs={{0,1},{1,0},{2,3},{3,2},{4,5},{5,4},{6,7},{7,6},{8,9},{9,8},{10,11... | collective-permute-start | bytes 2359304 | tf_op jit(solution)/shard_map/ppermute | solution.py:645
  21.2 7.9 %collective-permute-start = (f32[8,208,128]{2,1,0:T(8,128)}, f32[8,208,128]{2,1,0:T(8,128)S(1)}, u32[]{:S(2)}, u32[]{:S(2)}) collective-permute-start(f32[8,208,128]{2,1,0:T(8,128)} %get-tuple-element.64), channel_id=1, source_target_pairs={{0,1},{1,0},{2,3},{3,2},{4,5},{5,4},{6,7},{7,6},{8,9},{9,8},{10,11... | collective-permute-start | bytes 2555912 | tf_op jit(solution)/shard_map/ppermute | solution.py:645
  24.5 12.3 %collective-permute-start.5 = (f32[4,192,128]{2,1,0:T(8,128)S(1)}, f32[4,192,128]{2,1,0:T(8,128)S(1)}, u32[]{:S(2)}, u32[]{:S(2)}) collective-permute-start(f32[4,192,128]{2,1,0:T(8,128)S(1)} %get-tuple-element.114), channel_id=1, source_target_pairs={{0,2},{1,3},{2,0},{3,1},{4,6},{5,7},{6,4},{7,5},{8,10},{9,11},{10,... | collective-permute-start | bytes 1179656 | tf_op jit(solution)/shard_map/ppermute | solution.py:645
  27.5 27.3 %copy-start.3 = (f32[1024,128]{1,0:T(8,128)S(1)}, f32[1024,128]{1,0:T(8,128)}, u32[]{:S(2)}) copy-start(f32[1024,128]{1,0:T(8,128)} %get-tuple-element.80.refs_0_) | copy-start | bytes 1572868
  27.5 11.2 %collective-permute-start.4 = (f32[4,192,128]{2,1,0:T(8,128)S(1)}, f32[4,192,128]{2,1,0:T(8,128)S(1)}, u32[]{:S(2)}, u32[]{:S(2)}) collective-permute-start(f32[4,192,128]{2,1,0:T(8,128)S(1)} %get-tuple-element.116), channel_id=1, source_target_pairs={{0,4},{1,5},{2,6},{3,7},{4,0},{5,1},{6,2},{7,3},{8,12},{9,13},{10,... | collective-permute-start | bytes 1179656 | tf_op jit(solution)/shard_map/ppermute | solution.py:645
  29.1 25.6 %copy-start.1 = (bf16[6,1024,256]{2,1,0:T(8,128)(2,1)S(1)}, bf16[6,1024,256]{2,1,0:T(8,128)(2,1)}, u32[]{:S(2)}) copy-start(bf16[6,1024,256]{2,1,0:T(8,128)(2,1)} %get-tuple-element.83.refs_8_) | copy-start | bytes 9437188
  29.2 11.4 %collective-permute-start.3 = (f32[4,208,128]{2,1,0:T(8,128)S(1)}, f32[4,208,128]{2,1,0:T(8,128)S(1)}, u32[]{:S(2)}, u32[]{:S(2)}) collective-permute-start(f32[4,208,128]{2,1,0:T(8,128)S(1)} %get-tuple-element.111), channel_id=1, source_target_pairs={{0,8},{1,9},{2,10},{3,11},{4,12},{5,13},{6,14},{7,15},{8,0},{9,1},... | collective-permute-start | bytes 1277960 | tf_op jit(solution)/shard_map/ppermute | solution.py:645
  36.9 6.5 %collective-permute-start.8 = (f32[2,192,128]{2,1,0:T(8,128)S(1)}, f32[2,192,128]{2,1,0:T(8,128)S(1)}, u32[]{:S(2)}, u32[]{:S(2)}) collective-permute-start(f32[2,192,128]{2,1,0:T(8,128)S(1)} %get-tuple-element.120), channel_id=1, source_target_pairs={{0,4},{1,5},{2,6},{3,7},{4,0},{5,1},{6,2},{7,3},{8,12},{9,13},{10,... | collective-permute-start | bytes 589832 | tf_op jit(solution)/shard_map/ppermute | solution.py:645
  38.8 6.2 %collective-permute-start.7 = (f32[2,192,128]{2,1,0:T(8,128)S(1)}, f32[2,192,128]{2,1,0:T(8,128)S(1)}, u32[]{:S(2)}, u32[]{:S(2)}) collective-permute-start(f32[2,192,128]{2,1,0:T(8,128)S(1)} %get-tuple-element.122), channel_id=1, source_target_pairs={{0,8},{1,9},{2,10},{3,11},{4,12},{5,13},{6,14},{7,15},{8,0},{9,1},... | collective-permute-start | bytes 589832 | tf_op jit(solution)/shard_map/ppermute | solution.py:645
  40.7 6.6 %collective-permute-start.6 = (f32[2,208,128]{2,1,0:T(8,128)S(1)}, f32[2,208,128]{2,1,0:T(8,128)S(1)}, u32[]{:S(2)}, u32[]{:S(2)}) collective-permute-start(f32[2,208,128]{2,1,0:T(8,128)S(1)} %get-tuple-element.117), channel_id=1, source_target_pairs={{0,2},{1,3},{2,0},{3,1},{4,6},{5,7},{6,4},{7,5},{8,10},{9,11},{10,... | collective-permute-start | bytes 638984 | tf_op jit(solution)/shard_map/ppermute | solution.py:645
  43.4 4.8 %collective-permute-start.11 = (f32[1,192,128]{2,1,0:T(8,128)S(1)}, f32[1,192,128]{2,1,0:T(8,128)S(1)}, u32[]{:S(2)}, u32[]{:S(2)}) collective-permute-start(f32[1,192,128]{2,1,0:T(8,128)S(1)} %slice_add_fusion.16), channel_id=1, source_target_pairs={{0,8},{1,9},{2,10},{3,11},{4,12},{5,13},{6,14},{7,15},{8,0},{9,1},... | collective-permute-start | bytes 294920 | tf_op jit(solution)/shard_map/ppermute | solution.py:645
  45.0 5.8 %collective-permute-start.10 = (f32[1,192,128]{2,1,0:T(8,128)S(1)}, f32[1,192,128]{2,1,0:T(8,128)S(1)}, u32[]{:S(2)}, u32[]{:S(2)}) collective-permute-start(f32[1,192,128]{2,1,0:T(8,128)S(1)} %slice_add_fusion.17), channel_id=1, source_target_pairs={{0,2},{1,3},{2,0},{3,1},{4,6},{5,7},{6,4},{7,5},{8,10},{9,11},{10,... | collective-permute-start | bytes 294920 | tf_op jit(solution)/shard_map/ppermute | solution.py:645
  47.3 5.2 %collective-permute-start.9 = (f32[1,208,128]{2,1,0:T(8,128)S(1)}, f32[1,208,128]{2,1,0:T(8,128)S(1)}, u32[]{:S(2)}, u32[]{:S(2)}) collective-permute-start(f32[1,208,128]{2,1,0:T(8,128)S(1)} %slice_add_fusion.12), channel_id=1, source_target_pairs={{0,4},{1,5},{2,6},{3,7},{4,0},{5,1},{6,2},{7,3},{8,12},{9,13},{10,... | collective-permute-start | bytes 319496 | tf_op jit(solution)/shard_map/ppermute | solution.py:645
  48.2 12.1 %collective-permute-start.12 = (f32[1,192,128]{2,1,0:T(8,128)S(1)}, f32[1,192,128]{2,1,0:T(8,128)S(1)}, u32[]{:S(2)}, u32[]{:S(2)}) collective-permute-start(f32[1,192,128]{2,1,0:T(8,128)S(1)} %fusion.1), channel_id=1, source_target_pairs={{0,16},{1,17},{2,18},{3,19},{4,20},{5,21},{6,22},{7,23},{8,24},{9,... | collective-permute-start | bytes 294920 | tf_op jit(solution)/shard_map/ppermute | solution.py:645
  50.9 10.9 %collective-permute-start.15 = (f32[1,192,128]{2,1,0:T(8,128)S(1)}, f32[1,192,128]{2,1,0:T(8,128)S(1)}, u32[]{:S(2)}, u32[]{:S(2)}) collective-permute-start(f32[1,192,128]{2,1,0:T(8,128)S(1)} %fusion.2), channel_id=1, source_target_pairs={{0,16},{1,17},{2,18},{3,19},{4,20},{5,21},{6,22},{7,23},{8,24},{9,... | collective-permute-start | bytes 294920 | tf_op jit(solution)/shard_map/ppermute | solution.py:645
  52.5 10.8 %collective-permute-start.14 = (f32[1,208,128]{2,1,0:T(8,128)S(1)}, f32[1,208,128]{2,1,0:T(8,128)S(1)}, u32[]{:S(2)}, u32[]{:S(2)}) collective-permute-start(f32[1,208,128]{2,1,0:T(8,128)S(1)} %fusion), channel_id=1, source_target_pairs={{0,16},{1,17},{2,18},{3,19},{4,20},{5,21},{6,22},{7,23},{8,24},{9,... | collective-permute-start | bytes 319496 | tf_op jit(solution)/shard_map/ppermute | solution.py:645
  60.4 4.7 %collective-permute-start.13 = (f32[1,192,128]{2,1,0:T(8,128)S(1)}, f32[1,192,128]{2,1,0:T(8,128)S(1)}, u32[]{:S(2)}, u32[]{:S(2)}) collective-permute-start(f32[1,192,128]{2,1,0:T(8,128)S(1)} %add.97), channel_id=1, source_target_pairs={{0,8},{1,9},{2,10},{3,11},{4,12},{5,13},{6,14},{7,15},{8,0},{9,1},... | collective-permute-start | bytes 294920 | tf_op jit(solution)/shard_map/ppermute | solution.py:645
  61.8 4.7 %collective-permute-start.18 = (f32[1,192,128]{2,1,0:T(8,128)S(1)}, f32[1,192,128]{2,1,0:T(8,128)S(1)}, u32[]{:S(2)}, u32[]{:S(2)}) collective-permute-start(f32[1,192,128]{2,1,0:T(8,128)S(1)} %add.98), channel_id=1, source_target_pairs={{0,2},{1,3},{2,0},{3,1},{4,6},{5,7},{6,4},{7,5},{8,10},{9,11},{10,... | collective-permute-start | bytes 294920 | tf_op jit(solution)/shard_map/ppermute | solution.py:645
  63.3 5.8 %collective-permute-start.17 = (f32[1,208,128]{2,1,0:T(8,128)S(1)}, f32[1,208,128]{2,1,0:T(8,128)S(1)}, u32[]{:S(2)}, u32[]{:S(2)}) collective-permute-start(f32[1,208,128]{2,1,0:T(8,128)S(1)} %add.99), channel_id=1, source_target_pairs={{0,4},{1,5},{2,6},{3,7},{4,0},{5,1},{6,2},{7,3},{8,12},{9,13},{10,... | collective-permute-start | bytes 319496 | tf_op jit(solution)/shard_map/ppermute | solution.py:645
  65.1 6.1 %collective-permute-start.16 = (f32[2,192,128]{2,1,0:T(8,128)S(1)}, f32[2,192,128]{2,1,0:T(8,128)S(1)}, u32[]{:S(2)}, u32[]{:S(2)}) collective-permute-start(f32[2,192,128]{2,1,0:T(8,128)S(1)} %pad_maximum_fusion.4), channel_id=1, source_target_pairs={{0,4},{1,5},{2,6},{3,7},{4,0},{5,1},{6,2},{7,3},{8,12},{9,13},{10,... | collective-permute-start | bytes 589832 | tf_op jit(solution)/shard_map/ppermute | solution.py:645
  66.5 5.7 %collective-permute-start.22 = (f32[2,192,128]{2,1,0:T(8,128)S(1)}, f32[2,192,128]{2,1,0:T(8,128)S(1)}, u32[]{:S(2)}, u32[]{:S(2)}) collective-permute-start(f32[2,192,128]{2,1,0:T(8,128)S(1)} %pad_maximum_fusion.5), channel_id=1, source_target_pairs={{0,8},{1,9},{2,10},{3,11},{4,12},{5,13},{6,14},{7,15},{8,0},{9,1},... | collective-permute-start | bytes 589832 | tf_op jit(solution)/shard_map/ppermute | solution.py:645
  69.1 7.0 %collective-permute-start.21 = (f32[2,208,128]{2,1,0:T(8,128)S(1)}, f32[2,208,128]{2,1,0:T(8,128)S(1)}, u32[]{:S(2)}, u32[]{:S(2)}) collective-permute-start(f32[2,208,128]{2,1,0:T(8,128)S(1)} %pad_maximum_fusion.3), channel_id=1, source_target_pairs={{0,2},{1,3},{2,0},{3,1},{4,6},{5,7},{6,4},{7,5},{8,10},{9,11},{10,... | collective-permute-start | bytes 638984 | tf_op jit(solution)/shard_map/ppermute | solution.py:645
  76.1 8.6 %collective-permute-start.28 = (f32[4,208,128]{2,1,0:T(8,128)S(1)}, f32[4,208,128]{2,1,0:T(8,128)S(1)}, u32[]{:S(2)}, u32[]{:S(2)}) collective-permute-start(f32[4,208,128]{2,1,0:T(8,128)S(1)} %pad_maximum_fusion.refs_4_.refs_6_), channel_id=1, source_target_pairs={{0,8},{1,9},{2,10},{3,11},{4,12},{5,13},{6,14},{7,15},{8,0},{9,1},... | collective-permute-start | bytes 1277960 | tf_op jit(solution)/shard_map/ppermute | solution.py:645
  76.4 7.8 %collective-permute-start.20 = (f32[4,192,128]{2,1,0:T(8,128)S(1)}, f32[4,192,128]{2,1,0:T(8,128)S(1)}, u32[]{:S(2)}, u32[]{:S(2)}) collective-permute-start(f32[4,192,128]{2,1,0:T(8,128)S(1)} %pad_maximum_fusion.1.refs_0_), channel_id=1, source_target_pairs={{0,2},{1,3},{2,0},{3,1},{4,6},{5,7},{6,4},{7,5},{8,10},{9,11},{10,... | collective-permute-start | bytes 1179656 | tf_op jit(solution)/shard_map/ppermute | solution.py:645
  77.0 7.8 %collective-permute-start.25 = (f32[4,192,128]{2,1,0:T(8,128)S(1)}, f32[4,192,128]{2,1,0:T(8,128)S(1)}, u32[]{:S(2)}, u32[]{:S(2)}) collective-permute-start(f32[4,192,128]{2,1,0:T(8,128)S(1)} %pad_maximum_fusion.2.refs_2_), channel_id=1, source_target_pairs={{0,4},{1,5},{2,6},{3,7},{4,0},{5,1},{6,2},{7,3},{8,12},{9,13},{10,... | collective-permute-start | bytes 1179656 | tf_op jit(solution)/shard_map/ppermute | solution.py:645
  78.2 7.0 %collective-permute-start.24 = (f32[4,192,128]{2,1,0:T(8,128)S(1)}, f32[4,192,128]{2,1,0:T(8,128)S(1)}, u32[]{:S(2)}, u32[]{:S(2)}) collective-permute-start(f32[4,192,128]{2,1,0:T(8,128)S(1)} %pad_maximum_fusion.2.refs_2_), channel_id=1, source_target_pairs={{0,1},{1,0},{2,3},{3,2},{4,5},{5,4},{6,7},{7,6},{8,9},{9,8},{10,11... | collective-permute-start | bytes 1179656 | tf_op jit(solution)/shard_map/ppermute | solution.py:645
  78.2 9.1 %collective-permute-start.27 = (f32[4,208,128]{2,1,0:T(8,128)S(1)}, f32[4,208,128]{2,1,0:T(8,128)S(1)}, u32[]{:S(2)}, u32[]{:S(2)}) collective-permute-start(f32[4,208,128]{2,1,0:T(8,128)S(1)} %pad_maximum_fusion.refs_4_.refs_6_), channel_id=1, source_target_pairs={{0,1},{1,0},{2,3},{3,2},{4,5},{5,4},{6,7},{7,6},{8,9},{9,8},{10,11... | collective-permute-start | bytes 1277960 | tf_op jit(solution)/shard_map/ppermute | solution.py:645
  84.8 3.5 %collective-permute-start.29 = (f32[4,208,128]{2,1,0:T(8,128)S(1)}, f32[4,208,128]{2,1,0:T(8,128)S(1)}, u32[]{:S(2)}, u32[]{:S(2)}) collective-permute-start(f32[4,208,128]{2,1,0:T(8,128)S(1)} %collective-permute-done.28.refs_5_.refs_7_), channel_id=1, source_target_pairs={{0,1},{1,0},{2,3},{3,2},{4,5},{5,4},{6,7},{7,6},{8,9},{9,8},{10,11... | collective-permute-start | bytes 1277960 | tf_op jit(solution)/shard_map/ppermute | solution.py:645
  84.8 2.6 %collective-permute-start.19 = (f32[4,192,128]{2,1,0:T(8,128)S(1)}, f32[4,192,128]{2,1,0:T(8,128)S(1)}, u32[]{:S(2)}, u32[]{:S(2)}) collective-permute-start(f32[4,192,128]{2,1,0:T(8,128)S(1)} %pad_maximum_fusion.1.refs_0_), channel_id=1, source_target_pairs={{0,1},{1,0},{2,3},{3,2},{4,5},{5,4},{6,7},{7,6},{8,9},{9,8},{10,11... | collective-permute-start | bytes 1179656 | tf_op jit(solution)/shard_map/ppermute | solution.py:645
  85.3 2.4 %collective-permute-start.26 = (f32[4,192,128]{2,1,0:T(8,128)S(1)}, f32[4,192,128]{2,1,0:T(8,128)S(1)}, u32[]{:S(2)}, u32[]{:S(2)}) collective-permute-start(f32[4,192,128]{2,1,0:T(8,128)S(1)} %collective-permute-done.25.refs_3_), channel_id=1, source_target_pairs={{0,1},{1,0},{2,3},{3,2},{4,5},{5,4},{6,7},{7,6},{8,9},{9,8},{10,11... | collective-permute-start | bytes 1179656 | tf_op jit(solution)/shard_map/ppermute | solution.py:645
  85.3 2.9 %collective-permute-start.23 = (f32[4,192,128]{2,1,0:T(8,128)S(1)}, f32[4,192,128]{2,1,0:T(8,128)S(1)}, u32[]{:S(2)}, u32[]{:S(2)}) collective-permute-start(f32[4,192,128]{2,1,0:T(8,128)S(1)} %collective-permute-done.20.refs_1_), channel_id=1, source_target_pairs={{0,1},{1,0},{2,3},{3,2},{4,5},{5,4},{6,7},{7,6},{8,9},{9,8},{10,11... | collective-permute-start | bytes 1179656 | tf_op jit(solution)/shard_map/ppermute | solution.py:645
  (9 other events, 120.1 us)
